TPU v7x, 32 devices: a whole 2x2x4 slice. The times are simulated.
32 devices in a mesh: shard: 16 (over z, x, core), rep: 2 (over y).
Axes of the slice: x: 2, y: 2, z: 4, core: 2. Of those that a mesh axis runs over, the one named last changes fastest.
Arguments:
- layer_input: bfloat16 [32768, 1024], P(('shard', 'rep')), may hold values from -6 to 6
- attention_gain: float32 [1024], replicated, may hold values from 0.1 to 1.9
- query_weight: bfloat16 [1024, 1024], P('shard'), may hold values from -0.25 to 0.25
- key_weight: bfloat16 [1024, 512], P('shard'), may hold values from -0.25 to 0.25
- value_weight: bfloat16 [1024, 512], P('shard'), may hold values from -0.1875 to 0.1875
- output_weight: bfloat16 [1024, 1024], P('shard'), may hold values from -0.75 to 0.75
- expert_gain: float32 [1024], replicated, may hold values from 0.1 to 1.9
- router_weight: bfloat16 [1024, 32], replicated, may hold values from -0.08984375 to 0.08984375
- gate_weight: bfloat16 [32, 1024, 512], P('shard'), may hold values from -0.1875 to 0.1875
- up_weight: bfloat16 [32, 1024, 512], P('shard'), may hold values from -0.1875 to 0.1875
- down_weight: bfloat16 [32, 512, 1024], P('shard'), may hold values from -0.25 to 0.25
- lengths: int32 [32], P(('shard', 'rep')), may hold values from 512 to 1024, as said below
- routes: int32 [32768, 8], P(('shard', 'rep')), may hold values from 0 to 31, all different within a row; in each aligned block of 1024 rows (0 to 1023, 1024 to 2047, ...) at most 288 rows name the same one
- cotangent: bfloat16 [32768, 1024], P(('shard', 'rep')), may hold values from -6 to 6
Outputs:
- layer_output: bfloat16 [32768, 1024], P(('shard', 'rep'))
- input_gradient: bfloat16 [32768, 1024], P(('shard', 'rep'))
- attention_gain_gradient: float32 [1024], replicated
- query_weight_gradient: float32 [1024, 1024], P('shard')
- key_weight_gradient: float32 [1024, 512], P('shard')
- value_weight_gradient: float32 [1024, 512], P('shard')
- output_weight_gradient: float32 [1024, 1024], P('shard')
- expert_gain_gradient: float32 [1024], replicated
- router_weight_gradient: float32 [1024, 32], replicated
- gate_weight_gradient: float32 [32, 1024, 512], P('shard')
- up_weight_gradient: float32 [32, 1024, 512], P('shard')
- down_weight_gradient: float32 [32, 512, 1024], P('shard')
Inputs may be any that keep to these rules, and one draw needn't show every extreme that they name: `lengths`: every slot holds one sequence from position 0; some slot is filled to its end and some holds exactly 512 tokens. `routes`: A token's 8 experts are distinct; among the 1024 rows of one device no expert is named more than 288 times.
All inputs are finite; a program needn't handle non-finite values.
Results may differ from a plain program's by a relative error of at most 0.015.
The roundings to bfloat16 on the way count: a program that leaves them out, or rounds other values in their place, can miss the bound.
Values may be sent and summed in bfloat16 or wider, within the bound.
A program may use at most 448 MiB of HBM per device.

v0:
```python
import jax
import jax.numpy as jnp
from jax import lax
from jax.sharding import PartitionSpec as P

D = 1024
HEADS = 16
KV = 8
HD = 64
EXPERTS = 32
TOP = 8
CAP = 288


epsilon = 1e-06
masked_score = -1e30
rotary_base = 10000.0


def rope_tables(length_rows, head_width):
    halfway = head_width // 2
    index_float = jnp.arange(halfway, dtype=jnp.float32)
    frequency = jnp.exp(-jnp.log(rotary_base) * index_float * 2.0 / head_width)
    angle = jnp.arange(length_rows, dtype=jnp.float32)[:, None] * frequency[None, :]
    return (jnp.cos(angle)[:, None, :], jnp.sin(angle)[:, None, :])


def rotate(values, cosine, sine):
    halfway = values.shape[-1] // 2
    first_half = values[..., :halfway]
    second_half = values[..., halfway:]
    return jnp.concatenate(
        [first_half * cosine - second_half * sine, second_half * cosine + first_half * sine],
        axis=-1,
    )


def unrotate(slopes, cosine, sine):
    halfway = slopes.shape[-1] // 2
    first_half = slopes[..., :halfway]
    second_half = slopes[..., halfway:]
    return jnp.concatenate(
        [first_half * cosine + second_half * sine, second_half * cosine - first_half * sine],
        axis=-1,
    )


def softmax_last(values):
    maximum = jnp.max(values, axis=-1, keepdims=True)
    powered = jnp.exp(values - maximum)
    return powered / jnp.sum(powered, axis=-1, keepdims=True)


def block_scores(query_block, keys, start_row, length, scale):
    products = (
        jnp.einsum("qhgd,khd->hgqk", query_block, keys, preferred_element_type=jnp.float32) * scale
    )
    query_place = start_row + jnp.arange(query_block.shape[0], dtype=jnp.int32)
    key_place = jnp.arange(keys.shape[0], dtype=jnp.int32)
    allowed = (key_place[None, :] <= query_place[:, None]) & (key_place[None, :] < length)
    return jnp.where(allowed[None, None], products, masked_score)


def on_device(
    layer_input,
    attention_gain,
    query_weight,
    key_weight,
    value_weight,
    output_weight,
    expert_gain,
    router_weight,
    gate_weight,
    up_weight,
    down_weight,
    lengths,
    routes,
    cotangent,
):
    tokens = layer_input.shape[0]
    groups = HEADS // KV
    scale = HD ** (-0.5)
    length = lengths[0]
    inputs_f = layer_input.astype(jnp.float32)
    first_scale = lax.rsqrt(jnp.mean(inputs_f * inputs_f, axis=-1, keepdims=True) + epsilon)
    base_one = inputs_f * first_scale
    normed_one = (base_one * attention_gain).astype(jnp.bfloat16)
    query_full, key_full, value_full, output_full = (
        lax.all_gather(query_weight, "shard", axis=0, tiled=True),
        lax.all_gather(key_weight, "shard", axis=0, tiled=True),
        lax.all_gather(value_weight, "shard", axis=0, tiled=True),
        lax.all_gather(output_weight, "shard", axis=0, tiled=True),
    )
    cosine, sine = rope_tables(tokens, HD)
    query_pre = jnp.dot(normed_one, query_full, preferred_element_type=jnp.float32)
    key_pre = jnp.dot(normed_one, key_full, preferred_element_type=jnp.float32)
    queries = (
        rotate(query_pre.reshape(tokens, HEADS, HD), cosine, sine)
        .astype(jnp.bfloat16)
        .reshape(tokens, KV, groups, HD)
    )
    keys = rotate(key_pre.reshape(tokens, KV, HD), cosine, sine).astype(jnp.bfloat16)
    values = (
        jnp.dot(normed_one, value_full, preferred_element_type=jnp.float32)
        .astype(jnp.bfloat16)
        .reshape(tokens, KV, HD)
    )
    block = min(512, tokens)
    block_count = tokens // block
    mixed_parts = []
    log_totals = []
    for block_index in range(block_count):
        start_row = block_index * block
        scores = block_scores(
            queries[start_row : start_row + block], keys, start_row, length, scale
        )
        maximum = jnp.max(scores, axis=-1, keepdims=True)
        powered = jnp.exp(scores - maximum)
        total = jnp.sum(powered, axis=-1, keepdims=True)
        probs = (powered / total).astype(jnp.bfloat16)
        log_totals.append(maximum + jnp.log(total))
        mixed_parts.append(
            jnp.einsum("hgqk,khd->qhgd", probs, values, preferred_element_type=jnp.float32)
        )
    attended = jnp.concatenate(mixed_parts, axis=0).reshape(tokens, HEADS * HD).astype(jnp.bfloat16)
    branch = jnp.dot(attended, output_full, preferred_element_type=jnp.float32)
    residual = inputs_f + branch
    second_scale = lax.rsqrt(jnp.mean(residual * residual, axis=-1, keepdims=True) + epsilon)
    base_two = residual * second_scale
    normed_two = (base_two * expert_gain).astype(jnp.bfloat16)
    logits = jnp.dot(normed_two, router_weight, preferred_element_type=jnp.float32)
    picks = (routes[:, :, None] == jnp.arange(EXPERTS, dtype=jnp.int32)[None, None, :]).astype(
        jnp.float32
    )
    chosen = jnp.sum(picks * logits[:, None, :], axis=-1)
    gates = softmax_last(chosen)
    assigned = routes.reshape(-1)
    marks = (assigned[:, None] == jnp.arange(EXPERTS, dtype=jnp.int32)[None, :]).astype(jnp.int32)
    ranked = jnp.sum((jnp.cumsum(marks, axis=0) - marks) * marks, axis=1)
    targets = assigned * CAP + ranked
    spread_rows = jnp.broadcast_to(normed_two[:, None, :], (tokens, TOP, D)).reshape(
        tokens * TOP, D
    )
    outgoing = (
        jnp.zeros((EXPERTS * CAP, D), jnp.bfloat16)
        .at[targets]
        .set(spread_rows)
        .reshape(EXPERTS, 1, CAP, D)
    )
    incoming = lax.all_to_all(outgoing, "shard", split_axis=0, concat_axis=1, tiled=True)
    local_experts = gate_weight.shape[0]
    expert_rows = incoming.reshape(local_experts, -1, D)
    gate_part = jnp.einsum(
        "erd,edf->erf", expert_rows, gate_weight, preferred_element_type=jnp.float32
    )
    up_part = jnp.einsum("erd,edf->erf", expert_rows, up_weight, preferred_element_type=jnp.float32)
    hidden = (gate_part * jax.nn.sigmoid(gate_part) * up_part).astype(jnp.bfloat16)
    expert_out = jnp.einsum(
        "erf,efd->erd", hidden, down_weight, preferred_element_type=jnp.float32
    ).astype(jnp.bfloat16)
    returned = lax.all_to_all(
        expert_out.reshape(local_experts, -1, CAP, D),
        "shard",
        split_axis=1,
        concat_axis=0,
        tiled=True,
    )
    picked = returned.reshape(EXPERTS * CAP, D)[targets].reshape(tokens, TOP, D)
    mixture = jnp.sum(gates[:, :, None] * picked, axis=1)
    layer_output = (residual + mixture).astype(jnp.bfloat16)
    token_place = jnp.arange(tokens, dtype=jnp.int32)
    valid = (token_place < length)[:, None]
    slope = jnp.where(valid, cotangent.astype(jnp.float32), 0.0)
    gate_slope = jnp.sum(picked * slope[:, None, :], axis=-1)
    routed_slope = (
        (gates[:, :, None] * slope[:, None, :]).astype(jnp.bfloat16).reshape(tokens * TOP, D)
    )
    outgoing_slope = (
        jnp.zeros((EXPERTS * CAP, D), jnp.bfloat16)
        .at[targets]
        .set(routed_slope)
        .reshape(EXPERTS, 1, CAP, D)
    )
    incoming_slope = lax.all_to_all(
        outgoing_slope, "shard", split_axis=0, concat_axis=1, tiled=True
    )
    slope_rows = incoming_slope.reshape(local_experts, -1, D)
    down_grad = jnp.einsum("erf,erd->efd", hidden, slope_rows, preferred_element_type=jnp.float32)
    hidden_slope = jnp.einsum(
        "erd,efd->erf", slope_rows, down_weight, preferred_element_type=jnp.float32
    )
    sigma = jax.nn.sigmoid(gate_part)
    gate_part_slope = (hidden_slope * up_part * sigma * (1.0 + gate_part * (1.0 - sigma))).astype(
        jnp.bfloat16
    )
    up_part_slope = (hidden_slope * gate_part * sigma).astype(jnp.bfloat16)
    gate_grad = jnp.einsum(
        "erd,erf->edf", expert_rows, gate_part_slope, preferred_element_type=jnp.float32
    )
    up_grad = jnp.einsum(
        "erd,erf->edf", expert_rows, up_part_slope, preferred_element_type=jnp.float32
    )
    row_slope = (
        jnp.einsum("erf,edf->erd", gate_part_slope, gate_weight, preferred_element_type=jnp.float32)
        + jnp.einsum("erf,edf->erd", up_part_slope, up_weight, preferred_element_type=jnp.float32)
    ).astype(jnp.bfloat16)
    returned_slope = lax.all_to_all(
        row_slope.reshape(local_experts, -1, CAP, D),
        "shard",
        split_axis=1,
        concat_axis=0,
        tiled=True,
    )
    token_rows = returned_slope.reshape(EXPERTS * CAP, D)[targets].reshape(tokens, TOP, D)
    normed_slope = jnp.sum(token_rows, axis=1, dtype=jnp.float32)
    mean_slope = jnp.sum(gates * gate_slope, axis=-1, keepdims=True)
    chosen_slope = gates * (gate_slope - mean_slope)
    logit_slope = jnp.sum(picks * chosen_slope[:, :, None], axis=1).astype(jnp.bfloat16)
    router_grad = jnp.einsum(
        "sd,se->de", normed_two, logit_slope, preferred_element_type=jnp.float32
    )
    normed_slope = normed_slope + jnp.einsum(
        "se,de->sd", logit_slope, router_weight, preferred_element_type=jnp.float32
    )
    expert_gain_grad = jnp.sum(normed_slope * base_two, axis=0)
    scaled_two = normed_slope * expert_gain
    residual_slope = (
        slope
        + second_scale * scaled_two
        - base_two
        * second_scale
        * second_scale
        * jnp.mean(scaled_two * residual, axis=-1, keepdims=True)
    )
    branch_slope = residual_slope.astype(jnp.bfloat16)
    output_grad = jnp.einsum(
        "sc,sd->cd", attended, branch_slope, preferred_element_type=jnp.float32
    )
    attended_slope = (
        jnp.einsum("sd,cd->sc", branch_slope, output_full, preferred_element_type=jnp.float32)
        .astype(jnp.bfloat16)
        .reshape(tokens, KV, groups, HD)
    )
    query_parts = []
    key_total = jnp.zeros((tokens, KV, HD), jnp.float32)
    value_total = jnp.zeros((tokens, KV, HD), jnp.float32)
    for block_index in range(block_count):
        start_row = block_index * block
        query_block = queries[start_row : start_row + block]
        mixed_slope = attended_slope[start_row : start_row + block]
        scores = block_scores(query_block, keys, start_row, length, scale)
        weights_soft = jnp.exp(scores - log_totals[block_index])
        probs = weights_soft.astype(jnp.bfloat16)
        probs_slope = jnp.einsum(
            "qhgd,khd->hgqk", mixed_slope, values, preferred_element_type=jnp.float32
        )
        centre = jnp.sum(weights_soft * probs_slope, axis=-1, keepdims=True)
        score_slope = (weights_soft * (probs_slope - centre)).astype(jnp.bfloat16)
        query_parts.append(
            jnp.einsum("hgqk,khd->qhgd", score_slope, keys, preferred_element_type=jnp.float32)
            * scale
        )
        key_total = (
            key_total
            + jnp.einsum(
                "hgqk,qhgd->khd", score_slope, query_block, preferred_element_type=jnp.float32
            )
            * scale
        )
        value_total = value_total + jnp.einsum(
            "hgqk,qhgd->khd", probs, mixed_slope, preferred_element_type=jnp.float32
        )
    query_slope = jnp.concatenate(query_parts, axis=0).reshape(tokens, HEADS, HD)
    query_pre_slope = (
        unrotate(query_slope, cosine, sine).reshape(tokens, HEADS * HD).astype(jnp.bfloat16)
    )
    key_pre_slope = unrotate(key_total, cosine, sine).reshape(tokens, KV * HD).astype(jnp.bfloat16)
    value_pre_slope = value_total.reshape(tokens, KV * HD).astype(jnp.bfloat16)
    query_grad = jnp.einsum(
        "sd,sc->dc", normed_one, query_pre_slope, preferred_element_type=jnp.float32
    )
    key_grad = jnp.einsum(
        "sd,sc->dc", normed_one, key_pre_slope, preferred_element_type=jnp.float32
    )
    value_grad = jnp.einsum(
        "sd,sc->dc", normed_one, value_pre_slope, preferred_element_type=jnp.float32
    )
    normed_one_slope = (
        jnp.einsum("sc,dc->sd", query_pre_slope, query_full, preferred_element_type=jnp.float32)
        + jnp.einsum("sc,dc->sd", key_pre_slope, key_full, preferred_element_type=jnp.float32)
        + jnp.einsum("sc,dc->sd", value_pre_slope, value_full, preferred_element_type=jnp.float32)
    )
    attention_gain_grad = jnp.sum(normed_one_slope * base_one, axis=0)
    scaled_one = normed_one_slope * attention_gain
    input_slope = (
        residual_slope
        + first_scale * scaled_one
        - base_one
        * first_scale
        * first_scale
        * jnp.mean(scaled_one * inputs_f, axis=-1, keepdims=True)
    )
    input_gradient = input_slope.astype(jnp.bfloat16)
    small_sums = lax.psum((attention_gain_grad, expert_gain_grad, router_grad), ("shard", "rep"))
    owned = (
        lax.psum_scatter(query_grad, "shard", scatter_dimension=0, tiled=True),
        lax.psum_scatter(key_grad, "shard", scatter_dimension=0, tiled=True),
        lax.psum_scatter(value_grad, "shard", scatter_dimension=0, tiled=True),
        lax.psum_scatter(output_grad, "shard", scatter_dimension=0, tiled=True),
    )
    summed = lax.psum(
        (owned[0], owned[1], owned[2], owned[3], gate_grad, up_grad, down_grad), "rep"
    )
    query_sum, key_sum, value_sum, output_sum = (summed[0], summed[1], summed[2], summed[3])
    gate_sum, up_sum, down_sum = (summed[4], summed[5], summed[6])
    return (
        layer_output,
        input_gradient,
        small_sums[0],
        query_sum,
        key_sum,
        value_sum,
        output_sum,
        small_sums[1],
        small_sums[2],
        gate_sum,
        up_sum,
        down_sum,
    )


def solution(mesh):
    return jax.shard_map(
        on_device,
        mesh=mesh,
        in_specs=(
            P(("shard", "rep"), None),
            P(),
            P("shard", None),
            P("shard", None),
            P("shard", None),
            P("shard", None),
            P(),
            P(),
            P("shard", None, None),
            P("shard", None, None),
            P("shard", None, None),
            P(("shard", "rep")),
            P(("shard", "rep"), None),
            P(("shard", "rep"), None),
        ),
        out_specs=(
            P(("shard", "rep"), None),
            P(("shard", "rep"), None),
            P(),
            P("shard", None),
            P("shard", None),
            P("shard", None),
            P("shard", None),
            P(),
            P(),
            P("shard", None, None),
            P("shard", None, None),
            P("shard", None, None),
        ),
        check_vma=False,
    )
```

profile of v0, /device:TPU:0, one launch (start us, length us, event | category | flops | bytes accessed | tf_op | source)
XLA Modules:
  0.0 2979.5 jit_solution(12691508222840847292)
XLA Ops:
  54.5 35.5 %all-gather.5.cloned.1.call-done = bf16[1024,512]{1,0:T(8,128)(2,1)} async-done(((bf16[64,512]{1,0:T(8,128)(2,1)}), bf16[1024,512]{1,0:T(8,128)(2,1)}) %all-gather.5.cloned.1.call-update) | async-done | bytes 1048592 | tf_op jit(solution)/shard_map/all_gather | solution.py:91
  94.1 38.3 %all-gather.9.cloned.1.call-done = bf16[1024,1024]{1,0:T(8,128)(2,1)} async-done(((bf16[64,1024]{1,0:T(8,128)(2,1)}), bf16[1024,1024]{1,0:T(8,128)(2,1)}) %all-gather.9.cloned.1.call-update) | async-done | bytes 2097168 | tf_op jit(solution)/shard_map/all_gather | solution.py:89
  235.3 47.6 %scatter_custom_fusion = bf16[9216,1024]{1,0:T(8,128)(2,1)} fusion(s32[8192]{0:T(1024)} %bitcast.246, bf16[]{:T(256)} %constant.39.clone.1, bf16[1024,1024]{1,0:T(8,128)(2,1)} %copy.152), kind=kCustom, calls=%fused_computation.41 | custom fusion | bytes 20972032 | tf_op jit(solution)/shard_map/scatter | solution.py:147
  306.1 49.7 %scatter_custom_fusion.1 = bf16[9216,1024]{1,0:T(8,128)(2,1)} fusion(s32[8192]{0:T(1024)} %bitcast.247, f32[1024,1024]{1,0:T(8,128)} %copy.158, f32[8192]{0:T(1024)S(1)} %div.98, bf16[]{:T(256)} %constant.39.clone.1), kind=kCustom, calls=%fused_computation.40 | custom fusion | flops 16777216 | bytes 23101952 | tf_op jit(solution)/shard_map/scatter | solution.py:181
  355.9 265.9 %all-to-all-done = bf16[32,1,288,1024]{3,2,1,0:T(8,128)(2,1)} async-done(((bf16[32,1,288,1024]{3,2,1,0:T(8,128)(2,1)}), bf16[32,1,288,1024]{3,2,1,0:T(8,128)(2,1)}, u32[]{:S(2)}, u32[]{:S(2)}) %all-to-all-start) | async-done | bytes 18874400 | tf_op jit(solution)/shard_map/all_to_all | solution.py:150
  621.8 78.6 %all-to-all-start.2 = ((bf16[32,1,288,1024]{3,2,1,0:T(8,128)(2,1)}), bf16[32,1,288,1024]{3,2,1,0:T(8,128)(2,1)}, u32[]{:S(2)}, u32[]{:S(2)}) async-start(bf16[32,1,288,1024]{3,2,1,0:T(8,128)(2,1)} %bitcast.204), calls=%async_computation.2 | async-start | bytes 37748736 | tf_op jit(solution)/shard_map/all_to_all | solution.py:184
  717.5 316.2 %all-to-all-done.2 = bf16[32,1,288,1024]{3,2,1,0:T(8,128)(2,1)} async-done(((bf16[32,1,288,1024]{3,2,1,0:T(8,128)(2,1)}), bf16[32,1,288,1024]{3,2,1,0:T(8,128)(2,1)}, u32[]{:S(2)}, u32[]{:S(2)}) %all-to-all-start.2) | async-done | bytes 18874400 | tf_op jit(solution)/shard_map/all_to_all | solution.py:184
  1051.0 17.6 fusion.82
  1068.6 17.4 fusion.81
  1086.0 34.2 %multiply_convert_fusion = (bf16[2,4608,512]{2,1,0:T(8,128)(2,1)}, bf16[2,4608,512]{2,1,0:T(8,128)(2,1)}, bf16[2,4608,512]{2,1,0:T(8,128)(2,1)}) fusion(f32[2,4608,512]{2,1,0:T(8,128)} %fusion.81, f32[2,4608,512]{2,1,0:T(8,128)} %fusion.82, bf16[2,4608,1024]{2,1,0:T(8,128)(2,1)} %bitcast.205, bf16[2,512,1024]{2,1,0:T(8,128)(2,1)S(1)} %copy-done), kind=kOutput, calls=%fused_computation.34 | convolution fusion | flops 9739173888 | bytes 87031808 | tf_op jit(solution)/shard_map/erd,efd->erf/dot_general | solution.py:189
  1153.8 79.2 %all-to-all-start.1 = ((bf16[2,16,288,1024]{3,2,0,1:T(8,128)(2,1)}), bf16[2,16,288,1024]{3,2,0,1:T(8,128)(2,1)}, u32[]{:S(2)}, u32[]{:S(2)}) async-start(bf16[2,16,288,1024]{3,2,0,1:T(8,128)(2,1)} %copy.154), calls=%async_computation.1 | async-start | bytes 37748736 | tf_op jit(solution)/shard_map/all_to_all | solution.py:161
  1233.1 19.3 fusion.83
  1252.4 24.3 add_convert_fusion
  1293.8 272.5 %all-to-all-done.1 = bf16[2,16,288,1024]{3,2,0,1:T(8,128)(2,1)} async-done(((bf16[2,16,288,1024]{3,2,0,1:T(8,128)(2,1)}), bf16[2,16,288,1024]{3,2,0,1:T(8,128)(2,1)}, u32[]{:S(2)}, u32[]{:S(2)}) %all-to-all-start.1) | async-done | bytes 18874400 | tf_op jit(solution)/shard_map/all_to_all | solution.py:161
  1566.3 78.7 %all-to-all-start.3 = ((bf16[2,16,288,1024]{3,2,0,1:T(8,128)(2,1)}), bf16[2,16,288,1024]{3,2,0,1:T(8,128)(2,1)}, u32[]{:S(2)}, u32[]{:S(2)}) async-start(bf16[2,16,288,1024]{3,2,0,1:T(8,128)(2,1)} %copy.160), calls=%async_computation.3 | async-start | bytes 37748736 | tf_op jit(solution)/shard_map/all_to_all | solution.py:207
  1645.8 49.8 %gather_fusion = bf16[8192,1024]{1,0:T(8,128)(2,1)} fusion(bf16[9216,1024]{1,0:T(8,128)(2,1)} %bitcast.29, s32[8192]{0:T(1024)S(1)} %broadcast_clamp_fusion), kind=kCustom, calls=%fused_computation | custom fusion | bytes 33587200 | tf_op jit(solution)/shard_map/gather | solution.py:168
  1695.5 17.9 fusion.1
  1719.2 259.1 %all-to-all-done.3 = bf16[2,16,288,1024]{3,2,0,1:T(8,128)(2,1)} async-done(((bf16[2,16,288,1024]{3,2,0,1:T(8,128)(2,1)}), bf16[2,16,288,1024]{3,2,0,1:T(8,128)(2,1)}, u32[]{:S(2)}, u32[]{:S(2)}) %all-to-all-start.3) | async-done | bytes 18874400 | tf_op jit(solution)/shard_map/all_to_all | solution.py:207
  1978.3 49.5 %gather_fusion.1 = bf16[8192,1024]{1,0:T(8,128)(2,1)} fusion(bf16[9216,1024]{1,0:T(8,128)(2,1)} %bitcast.39, s32[8192]{0:T(1024)S(1)} %broadcast_clamp_fusion), kind=kCustom, calls=%fused_computation.1 | custom fusion | bytes 33587200 | tf_op jit(solution)/shard_map/gather | solution.py:214
  2075.9 21.7 fusion.2
  2097.6 21.7 fusion.5
  2138.4 27.8 fusion.7
  2166.2 27.5 fusion.4
  2258.2 18.0 fusion.86
  2276.1 17.9 fusion.85
  2297.3 17.4 fusion.87
  2314.7 47.6 %reduce-scatter.7.cloned.1.call-done = f32[64,512]{1,0:T(8,128)} async-done(((f32[1024,512]{1,0:T(8,128)}), f32[64,512]{1,0:T(8,128)}) %reduce-scatter.7.cloned.1.call-update) | async-done | bytes 131088 | tf_op jit(solution)/shard_map/reduce_scatter | solution.py:307
  2362.3 76.1 %reduce-scatter.11.cloned.1.call-done = f32[64,1024]{1,0:T(8,128)} async-done(((f32[1024,1024]{1,0:T(8,128)}), f32[64,1024]{1,0:T(8,128)}) %reduce-scatter.11.cloned.1.call-update) | async-done | bytes 262160 | tf_op jit(solution)/shard_map/reduce_scatter | solution.py:309
  2438.3 76.5 %reduce-scatter.5.cloned.1.call-done = f32[64,1024]{1,0:T(8,128)} async-done(((f32[1024,1024]{1,0:T(8,128)}), f32[64,1024]{1,0:T(8,128)}) %reduce-scatter.5.cloned.1.call-update) | async-done | bytes 262160 | tf_op jit(solution)/shard_map/reduce_scatter | solution.py:306
  2532.7 39.6 %all-reduce = (f32[1024]{0:T(1024)}, f32[1024]{0:T(1024)}) all-reduce(f32[1024]{0:T(1024)S(1)} %get-tuple-element.76, f32[1024]{0:T(1024)S(1)} %copy-done.65), channel_id=1, replica_groups=mesh['shard'=16,'rep'=2] {'shard','rep'}, use_global_device_ids=true, to_apply=%region_24.25 | all-reduce | flops 2048 | bytes 16384 | tf_op jit(solution)/shard_map/psum | solution.py:304
  2572.3 70.2 %all-reduce.5.cloned.1.call-done = f32[1024,32]{0,1:T(8,128)} async-done(((f32[1024,32]{0,1:T(8,128)}), f32[1024,32]{0,1:T(8,128)}) %all-reduce.5.cloned.1.call-update) | async-done | bytes 131088 | tf_op jit(solution)/shard_map/psum | solution.py:304
  2642.5 311.2 %all-reduce.7.cloned.1.call-done = (f32[64,1024]{1,0:T(8,128)}, f32[64,512]{1,0:T(8,128)}, f32[64,512]{1,0:T(8,128)}, f32[64,1024]{1,0:T(8,128)}, f32[2,1024,512...) async-done(((f32[64,1024]{1,0:T(8,128)}, f32[64,512]{1,0:T(8,128)}, f32[64,512]{1,0:T(8,128)}, f32[64,1024]{1,0:T(8,128)}, f32[2,1024,512]{2,1,0:T(8,128)}, ...) | async-done | bytes 13369360 | tf_op jit(solution)/shard_map/psum | solution.py:311
  (271 shorter events, 439.0 us)
Async XLA Ops:
  7.2 1078.8 %copy-start = (bf16[2,512,1024]{2,1,0:T(8,128)(2,1)S(1)}, bf16[2,512,1024]{2,1,0:T(8,128)(2,1)}, u32[]{:S(2)}) copy-start(bf16[2,512,1024]{2,1,0:T(8,128)(2,1)} %param.24) | copy-start | bytes 6291460
  7.2 43.7 %all-gather.7.cloned.1.call-start = ((), (), s32[]{:S(2)}) async-start(), calls=%async_computation.9 | async-start | bytes 1114112 | tf_op jit(solution)/shard_map/all_gather | solution.py:90
  7.9 82.0 %all-gather.5.cloned.1.call-start = ((), (), s32[]{:S(2)}) async-start(), calls=%async_computation.8 | async-start | bytes 1114112 | tf_op jit(solution)/shard_map/all_gather | solution.py:91
  8.7 123.8 %all-gather.9.cloned.1.call-start = ((), (), s32[]{:S(2)}) async-start(), calls=%async_computation.10 | async-start | bytes 2228224 | tf_op jit(solution)/shard_map/all_gather | solution.py:89
  9.4 212.8 %all-gather.11.cloned.1.call-start = ((), (), s32[]{:S(2)}) async-start(), calls=%async_computation.11 | async-start | bytes 2228224 | tf_op jit(solution)/shard_map/all_gather | solution.py:92
  12.9 29.4 copy-start.66
  13.5 123.8 %copy-start.26 = (f32[1024,32]{0,1:T(8,128)}, f32[1024,32]{0,1:T(8,128)S(1)}, u32[]{:S(2)}) copy-start(f32[1024,32]{0,1:T(8,128)S(1)} %get-tuple-element.106) | copy-start | bytes 393220
  13.5 123.8 %copy-start.28 = (f32[1024,32]{0,1:T(8,128)}, f32[1024,32]{0,1:T(8,128)S(1)}, u32[]{:S(2)}) copy-start(f32[1024,32]{0,1:T(8,128)S(1)} %get-tuple-element.107) | copy-start | bytes 393220
  40.8 91.7 %copy-start.59 = (f32[1024]{0:T(1024)}, f32[1024]{0:T(1024)S(1)}, u32[]{:S(2)}) copy-start(f32[1024]{0:T(1024)S(1)} %add_rsqrt_fusion.1) | copy-start | bytes 12292
  54.5 125.4 %copy-start.9 = (bf16[1024,8,32]{0,2,1:T(8,128)(2,1)}, bf16[1024,8,32]{0,2,1:T(8,128)(2,1)S(1)}, u32[]{:S(2)}) copy-start(bf16[1024,8,32]{0,2,1:T(8,128)(2,1)S(1)} %get-tuple-element.98) | copy-start | bytes 1572868
  54.5 125.4 %copy-start.11 = (bf16[1024,8,32]{0,2,1:T(8,128)(2,1)}, bf16[1024,8,32]{0,2,1:T(8,128)(2,1)S(1)}, u32[]{:S(2)}) copy-start(bf16[1024,8,32]{0,2,1:T(8,128)(2,1)S(1)} %get-tuple-element.99) | copy-start | bytes 1572868
  138.3 41.5 %copy-start.13 = (bf16[512,16,64]{0,2,1:T(8,128)(2,1)}, bf16[512,16,64]{0,2,1:T(8,128)(2,1)S(1)}, u32[]{:S(2)}) copy-start(bf16[512,16,64]{0,2,1:T(8,128)(2,1)S(1)} %get-tuple-element.102) | copy-start | bytes 3145732
  282.9 338.9 %all-to-all-start = ((bf16[32,1,288,1024]{3,2,1,0:T(8,128)(2,1)}), bf16[32,1,288,1024]{3,2,1,0:T(8,128)(2,1)}, u32[]{:S(2)}, u32[]{:S(2)}) async-start(bf16[32,1,288,1024]{3,2,1,0:T(8,128)(2,1)} %bitcast.203), calls=%async_computation | async-start | bytes 37748736 | tf_op jit(solution)/shard_map/all_to_all | solution.py:150
  305.8 50.0 %copy-start.17 = (f32[1024,8]{1,0:T(8,128)}, f32[1024,8]{1,0:T(8,128)S(1)}, u32[]{:S(2)}) copy-start(f32[1024,8]{1,0:T(8,128)S(1)} %copy.148) | copy-start | bytes 98308
  621.8 411.9 %all-to-all-start.2 = ((bf16[32,1,288,1024]{3,2,1,0:T(8,128)(2,1)}), bf16[32,1,288,1024]{3,2,1,0:T(8,128)(2,1)}, u32[]{:S(2)}, u32[]{:S(2)}) async-start(bf16[32,1,288,1024]{3,2,1,0:T(8,128)(2,1)} %bitcast.204), calls=%async_computation.2 | async-start | bytes 37748736 | tf_op jit(solution)/shard_map/all_to_all | solution.py:184
  1153.8 79.2 %copy-start.70 = (bf16[2,1024,512]{2,1,0:T(8,128)(2,1)S(1)}, bf16[2,1024,512]{2,1,0:T(8,128)(2,1)}, u32[]{:S(2)}) copy-start(bf16[2,1024,512]{2,1,0:T(8,128)(2,1)} %param.22) | copy-start | bytes 6291460
  1153.8 412.5 %all-to-all-start.1 = ((bf16[2,16,288,1024]{3,2,0,1:T(8,128)(2,1)}), bf16[2,16,288,1024]{3,2,0,1:T(8,128)(2,1)}, u32[]{:S(2)}, u32[]{:S(2)}) async-start(bf16[2,16,288,1024]{3,2,0,1:T(8,128)(2,1)} %copy.154), calls=%async_computation.1 | async-start | bytes 37748736 | tf_op jit(solution)/shard_map/all_to_all | solution.py:161
  1293.8 351.3 %copy-start.48 = (s32[8192,1]{0,1:T(1,128)S(1)}, s32[8192,1]{0,1:T(1,128)}, u32[]{:S(2)}) copy-start(s32[8192,1]{0,1:T(1,128)} %compare_select_fusion) | copy-start | bytes 98308
  1293.8 351.3 %copy-start.43 = (f32[8,2,512]{2,1,0:T(2,128)S(1)}, f32[8,2,512]{2,1,0:T(2,128)}, u32[]{:S(2)}) copy-start(f32[8,2,512]{2,1,0:T(2,128)} %copy-done.42) | copy-start | bytes 98308
  1293.8 351.3 %copy-start.50 = (f32[8,2,512]{2,1,0:T(2,128)S(1)}, f32[8,2,512]{2,1,0:T(2,128)}, u32[]{:S(2)}) copy-start(f32[8,2,512]{2,1,0:T(2,128)} %copy-done.49) | copy-start | bytes 98308
  1293.8 351.4 %copy-start.45 = (f32[8,2,512]{2,1,0:T(2,128)S(1)}, f32[8,2,512]{2,1,0:T(2,128)}, u32[]{:S(2)}) copy-start(f32[8,2,512]{2,1,0:T(2,128)} %copy-done.44) | copy-start | bytes 98308
  1293.8 351.4 %copy-start.52 = (f32[8,2,512]{2,1,0:T(2,128)S(1)}, f32[8,2,512]{2,1,0:T(2,128)}, u32[]{:S(2)}) copy-start(f32[8,2,512]{2,1,0:T(2,128)} %copy-done.51) | copy-start | bytes 98308
  1566.3 412.0 %all-to-all-start.3 = ((bf16[2,16,288,1024]{3,2,0,1:T(8,128)(2,1)}), bf16[2,16,288,1024]{3,2,0,1:T(8,128)(2,1)}, u32[]{:S(2)}, u32[]{:S(2)}) async-start(bf16[2,16,288,1024]{3,2,0,1:T(8,128)(2,1)} %copy.160), calls=%async_computation.3 | async-start | bytes 37748736 | tf_op jit(solution)/shard_map/all_to_all | solution.py:207
  1645.0 669.7 %reduce-scatter.9.cloned.1.call-start = ((), (), s32[]{:S(2)}) async-start(), calls=%async_computation.14 | async-start | bytes 2228224 | tf_op jit(solution)/shard_map/reduce_scatter | solution.py:308
  1645.8 49.8 %copy-start.18 = (f32[1024,8]{1,0:T(8,128)S(1)}, f32[1024,8]{1,0:T(8,128)}, u32[]{:S(2)}) copy-start(f32[1024,8]{1,0:T(8,128)} %copy-done.17) | copy-start | bytes 98308
  1719.2 329.0 %copy-start.38 = (bf16[1024,32]{0,1:T(8,128)(2,1)}, bf16[1024,32]{0,1:T(8,128)(2,1)S(1)}, u32[]{:S(2)}) copy-start(bf16[1024,32]{0,1:T(8,128)(2,1)S(1)} %select_reduce_fusion) | copy-start | bytes 196612
  2138.3 223.9 %reduce-scatter.7.cloned.1.call-start = ((), (), s32[]{:S(2)}) async-start(), calls=%async_computation.13 | async-start | bytes 2228224 | tf_op jit(solution)/shard_map/reduce_scatter | solution.py:307
  2166.2 27.5 copy-start.14
  2224.8 213.6 %reduce-scatter.11.cloned.1.call-start = ((), (), s32[]{:S(2)}) async-start(), calls=%async_computation.15 | async-start | bytes 4456448 | tf_op jit(solution)/shard_map/reduce_scatter | solution.py:309
  2232.2 282.6 %reduce-scatter.5.cloned.1.call-start = ((), (), s32[]{:S(2)}) async-start(), calls=%async_computation.12 | async-start | bytes 4456448 | tf_op jit(solution)/shard_map/reduce_scatter | solution.py:306
  2257.9 384.6 %all-reduce.5.cloned.1.call-start = ((), (), s32[]{:S(2)}) async-start(), calls=%async_computation.16 | async-start | bytes 262144 | tf_op jit(solution)/shard_map/psum | solution.py:304
  2297.0 656.7 %all-reduce.7.cloned.1.call-start = ((), (), s32[]{:S(2)}) async-start(), calls=%async_computation.17 | async-start | bytes 26738688 | tf_op jit(solution)/shard_map/psum | solution.py:311
  (56 other events, 418.1 us)
Sparse Core Ops, SparseCore 0:
  10.2 40.6 all-gather.6
  53.1 36.8 all-gather.4
  92.1 40.3 all-gather.8
  134.5 40.1 all-gather.10
  2138.4 135.2 reduce-scatter.8
  2277.8 84.4 reduce-scatter.6
  2366.7 71.5 reduce-scatter.10
  2443.3 71.4 reduce-scatter.4
  2520.9 121.5 all-reduce.4
  2645.4 308.1 all-reduce.6
where the time goes:
time: 2990 us; the launch traced here: 2980 us
  waiting for transfers between devices  1780 us (60%)
  matrix products  410 us (14%)
  local copies, waits for them, and re-layouts  281 us (9%)
  starting transfers between devices  243 us (8%)
  other arithmetic  210 us (7%)
  blocking collectives  39.6 us (1%)
    all_to_all x1, waiting for transfers between devices, on_device(): lax.all_to_all(outgoing_slope, 'shard', split_axis=0, concat_axis=1, tile...  316 us
    psum x1, waiting for transfers between devices, on_device(): lax.psum((owned[0], owned[1], owned[2], owned[3], gate_grad, up_grad, dow...  311 us
    all_to_all x1, waiting for transfers between devices, on_device(): lax.all_to_all(expert_out.reshape(local_experts, -1, CAP, D), 'shard', sp...  273 us
    all_to_all x1, waiting for transfers between devices, on_device(): lax.all_to_all(outgoing, 'shard', split_axis=0, concat_axis=1, tiled=True)  266 us
    all_to_all x1, waiting for transfers between devices, on_device(): lax.all_to_all(row_slope.reshape(local_experts, -1, CAP, D), 'shard', spl...  259 us
    all_to_all x1, starting transfers between devices, on_device(): lax.all_to_all(expert_out.reshape(local_experts, -1, CAP, D), 'shard', sp...  79.2 us
    all_to_all x1, starting transfers between devices, on_device(): lax.all_to_all(row_slope.reshape(local_experts, -1, CAP, D), 'shard', spl...  78.7 us
    all_to_all x1, starting transfers between devices, on_device(): lax.all_to_all(outgoing_slope, 'shard', split_axis=0, concat_axis=1, tile...  78.6 us
  transfers between devices with their start and end apart: 14, of which 12 were waited for; matrix products, arithmetic and copies ran while one was open for 18% of the time, Pallas kernels for 0%

commit v1 on v0

v1 whole, which is shorter than its diff:
```python
import functools

import jax
import jax.numpy as jnp
import numpy as np
from jax import lax
from jax.experimental import pallas as pl
from jax.experimental.pallas import tpu as pltpu
from jax.sharding import PartitionSpec as P

D = 1024
HEADS = 16
KV = 8
HD = 64
EXPERTS = 32
TOP = 8
CAP = 288
ABSENT = -100000


epsilon = 1e-06
masked_score = -1e30
rotary_base = 10000.0


def chip_cycle(count):
    if count % 4 == 0 and count >= 8:
        wide = count // 4
        tall = 4
    else:
        return list(range(count))
    if wide == 1:
        return list(range(count))
    order = [row * wide for row in range(tall)]
    for step, row in enumerate(reversed(range(tall))):
        columns = range(1, wide) if step % 2 == 0 else reversed(range(1, wide))
        order += [row * wide + column for column in columns]
    return order


class Ring:
    def __init__(self, shards):
        chips = chip_cycle(shards // 2)
        count = len(chips)
        self.steps = count
        self.forward = []
        for place in range(count):
            here, there = chips[place], chips[(place + 1) % count]
            self.forward += [(2 * here, 2 * there), (2 * there + 1, 2 * here + 1)]
        self.swap = [(s, s ^ 1) for s in range(shards)]
        near = np.zeros((shards, count), np.int32)
        far = np.zeros((shards, count), np.int32)
        for place in range(count):
            for core in range(2):
                way = 1 - 2 * core
                for step in range(count):
                    me = 2 * chips[place] + core
                    near[me, step] = 2 * chips[(place - way * step) % count] + core
                    far[me, step] = 2 * chips[(place + way * step) % count] + 1 - core
        self.near, self.far = near, far

    def hop(self, array):
        return lax.ppermute(array, "shard", self.forward)

    def cross(self, array):
        return lax.ppermute(array, "shard", self.swap)

    def gather(self, array):
        near, far = [array], [self.cross(array)]
        for _ in range(self.steps - 1):
            near.append(self.hop(near[-1]))
            far.append(self.cross(near[-1]))
        return near, far


def rope_tables(length_rows, head_width):
    halfway = head_width // 2
    index_float = jnp.arange(halfway, dtype=jnp.float32)
    frequency = jnp.exp(-jnp.log(rotary_base) * index_float * 2.0 / head_width)
    angle = jnp.arange(length_rows, dtype=jnp.float32)[:, None] * frequency[None, :]
    return (jnp.cos(angle)[:, None, :], jnp.sin(angle)[:, None, :])


def rotate(values, cosine, sine):
    halfway = values.shape[-1] // 2
    first_half = values[..., :halfway]
    second_half = values[..., halfway:]
    return jnp.concatenate(
        [first_half * cosine - second_half * sine, second_half * cosine + first_half * sine],
        axis=-1,
    )


def unrotate(slopes, cosine, sine):
    halfway = slopes.shape[-1] // 2
    first_half = slopes[..., :halfway]
    second_half = slopes[..., halfway:]
    return jnp.concatenate(
        [first_half * cosine + second_half * sine, second_half * cosine - first_half * sine],
        axis=-1,
    )


def block_scores(query_block, keys, start_row, length, scale):
    products = (
        jnp.einsum("qhgd,khd->hgqk", query_block, keys, preferred_element_type=jnp.float32) * scale
    )
    query_place = start_row + jnp.arange(query_block.shape[0], dtype=jnp.int32)
    key_place = jnp.arange(keys.shape[0], dtype=jnp.int32)
    allowed = (key_place[None, :] <= query_place[:, None]) & (key_place[None, :] < length)
    return jnp.where(allowed[None, None], products, masked_score)


def dot(left, right):
    return jnp.dot(left, right, preferred_element_type=jnp.float32)


def experts_kernel(
    local_experts,
    chained,
    where_ref,
    tokens_ref,
    slope_ref,
    slot_row_ref,
    slot_column_ref,
    mask_ref,
    router_ref,
    in_ref,
    in_turned_ref,
    down_ref,
    down_turned_ref,
    *rest,
):
    rest = rest[5:] if chained else rest
    (
        back_ref,
        mix_ref,
        rows_ref,
        routed_ref,
        hidden_ref,
        slopes_ref,
        gate_slope_ref,
        mixed_rows,
        back_rows,
    ) = rest
    expert = pl.program_id(0)
    tokens = tokens_ref.shape[0]
    half = hidden_ref.shape[-1]
    bf16 = jnp.bfloat16

    slot_row = slot_row_ref[0, 0]
    place = lax.broadcasted_iota(jnp.int32, (CAP, tokens), 0)
    taken = slot_row == place
    pick = jnp.where(taken, 1.0, 0.0).astype(bf16)
    rows = dot(pick, tokens_ref[...]).astype(bf16)
    slope_rows = dot(pick, slope_ref[...])
    chosen = dot(pick, mask_ref[0])
    logits = dot(rows, router_ref[...])
    kept = jnp.where(chosen > 0.5, logits, masked_score)
    top = jnp.max(kept, axis=-1, keepdims=True)
    powered = jnp.exp(kept - top) * chosen
    total = jnp.sum(powered, axis=-1, keepdims=True)
    lane = lax.broadcasted_iota(jnp.int32, powered.shape, 1)
    mine = lane == where_ref[1] * local_experts + expert
    gate = jnp.sum(jnp.where(mine, powered, 0.0), axis=-1, keepdims=True) / jnp.where(
        total > 0.0, total, 1.0
    )
    both = dot(rows, in_ref[0])
    gate_part, up_part = both[:, :half], both[:, half:]
    sigma = 1.0 / (1.0 + jnp.exp(-gate_part))
    silu = gate_part * sigma
    hidden = (silu * up_part).astype(bf16)
    out = dot(hidden, down_ref[0]).astype(bf16).astype(jnp.float32)
    gate_slope = jnp.sum(out * slope_rows, axis=-1, keepdims=True)
    gate_slope_ref[0, 0] = jnp.sum(jnp.where(taken, gate_slope, 0.0), axis=0, keepdims=True)
    routed = (gate * slope_rows).astype(bf16)
    hidden_slope = dot(routed, down_turned_ref[0])
    gate_back = (hidden_slope * up_part * sigma * (1.0 + gate_part * (1.0 - sigma))).astype(bf16)
    up_back = (hidden_slope * silu).astype(bf16)
    slopes = jnp.concatenate([gate_back, up_back], axis=-1)
    back = dot(slopes, in_turned_ref[0]).astype(bf16)
    start = pl.multiple_of(expert * CAP, CAP)
    mixed_rows[pl.ds(start, CAP), :] = (gate * out).astype(bf16)
    back_rows[pl.ds(start, CAP), :] = back
    rows_ref[0] = rows
    routed_ref[0] = routed
    hidden_ref[0] = hidden
    slopes_ref[0] = slopes

    @pl.when(expert == local_experts - 1)
    def _():
        column = lax.broadcasted_iota(jnp.int32, (tokens, local_experts * CAP), 1)
        spread = jnp.zeros(column.shape, jnp.float32)
        for e in range(local_experts):
            spread = jnp.where(column - e * CAP == slot_column_ref[0, :, e : e + 1], 1.0, spread)
        spread = spread.astype(bf16)
        back_ref[...] = dot(spread, back_rows[...]).astype(bf16)
        mix_ref[...] = dot(spread, mixed_rows[...]).astype(bf16)


def experts_block(where, tokens_block, slope_block, plan, weights, kept):
    slot_row, slot_column, mask = plan
    router, into, into_turned, down, down_turned = weights
    tokens, width = tokens_block.shape
    blocks = slot_row.shape[0]
    local_experts, half = down.shape[0], down.shape[1]
    bf16 = jnp.bfloat16
    chained = kept is not None
    once = pl.Buffered(1)
    any_spec = pl.BlockSpec(memory_space=pl.ANY)
    in_specs = [
        pl.BlockSpec((tokens, width), lambda e, w: (0, 0), pipeline_mode=once),
        pl.BlockSpec((tokens, width), lambda e, w: (0, 0), pipeline_mode=once),
        pl.BlockSpec((1, 1, 1, tokens), lambda e, w: (w[0], e, 0, 0)),
        pl.BlockSpec((1, tokens, local_experts), lambda e, w: (w[0], 0, 0), pipeline_mode=once),
        pl.BlockSpec((1, tokens, EXPERTS), lambda e, w: (w[0], 0, 0), pipeline_mode=once),
        pl.BlockSpec((width, EXPERTS), lambda e, w: (0, 0), pipeline_mode=once),
        pl.BlockSpec((1, width, 2 * half), lambda e, w: (e, 0, 0)),
        pl.BlockSpec((1, 2 * half, width), lambda e, w: (e, 0, 0)),
        pl.BlockSpec((1, half, width), lambda e, w: (e, 0, 0)),
        pl.BlockSpec((1, width, half), lambda e, w: (e, 0, 0)),
    ]
    shapes = [
        jax.ShapeDtypeStruct((tokens, width), bf16),
        jax.ShapeDtypeStruct((tokens, width), bf16),
        jax.ShapeDtypeStruct((local_experts, blocks * CAP, width), bf16),
        jax.ShapeDtypeStruct((local_experts, blocks * CAP, width), bf16),
        jax.ShapeDtypeStruct((local_experts, blocks * CAP, half), bf16),
        jax.ShapeDtypeStruct((local_experts, blocks * CAP, 2 * half), bf16),
        jax.ShapeDtypeStruct((blocks, local_experts, 1, tokens), jnp.float32),
    ]
    out_specs = [
        pl.BlockSpec((tokens, width), lambda e, w: (0, 0), pipeline_mode=once),
        pl.BlockSpec((tokens, width), lambda e, w: (0, 0), pipeline_mode=once),
        pl.BlockSpec((1, CAP, width), lambda e, w: (e, w[0], 0)),
        pl.BlockSpec((1, CAP, width), lambda e, w: (e, w[0], 0)),
        pl.BlockSpec((1, CAP, half), lambda e, w: (e, w[0], 0)),
        pl.BlockSpec((1, CAP, 2 * half), lambda e, w: (e, w[0], 0)),
        pl.BlockSpec((1, 1, 1, tokens), lambda e, w: (w[0], e, 0, 0)),
    ]
    operands = [
        tokens_block, slope_block, slot_row, slot_column, mask,
        router, into, into_turned, down, down_turned,
    ]
    aliases = {}
    if chained:
        first = 1 + len(operands)
        operands += list(kept)
        in_specs += [any_spec] * 5
        aliases = {first + place: 2 + place for place in range(5)}
    flops = local_experts * 2 * CAP * (2 * tokens * width + 6 * width * half + 2 * tokens * width)
    return pl.pallas_call(
        functools.partial(experts_kernel, local_experts, chained),
        out_shape=shapes,
        grid_spec=pltpu.PrefetchScalarGridSpec(
            num_scalar_prefetch=1,
            grid=(local_experts,),
            in_specs=in_specs,
            out_specs=out_specs,
            scratch_shapes=[
                pltpu.VMEM((local_experts * CAP, width), bf16),
                pltpu.VMEM((local_experts * CAP, width), bf16),
            ],
        ),
        input_output_aliases=aliases,
        compiler_params=pltpu.CompilerParams(vmem_limit_bytes=52 * 1024 * 1024),
        cost_estimate=pl.CostEstimate(
            flops=flops, bytes_accessed=20 * 1024 * 1024, transcendentals=0
        ),
    )(where, *operands)


def on_device(
    shards,
    reps,
    layer_input,
    attention_gain,
    query_weight,
    key_weight,
    value_weight,
    output_weight,
    expert_gain,
    router_weight,
    gate_weight,
    up_weight,
    down_weight,
    lengths,
    routes,
    cotangent,
):
    ring = Ring(shards)
    me = lax.axis_index("shard")
    tokens = layer_input.shape[0]
    local_experts = gate_weight.shape[0]
    groups = HEADS // KV
    scale = HD ** (-0.5)
    length = lengths[0]
    bf16 = jnp.bfloat16

    packed = jnp.concatenate([query_weight, key_weight, value_weight, output_weight], axis=1)
    packed_full = lax.all_gather(packed, "shard", axis=0, tiled=True)
    input_full = packed_full[:, : (HEADS + 2 * KV) * HD]
    output_full = packed_full[:, (HEADS + 2 * KV) * HD :]

    expert_ids = jnp.arange(EXPERTS, dtype=jnp.int32)
    picks = jnp.any(routes[:, None, :] == expert_ids[None, :, None], axis=-1)
    picks_turned = picks.T
    earlier = jnp.triu(jnp.ones((tokens, tokens), bf16), k=1)
    ranks = dot(picks_turned.astype(bf16), earlier).astype(jnp.int32)
    slots_home = jnp.where(picks_turned, ranks, ABSENT)
    slots_all = lax.all_gather(slots_home, "shard", axis=0, tiled=False)
    slots_mine = lax.dynamic_slice_in_dim(slots_all, me * local_experts, local_experts, axis=1)
    slot_row = slots_mine[:, :, None, :]
    slot_column = jnp.swapaxes(slots_mine, 1, 2)
    mask = jnp.swapaxes((slots_all >= 0).astype(bf16), 1, 2)
    plan = (slot_row, slot_column, mask)
    into = jnp.concatenate([gate_weight, up_weight], axis=-1)
    weights = (
        router_weight,
        into,
        jnp.swapaxes(into, 1, 2),
        down_weight,
        jnp.swapaxes(down_weight, 1, 2),
    )

    valid = (jnp.arange(tokens, dtype=jnp.int32) < length)[:, None]
    slope_low = jnp.where(valid, cotangent, jnp.zeros_like(cotangent))
    slope_low, packed_full, slots_all = lax.optimization_barrier(
        (slope_low, packed_full, slots_all)
    )
    slope_near, slope_far = ring.gather(slope_low)
    slope = slope_low.astype(jnp.float32)

    inputs_f = layer_input.astype(jnp.float32)
    first_scale = lax.rsqrt(jnp.mean(inputs_f * inputs_f, axis=-1, keepdims=True) + epsilon)
    base_one = inputs_f * first_scale
    normed_one = (base_one * attention_gain).astype(bf16)
    cosine, sine = rope_tables(tokens, HD)
    heads_pre = dot(normed_one, input_full)
    query_pre = heads_pre[:, : HEADS * HD]
    key_pre = heads_pre[:, HEADS * HD : (HEADS + KV) * HD]
    values = heads_pre[:, (HEADS + KV) * HD :].astype(bf16).reshape(tokens, KV, HD)
    queries = (
        rotate(query_pre.reshape(tokens, HEADS, HD), cosine, sine)
        .astype(bf16)
        .reshape(tokens, KV, groups, HD)
    )
    keys = rotate(key_pre.reshape(tokens, KV, HD), cosine, sine).astype(bf16)
    block = min(512, tokens)
    block_count = tokens // block
    mixed_parts = []
    log_totals = []
    for block_index in range(block_count):
        start_row = block_index * block
        scores = block_scores(
            queries[start_row : start_row + block], keys, start_row, length, scale
        )
        maximum = jnp.max(scores, axis=-1, keepdims=True)
        powered = jnp.exp(scores - maximum)
        total = jnp.sum(powered, axis=-1, keepdims=True)
        probs = (powered / total).astype(bf16)
        log_totals.append(maximum + jnp.log(total))
        mixed_parts.append(
            jnp.einsum("hgqk,khd->qhgd", probs, values, preferred_element_type=jnp.float32)
        )
    attended = jnp.concatenate(mixed_parts, axis=0).reshape(tokens, HEADS * HD).astype(bf16)
    residual = inputs_f + dot(attended, output_full)
    second_scale = lax.rsqrt(jnp.mean(residual * residual, axis=-1, keepdims=True) + epsilon)
    base_two = residual * second_scale
    normed_two = (base_two * expert_gain).astype(bf16)

    near, far = ring.gather(normed_two)
    near_table, far_table = jnp.asarray(ring.near)[me], jnp.asarray(ring.far)[me]
    kept = None
    back_near, back_far, mix_near, mix_far = [], [], [], []
    for step in range(ring.steps):
        for side in ("far", "near"):
            here = side == "near"
            table = near_table if here else far_table
            results = experts_block(
                jnp.stack([table[step], me]).astype(jnp.int32),
                near[step] if here else far[step],
                slope_near[step] if here else slope_far[step],
                plan,
                weights,
                kept,
            )
            kept = results[2:]
            (back_near if here else back_far).append(results[0])
            (mix_near if here else mix_far).append(results[1])

    def ring_sum(near_parts, far_parts, after=None):
        def chip_part(step, arrived):
            parts = near_parts[step].astype(jnp.float32) + ring.cross(far_parts[step]).astype(
                jnp.float32
            )
            return parts if arrived is None else parts + arrived.astype(jnp.float32)

        total = None
        for step in range(1, ring.steps):
            total = ring.hop(chip_part(step, total).astype(bf16))
        return chip_part(0, total)

    normed_slope = ring_sum(back_near, back_far)
    rows_all, routed_all, hidden_all, slopes_all, gate_slopes = kept
    half = down_weight.shape[1]
    in_grad = jnp.einsum("erd,erf->edf", rows_all, slopes_all, preferred_element_type=jnp.float32)
    down_grad = jnp.einsum(
        "erf,erd->efd", hidden_all, routed_all, preferred_element_type=jnp.float32
    )

    gate_slope = lax.all_to_all(
        gate_slopes.reshape(shards, local_experts, tokens),
        "shard",
        split_axis=0,
        concat_axis=0,
        tiled=True,
    ).reshape(EXPERTS, tokens)
    logits = lax.dot_general(
        router_weight, normed_two, (((0,), (1,)), ((), ())), preferred_element_type=jnp.float32
    )
    kept_logits = jnp.where(picks_turned, logits, masked_score)
    powered = jnp.where(
        picks_turned, jnp.exp(kept_logits - jnp.max(kept_logits, axis=0, keepdims=True)), 0.0
    )
    gates = powered / jnp.sum(powered, axis=0, keepdims=True)
    mean_slope = jnp.sum(gates * gate_slope, axis=0, keepdims=True)
    logit_slope = (gates * (gate_slope - mean_slope)).astype(bf16)
    router_grad = lax.dot_general(
        normed_two, logit_slope, (((0,), (1,)), ((), ())), preferred_element_type=jnp.float32
    )
    normed_slope = normed_slope + lax.dot_general(
        logit_slope, router_weight, (((0,), (1,)), ((), ())), preferred_element_type=jnp.float32
    )

    mix_near, mix_far, normed_slope = lax.optimization_barrier((mix_near, mix_far, normed_slope))
    layer_output = (residual + ring_sum(mix_near, mix_far)).astype(bf16)

    expert_gain_grad = jnp.sum(normed_slope * base_two, axis=0)
    scaled_two = normed_slope * expert_gain
    residual_slope = (
        slope
        + second_scale * scaled_two
        - base_two
        * second_scale
        * second_scale
        * jnp.mean(scaled_two * residual, axis=-1, keepdims=True)
    )
    branch_slope = residual_slope.astype(bf16)
    output_grad = jnp.einsum(
        "sc,sd->cd", attended, branch_slope, preferred_element_type=jnp.float32
    )
    attended_slope = (
        jnp.einsum("sd,cd->sc", branch_slope, output_full, preferred_element_type=jnp.float32)
        .astype(bf16)
        .reshape(tokens, KV, groups, HD)
    )
    query_parts = []
    key_total = jnp.zeros((tokens, KV, HD), jnp.float32)
    value_total = jnp.zeros((tokens, KV, HD), jnp.float32)
    for block_index in range(block_count):
        start_row = block_index * block
        query_block = queries[start_row : start_row + block]
        mixed_slope = attended_slope[start_row : start_row + block]
        scores = block_scores(query_block, keys, start_row, length, scale)
        weights_soft = jnp.exp(scores - log_totals[block_index])
        probs = weights_soft.astype(bf16)
        probs_slope = jnp.einsum(
            "qhgd,khd->hgqk", mixed_slope, values, preferred_element_type=jnp.float32
        )
        centre = jnp.sum(weights_soft * probs_slope, axis=-1, keepdims=True)
        score_slope = (weights_soft * (probs_slope - centre)).astype(bf16)
        query_parts.append(
            jnp.einsum("hgqk,khd->qhgd", score_slope, keys, preferred_element_type=jnp.float32)
            * scale
        )
        key_total = (
            key_total
            + jnp.einsum(
                "hgqk,qhgd->khd", score_slope, query_block, preferred_element_type=jnp.float32
            )
            * scale
        )
        value_total = value_total + jnp.einsum(
            "hgqk,qhgd->khd", probs, mixed_slope, preferred_element_type=jnp.float32
        )
    query_slope = jnp.concatenate(query_parts, axis=0).reshape(tokens, HEADS, HD)
    query_pre_slope = unrotate(query_slope, cosine, sine).reshape(tokens, HEADS * HD).astype(bf16)
    key_pre_slope = unrotate(key_total, cosine, sine).reshape(tokens, KV * HD).astype(bf16)
    value_pre_slope = value_total.reshape(tokens, KV * HD).astype(bf16)
    pre_slopes = jnp.concatenate([query_pre_slope, key_pre_slope, value_pre_slope], axis=1)
    input_grad = jnp.einsum("sd,sc->dc", normed_one, pre_slopes, preferred_element_type=jnp.float32)
    normed_one_slope = jnp.einsum(
        "sc,dc->sd", pre_slopes, input_full, preferred_element_type=jnp.float32
    )
    attention_gain_grad = jnp.sum(normed_one_slope * base_one, axis=0)
    scaled_one = normed_one_slope * attention_gain
    input_slope = (
        residual_slope
        + first_scale * scaled_one
        - base_one
        * first_scale
        * first_scale
        * jnp.mean(scaled_one * inputs_f, axis=-1, keepdims=True)
    )
    input_gradient = input_slope.astype(bf16)

    def rep_sum(*arrays):
        if reps != 2:
            return lax.psum(arrays, "rep")
        low = [array.astype(bf16) for array in arrays]
        other = [lax.ppermute(array, "rep", [(0, 1), (1, 0)]) for array in low]
        return tuple(
            a.astype(jnp.float32) + b.astype(jnp.float32) for a, b in zip(low, other, strict=True)
        )

    in_sum, down_sum = rep_sum(in_grad, down_grad)
    gate_sum, up_sum = in_sum[..., :half], in_sum[..., half:]
    early = lax.psum(
        (expert_gain_grad, router_grad), ("shard", "rep")
    )
    gain_sum = lax.psum(attention_gain_grad, ("shard", "rep"))
    output_sum = lax.psum(
        lax.psum_scatter(output_grad, "shard", scatter_dimension=0, tiled=True), "rep"
    )
    input_sum = lax.psum(
        lax.psum_scatter(input_grad, "shard", scatter_dimension=0, tiled=True), "rep"
    )
    return (
        layer_output,
        input_gradient,
        gain_sum,
        input_sum[:, : HEADS * HD],
        input_sum[:, HEADS * HD : (HEADS + KV) * HD],
        input_sum[:, (HEADS + KV) * HD :],
        output_sum,
        early[0],
        early[1],
        gate_sum,
        up_sum,
        down_sum,
    )


def solution(mesh):
    return jax.shard_map(
        functools.partial(on_device, mesh.shape["shard"], mesh.shape["rep"]),
        mesh=mesh,
        in_specs=(
            P(("shard", "rep"), None),
            P(),
            P("shard", None),
            P("shard", None),
            P("shard", None),
            P("shard", None),
            P(),
            P(),
            P("shard", None, None),
            P("shard", None, None),
            P("shard", None, None),
            P(("shard", "rep")),
            P(("shard", "rep"), None),
            P(("shard", "rep"), None),
        ),
        out_specs=(
            P(("shard", "rep"), None),
            P(("shard", "rep"), None),
            P(),
            P("shard", None),
            P("shard", None),
            P("shard", None),
            P("shard", None),
            P(),
            P(),
            P("shard", None, None),
            P("shard", None, None),
            P("shard", None, None),
        ),
        check_vma=False,
    )
```

time: 2990 us -> 1500 us (0.50)
  waiting for transfers between devices: 1780 us -> 549 us
  Pallas kernels: 0 us -> 315 us
  starting transfers between devices: 243 us -> 35.4 us
  local copies, waits for them, and re-layouts: 281 us -> 92.5 us
  matrix products: 410 us -> 264 us
    all_to_all x4 -> x1, waiting for transfers between devices: 1110 us -> 21.7 us  [on_device(): lax.all_to_all(gate_slopes.reshape(shards, local_experts, tokens), 'shard...]
    psum x2, waiting for transfers between devices: 381 us -> 59.5 us  [the longest x1 59.5 us: on_device(): early = lax.psum((expert_gain_grad, router_grad), ('shard', 'rep'))]
    pallas_call x0 -> x16, Pallas kernels: none -> 315 us  [experts_block(): pl.pallas_call(functools.partial(experts_kernel, local_experts, chained),...]
    ppermute x0 -> x62, waiting for transfers between devices: none -> 300 us  [the longest x28 245 us: hop(): return lax.ppermute(array, 'shard', self.forward)]
    all_to_all x4 -> x1, starting transfers between devices: 242 us -> 3.51 us  [on_device(): lax.all_to_all(gate_slopes.reshape(shards, local_experts, tokens), 'shard...]
    dot_general x22 -> x10, matrix products: 229 us -> 82.3 us  [the longest x1 29.6 us: on_device(): jnp.einsum('erd,erf->edf', rows_all, slopes_all, preferred_element_type=j...]
    gather x2 -> x0, local copies, waits for them, and re-layouts: 99.2 us -> none  [the longest x1 49.8 us: on_device(): picked = returned.reshape(EXPERTS * CAP, D)[targets].reshape(tokens, TOP, D)]
    reduce_scatter x1, waiting for transfers between devices: 76.1 us -> 0.01 us  [on_device(): lax.psum_scatter(output_grad, 'shard', scatter_dimension=0, tiled=True)]
  transfers between devices with their start and end apart: 14 -> 69, of which waited for: 12 -> 19; matrix products, arithmetic and copies ran while one was open for 18% -> 18% of each run, Pallas kernels for 0% -> 21%
where the time goes in v1:
time: 1500 us
  waiting for transfers between devices  549 us (37%)
  Pallas kernels  315 us (21%)
  matrix products  264 us (18%)
  other arithmetic  188 us (13%)
  local copies, waits for them, and re-layouts  92.5 us (6%)
  blocking collectives  38.5 us (3%)
  starting transfers between devices  35.4 us (2%)
  between operations  16.9 us (1%)
    pallas_call x16, Pallas kernels, experts_block(): pl.pallas_call(functools.partial(experts_kernel, local_experts, chained),...  315 us
    ppermute x28, waiting for transfers between devices, hop(): return lax.ppermute(array, 'shard', self.forward)  245 us
    reduce_scatter x1, waiting for transfers between devices, on_device(): lax.psum_scatter(input_grad, 'shard', scatter_dimension=0, tiled=True)  78.2 us
    psum x1, waiting for transfers between devices, on_device(): early = lax.psum((expert_gain_grad, router_grad), ('shard', 'rep'))  59.5 us
    all_gather x1, waiting for transfers between devices, on_device(): packed_full = lax.all_gather(packed, 'shard', axis=0, tiled=True)  58.4 us
    convert_element_type x2, other arithmetic, on_device(): score_slope = (weights_soft * (probs_slope - centre)).astype(bf16)  55.1 us
    ppermute x2, waiting for transfers between devices, rep_sum(): other = [lax.ppermute(array, 'rep', [(0, 1), (1, 0)]) for array in low]  50 us
    convert_element_type x14, other arithmetic, ring_sum(): total = ring.hop(chip_part(step, total).astype(bf16))  46.6 us
  transfers between devices with their start and end apart: 69, of which 19 were waited for; matrix products, arithmetic and copies ran while one was open for 18% of the time, Pallas kernels for 21%

profile of v1, /device:TPU:0, one launch (start us, length us, event | category | flops | bytes accessed | tf_op | source)
XLA Modules:
  0.0 1499.6 jit_solution(16450114294229701023)
XLA Ops:
  17.0 58.4 %all-gather.4.cloned.1.call-done = bf16[1024,3072]{1,0:T(8,128)(2,1)} async-done(((bf16[64,3072]{1,0:T(8,128)(2,1)}), bf16[1024,3072]{1,0:T(8,128)(2,1)}) %all-gather.4.cloned.1.call-update) | async-done | bytes 6291472 | tf_op jit(solution)/shard_map/all_gather | solution.py:301
  86.8 31.4 %all-gather.6.cloned.1.call-done = s32[512,1024]{1,0:T(8,128)} async-done(((s32[32,1024]{1,0:T(8,128)}), s32[512,1024]{1,0:T(8,128)}) %all-gather.6.cloned.1.call-update) | async-done | bytes 2097168 | tf_op jit(solution)/shard_map/all_gather | solution.py:311
  287.0 19.6 %shard_map.247 = (bf16[1024,1024]{1,0:T(8,128)(2,1)}, bf16[1024,1024]{1,0:T(8,128)(2,1)}, bf16[2,4608,1024]{2,1,0:T(8,128)(2,1)}, bf16[2,4608,1024]{2,1,0:T(8,12...) custom-call(s32[2]{0:T(128)S(1)} %get-tuple-element.334.where_ref, ...), custom_call_target="tpu_custom_call" | custom-call | flops 8455716864 | bytes 20971520 | tf_op jit(solution)/shard_map/pallas_call | solution.py:252
  327.4 19.7 %shard_map.249 = (bf16[1024,1024]{1,0:T(8,128)(2,1)}, bf16[1024,1024]{1,0:T(8,128)(2,1)}, bf16[2,4608,1024]{2,1,0:T(8,128)(2,1)}, bf16[2,4608,1024]{2,1,0:T(8,12...) custom-call(s32[2]{0:T(128)S(1)} %get-tuple-element.336.where_ref, ...), custom_call_target="tpu_custom_call", output_to_operand_aliasing={{2}: (11, {}), {3}: (12, {}), {4}: (13, {}), {5}: (14, {}),... | custom-call | flops 8455716864 | bytes 20971520 | tf_op jit(solution)/shard_map/pallas_call | solution.py:252
  350.6 19.9 %shard_map.250 = (bf16[1024,1024]{1,0:T(8,128)(2,1)}, bf16[1024,1024]{1,0:T(8,128)(2,1)}, bf16[2,4608,1024]{2,1,0:T(8,128)(2,1)}, bf16[2,4608,1024]{2,1,0:T(8,12...) custom-call(s32[2]{0:T(128)S(1)} %get-tuple-element.335.where_ref, ...), custom_call_target="tpu_custom_call", output_to_operand_aliasing={{2}: (11, {}), {3}: (12, {}), {4}: (13, {}), {5}: (14, {}),... | custom-call | flops 8455716864 | bytes 20971520 | tf_op jit(solution)/shard_map/pallas_call | solution.py:252
  377.9 19.7 %shard_map.251 = (bf16[1024,1024]{1,0:T(8,128)(2,1)}, bf16[1024,1024]{1,0:T(8,128)(2,1)}, bf16[2,4608,1024]{2,1,0:T(8,128)(2,1)}, bf16[2,4608,1024]{2,1,0:T(8,12...) custom-call(s32[2]{0:T(128)S(1)} %get-tuple-element.338.where_ref, ...), custom_call_target="tpu_custom_call", output_to_operand_aliasing={{2}: (11, {}), {3}: (12, {}), {4}: (13, {}), {5}: (14, {}),... | custom-call | flops 8455716864 | bytes 20971520 | tf_op jit(solution)/shard_map/pallas_call | solution.py:252
  400.1 20.1 %collective-permute-done.38 = bf16[1024,1024]{1,0:T(8,128)(2,1)} collective-permute-done((bf16[1024,1024]{1,0:T(8,128)(2,1)}, bf16[1024,1024]{1,0:T(8,128)(2,1)}, u32[]{:S(2)}, u32[]{:S(2)}) %collective-permute-start.38) | collective-permute-done | bytes 2097184 | tf_op jit(solution)/shard_map/ppermute | solution.py:63
  420.4 19.7 %shard_map.252 = (bf16[1024,1024]{1,0:T(8,128)(2,1)}, bf16[1024,1024]{1,0:T(8,128)(2,1)}, bf16[2,4608,1024]{2,1,0:T(8,128)(2,1)}, bf16[2,4608,1024]{2,1,0:T(8,12...) custom-call(s32[2]{0:T(128)S(1)} %get-tuple-element.337.where_ref, ...), custom_call_target="tpu_custom_call", output_to_operand_aliasing={{2}: (11, {}), {3}: (12, {}), {4}: (13, {}), {5}: (14, {}),... | custom-call | flops 8455716864 | bytes 20971520 | tf_op jit(solution)/shard_map/pallas_call | solution.py:252
  487.8 19.6 %shard_map.254 = (bf16[1024,1024]{1,0:T(8,128)(2,1)}, bf16[1024,1024]{1,0:T(8,128)(2,1)}, bf16[2,4608,1024]{2,1,0:T(8,128)(2,1)}, bf16[2,4608,1024]{2,1,0:T(8,12...) custom-call(s32[2]{0:T(128)S(1)} %pad_add_fusion.6.where_ref, ...), custom_call_target="tpu_custom_call", output_to_operand_aliasing={{2}: (11, {}), {3}: (12, {}), {4}: (13, {}), {5}: (14, {}),... | custom-call | flops 8455716864 | bytes 20971520 | tf_op jit(solution)/shard_map/pallas_call | solution.py:252
  515.9 20.0 %shard_map.255 = (bf16[1024,1024]{1,0:T(8,128)(2,1)}, bf16[1024,1024]{1,0:T(8,128)(2,1)}, bf16[2,4608,1024]{2,1,0:T(8,128)(2,1)}, bf16[2,4608,1024]{2,1,0:T(8,12...) custom-call(s32[2]{0:T(128)S(1)} %pad_add_fusion.9.where_ref, ...), custom_call_target="tpu_custom_call", output_to_operand_aliasing={{2}: (11, {}), {3}: (12, {}), {4}: (13, {}), {5}: (14, {}),... | custom-call | flops 8455716864 | bytes 20971520 | tf_op jit(solution)/shard_map/pallas_call | solution.py:252
  583.2 19.7 %shard_map.257 = (bf16[1024,1024]{1,0:T(8,128)(2,1)}, bf16[1024,1024]{1,0:T(8,128)(2,1)}, bf16[2,4608,1024]{2,1,0:T(8,128)(2,1)}, bf16[2,4608,1024]{2,1,0:T(8,12...) custom-call(s32[2]{0:T(128)S(1)} %pad_add_fusion.11.where_ref, ...), custom_call_target="tpu_custom_call", output_to_operand_aliasing={{2}: (11, {}), {3}: (12, {}), {4}: (13, {}), {5}: (14, {}),... | custom-call | flops 8455716864 | bytes 20971520 | tf_op jit(solution)/shard_map/pallas_call | solution.py:252
  622.6 19.8 %shard_map.258 = (bf16[1024,1024]{1,0:T(8,128)(2,1)}, bf16[1024,1024]{1,0:T(8,128)(2,1)}, bf16[2,4608,1024]{2,1,0:T(8,128)(2,1)}, bf16[2,4608,1024]{2,1,0:T(8,12...) custom-call(s32[2]{0:T(128)S(1)} %pad_add_fusion.10.where_ref, ...), custom_call_target="tpu_custom_call", output_to_operand_aliasing={{2}: (11, {}), {3}: (12, {}), {4}: (13, {}), {5}: (14, {}),... | custom-call | flops 8455716864 | bytes 20971520 | tf_op jit(solution)/shard_map/pallas_call | solution.py:252
  650.7 19.9 %shard_map.259 = (bf16[1024,1024]{1,0:T(8,128)(2,1)}, bf16[1024,1024]{1,0:T(8,128)(2,1)}, bf16[2,4608,1024]{2,1,0:T(8,128)(2,1)}, bf16[2,4608,1024]{2,1,0:T(8,12...) custom-call(s32[2]{0:T(128)S(1)} %pad_add_fusion.13.where_ref, ...), custom_call_target="tpu_custom_call", output_to_operand_aliasing={{2}: (11, {}), {3}: (12, {}), {4}: (13, {}), {5}: (14, {}),... | custom-call | flops 8455716864 | bytes 20971520 | tf_op jit(solution)/shard_map/pallas_call | solution.py:252
  672.8 19.6 %shard_map.260 = (bf16[1024,1024]{1,0:T(8,128)(2,1)}, bf16[1024,1024]{1,0:T(8,128)(2,1)}, bf16[2,4608,1024]{2,1,0:T(8,128)(2,1)}, bf16[2,4608,1024]{2,1,0:T(8,12...) custom-call(s32[2]{0:T(128)S(1)} %pad_add_fusion.12.where_ref, ...), custom_call_target="tpu_custom_call", output_to_operand_aliasing={{2}: (11, {}), {3}: (12, {}), {4}: (13, {}), {5}: (14, {}),... | custom-call | flops 8455716864 | bytes 20971520 | tf_op jit(solution)/shard_map/pallas_call | solution.py:252
  721.6 19.9 %shard_map.262 = (bf16[1024,1024]{1,0:T(8,128)(2,1)}, bf16[1024,1024]{1,0:T(8,128)(2,1)}, bf16[2,4608,1024]{2,1,0:T(8,128)(2,1)}, bf16[2,4608,1024]{2,1,0:T(8,12...) custom-call(s32[2]{0:T(128)S(1)} %pad_add_fusion.14.where_ref, ...), custom_call_target="tpu_custom_call", output_to_operand_aliasing={{2}: (11, {}), {3}: (12, {}), {4}: (13, {}), {5}: (14, {}),... | custom-call | flops 8455716864 | bytes 20971520 | tf_op jit(solution)/shard_map/pallas_call | solution.py:252
  754.1 21.7 %all-to-all-done = f32[16,2,1024]{2,1,0:T(2,128)S(1)} async-done(((f32[16,2,1024]{2,1,0:T(2,128)}), f32[16,2,1024]{2,1,0:T(2,128)S(1)}, u32[]{:S(2)}, u32[]{:S(2)}) %all-to-all-start) | async-done | bytes 131104 | tf_op jit(solution)/shard_map/all_to_all | solution.py:412
  788.1 24.1 %collective-permute-done.53 = bf16[1024,1024]{1,0:T(8,128)(2,1)S(1)} collective-permute-done((bf16[1024,1024]{1,0:T(8,128)(2,1)S(1)}, bf16[1024,1024]{1,0:T(8,128)(2,1)S(1)}, u32[]{:S(2)}, u32[]{:S(2)}) %collective-permute-start.53) | collective-permute-done | bytes 2097184 | tf_op jit(solution)/shard_map/ppermute | solution.py:63
  814.1 25.7 %collective-permute-done.54 = bf16[1024,1024]{1,0:T(8,128)(2,1)S(1)} collective-permute-done((bf16[1024,1024]{1,0:T(8,128)(2,1)S(1)}, bf16[1024,1024]{1,0:T(8,128)(2,1)S(1)}, u32[]{:S(2)}, u32[]{:S(2)}) %collective-permute-start.54) | collective-permute-done | bytes 2097184 | tf_op jit(solution)/shard_map/ppermute | solution.py:63
  841.7 25.7 %collective-permute-done.55 = bf16[1024,1024]{1,0:T(8,128)(2,1)S(1)} collective-permute-done((bf16[1024,1024]{1,0:T(8,128)(2,1)S(1)}, bf16[1024,1024]{1,0:T(8,128)(2,1)S(1)}, u32[]{:S(2)}, u32[]{:S(2)}) %collective-permute-start.55) | collective-permute-done | bytes 2097184 | tf_op jit(solution)/shard_map/ppermute | solution.py:63
  869.3 25.7 %collective-permute-done.56 = bf16[1024,1024]{1,0:T(8,128)(2,1)S(1)} collective-permute-done((bf16[1024,1024]{1,0:T(8,128)(2,1)S(1)}, bf16[1024,1024]{1,0:T(8,128)(2,1)S(1)}, u32[]{:S(2)}, u32[]{:S(2)}) %collective-permute-start.56) | collective-permute-done | bytes 2097184 | tf_op jit(solution)/shard_map/ppermute | solution.py:63
  896.9 25.7 %collective-permute-done.57 = bf16[1024,1024]{1,0:T(8,128)(2,1)S(1)} collective-permute-done((bf16[1024,1024]{1,0:T(8,128)(2,1)S(1)}, bf16[1024,1024]{1,0:T(8,128)(2,1)S(1)}, u32[]{:S(2)}, u32[]{:S(2)}) %collective-permute-start.57) | collective-permute-done | bytes 2097184 | tf_op jit(solution)/shard_map/ppermute | solution.py:63
  924.6 25.7 %collective-permute-done.58 = bf16[1024,1024]{1,0:T(8,128)(2,1)S(1)} collective-permute-done((bf16[1024,1024]{1,0:T(8,128)(2,1)S(1)}, bf16[1024,1024]{1,0:T(8,128)(2,1)S(1)}, u32[]{:S(2)}, u32[]{:S(2)}) %collective-permute-start.58) | collective-permute-done | bytes 2097184 | tf_op jit(solution)/shard_map/ppermute | solution.py:63
  954.0 23.9 %collective-permute-done.59 = bf16[1024,1024]{1,0:T(8,128)(2,1)S(1)} collective-permute-done((bf16[1024,1024]{1,0:T(8,128)(2,1)S(1)}, bf16[1024,1024]{1,0:T(8,128)(2,1)S(1)}, u32[]{:S(2)}, u32[]{:S(2)}) %collective-permute-start.59) | collective-permute-done | bytes 2097184 | tf_op jit(solution)/shard_map/ppermute | solution.py:63
  995.8 21.8 %fusion.3 = (f32[8,2,512]{2,1,0:T(2,128)S(1)}, f32[8,1024,512,2]{2,1,3,0:T(8,128)}) fusion(f32[8,2,512,1024]{2,3,1,0:T(8,128)} %get-tuple-element.323, f32[8,2,512]{2,1,0:T(2,128)S(1)} %bitcast.206, bf16[1024,8,64,1]{0,2,3,1:T(8,128)(2,1)S(1)} %bitcast.195, bf16[512,8,2,64]{0,3,2,1:T(8,128)(2,1)S(1)} %bitcast.184), kind=kOutput, calls=%fused_computation.7 | convolution fusion | flops 1098899456 | bytes 69271552 | tf_op jit(solution)/shard_map/qhgd,khd->hgqk/dot_general | solution.py:468
  1017.7 27.4 %fusion.5 = bf16[8,2,512,1024]{2,3,1,0:T(8,128)(2,1)} fusion(f32[8,1024,512,2]{2,1,3,0:T(8,128)} %get-tuple-element.329, f32[8,2,512,1024]{2,3,1,0:T(8,128)} %get-tuple-element.323, f32[8,2,512]{2,1,0:T(2,128)S(1)} %get-tuple-element.328, f32[8,2,512]{2,1,0:T(2,128)S(1)} %bitcast.207), kind=kLoop, calls=%fused_computation.9 | loop fusion | flops 33554432 | bytes 83951616 | tf_op jit(solution)/shard_map/convert_element_type | solution.py:472
  1056.3 22.6 %fusion = (f32[8,2,512]{2,1,0:T(2,128)S(1)}, f32[8,1024,512,2]{2,1,3,0:T(8,128)}) fusion(f32[8,2,512,1024]{2,3,1,0:T(8,128)} %get-tuple-element.321, f32[8,2,512]{2,1,0:T(2,128)S(1)} %bitcast.209, bf16[1024,8,64,1]{0,2,3,1:T(8,128)(2,1)} %bitcast.194, bf16[512,8,2,64]{0,3,2,1:T(8,128)(2,1)S(1)} %bitcast.186), kind=kOutput, calls=%fused_computation.2 | convolution fusion | flops 1098899456 | bytes 69271552 | tf_op jit(solution)/shard_map/qhgd,khd->hgqk/dot_general | solution.py:468
  1079.0 27.7 %fusion.2 = bf16[8,2,512,1024]{2,3,1,0:T(8,128)(2,1)} fusion(f32[8,1024,512,2]{2,1,3,0:T(8,128)} %get-tuple-element.331, f32[8,2,512,1024]{2,3,1,0:T(8,128)} %get-tuple-element.321, f32[8,2,512]{2,1,0:T(2,128)S(1)} %get-tuple-element.330, f32[8,2,512]{2,1,0:T(2,128)S(1)} %bitcast.210), kind=kLoop, calls=%fused_computation.4 | loop fusion | flops 33554432 | bytes 83951616 | tf_op jit(solution)/shard_map/convert_element_type | solution.py:472
  1185.3 29.6 %convolution_convert_fusion = bf16[2,1024,1024]{2,1,0:T(8,128)(2,1)} fusion(bf16[2,4608,1024]{2,1,0:T(8,128)(2,1)} %get-tuple-element.268, bf16[2,4608,1024]{2,1,0:T(8,128)(2,1)} %get-tuple-element.269), kind=kOutput, calls=%fused_computation.77 | convolution fusion | flops 19329449984 | bytes 41943040 | tf_op jit(solution)/shard_map/erd,erf->edf/dot_general | solution.py:407
  1232.9 78.2 %reduce-scatter.3.cloned.1.call-done = f32[64,2048]{1,0:T(8,128)} async-done(((f32[1024,2048]{1,0:T(8,128)}), f32[64,2048]{1,0:T(8,128)}) %reduce-scatter.3.cloned.1.call-update) | async-done | bytes 524304 | tf_op jit(solution)/shard_map/reduce_scatter | solution.py:527
  1314.1 50.0 %collective-permute-done.61 = bf16[2,512,1024]{2,1,0:T(8,128)(2,1)} collective-permute-done((bf16[2,512,1024]{2,1,0:T(8,128)(2,1)}, bf16[2,512,1024]{2,1,0:T(8,128)(2,1)}, u32[]{:S(2)}, u32[]{:S(2)}) %collective-permute-start.61) | collective-permute-done | bytes 2097184 | tf_op jit(solution)/shard_map/ppermute | solution.py:512
  1387.9 38.5 %all-reduce = (f32[1024]{0:T(1024)}, f32[1024]{0:T(1024)}) all-reduce(f32[1024]{0:T(1024)S(1)} %get-tuple-element.274, f32[1024]{0:T(1024)S(1)} %copy-done.85), channel_id=1, replica_groups=mesh['shard'=16,'rep'=2] {'shard','rep'}, use_global_device_ids=true, to_apply=%region_15.16 | all-reduce | flops 2048 | bytes 16384 | tf_op jit(solution)/shard_map/psum | solution.py:522
  1429.7 59.5 %all-reduce.5.cloned.1.call-done = f32[1024,32]{0,1:T(8,128)} async-done(((f32[1024,32]{0,1:T(8,128)}), f32[1024,32]{0,1:T(8,128)}) %all-reduce.5.cloned.1.call-update) | async-done | bytes 131088 | tf_op jit(solution)/shard_map/psum | solution.py:519
  (453 shorter events, 582.1 us)
Async XLA Ops:
  7.2 68.3 %all-gather.4.cloned.1.call-start = ((), (), s32[]{:S(2)}) async-start(), calls=%async_computation.3 | async-start | bytes 6684672 | tf_op jit(solution)/shard_map/all_gather | solution.py:301
  9.2 109.0 %all-gather.6.cloned.1.call-start = ((), (), s32[]{:S(2)}) async-start(), calls=%async_computation.7 | async-start | bytes 2228224 | tf_op jit(solution)/shard_map/all_gather | solution.py:311
  222.4 58.4 %collective-permute-start.2 = (bf16[1024,1024]{1,0:T(8,128)(2,1)}, bf16[1024,1024]{1,0:T(8,128)(2,1)}, u32[]{:S(2)}, u32[]{:S(2)}) collective-permute-start(bf16[1024,1024]{1,0:T(8,128)(2,1)} %multiply_convert_fusion.tokens_ref), channel_id=1, source_target_pairs={{0,8},{10,2},{8,16},{18,10},{16,24},{26,18},{24,28},{30,26},{28,20... | collective-permute-start | bytes 6291464 | tf_op jit(solution)/shard_map/ppermute | solution.py:63
  222.9 57.8 %collective-permute-start.3 = (bf16[1024,1024]{1,0:T(8,128)(2,1)}, bf16[1024,1024]{1,0:T(8,128)(2,1)}, u32[]{:S(2)}, u32[]{:S(2)}) collective-permute-start(bf16[1024,1024]{1,0:T(8,128)(2,1)} %broadcast_select_fusion.slope_ref), channel_id=1, source_target_pairs={{0,8},{10,2},{8,16},{18,10},{16,24},{26,18},{24,28},{30,26},{28,20... | collective-permute-start | bytes 6291464 | tf_op jit(solution)/shard_map/ppermute | solution.py:63
  230.9 55.5 %collective-permute-start = (bf16[1024,1024]{1,0:T(8,128)(2,1)}, bf16[1024,1024]{1,0:T(8,128)(2,1)}, u32[]{:S(2)}, u32[]{:S(2)}) collective-permute-start(bf16[1024,1024]{1,0:T(8,128)(2,1)} %multiply_convert_fusion.tokens_ref), channel_id=1, source_target_pairs={{0,2},{2,0},{4,6},{6,4},{8,10},{10,8},{12,14},{14,12},{16,18},{18,... | collective-permute-start | bytes 6291464 | tf_op jit(solution)/shard_map/ppermute | solution.py:66
  230.9 56.1 %collective-permute-start.1 = (bf16[1024,1024]{1,0:T(8,128)(2,1)}, bf16[1024,1024]{1,0:T(8,128)(2,1)}, u32[]{:S(2)}, u32[]{:S(2)}) collective-permute-start(bf16[1024,1024]{1,0:T(8,128)(2,1)} %broadcast_select_fusion.slope_ref), channel_id=1, source_target_pairs={{0,2},{2,0},{4,6},{6,4},{8,10},{10,8},{12,14},{14,12},{16,18},{18,... | collective-permute-start | bytes 6291464 | tf_op jit(solution)/shard_map/ppermute | solution.py:66
  284.5 62.8 %collective-permute-start.6 = (bf16[1024,1024]{1,0:T(8,128)(2,1)}, bf16[1024,1024]{1,0:T(8,128)(2,1)S(1)}, u32[]{:S(2)}, u32[]{:S(2)}) collective-permute-start(bf16[1024,1024]{1,0:T(8,128)(2,1)} %collective-permute-done.2.tokens_ref), channel_id=1, source_target_pairs={{0,8},{10,2},{8,16},{18,10},{16,24},{26,18},{24,28},{30,26},{28,20... | collective-permute-start | bytes 6291464 | tf_op jit(solution)/shard_map/ppermute | solution.py:63
  286.5 61.3 %collective-permute-start.7 = (bf16[1024,1024]{1,0:T(8,128)(2,1)}, bf16[1024,1024]{1,0:T(8,128)(2,1)S(1)}, u32[]{:S(2)}, u32[]{:S(2)}) collective-permute-start(bf16[1024,1024]{1,0:T(8,128)(2,1)} %collective-permute-done.3.slope_ref), channel_id=1, source_target_pairs={{0,8},{10,2},{8,16},{18,10},{16,24},{26,18},{24,28},{30,26},{28,20... | collective-permute-start | bytes 6291464 | tf_op jit(solution)/shard_map/ppermute | solution.py:63
  349.1 48.5 %collective-permute-start.10 = (bf16[1024,1024]{1,0:T(8,128)(2,1)S(1)}, bf16[1024,1024]{1,0:T(8,128)(2,1)S(1)}, u32[]{:S(2)}, u32[]{:S(2)}) collective-permute-start(bf16[1024,1024]{1,0:T(8,128)(2,1)S(1)} %collective-permute-done.6.tokens_ref), channel_id=1, source_target_pairs={{0,8},{10,2},{8,16},{18,10},{16,24},{26,18},{24,28},{30,26},{28,20... | collective-permute-start | bytes 6291464 | tf_op jit(solution)/shard_map/ppermute | solution.py:63
  349.3 48.9 %collective-permute-start.11 = (bf16[1024,1024]{1,0:T(8,128)(2,1)S(1)}, bf16[1024,1024]{1,0:T(8,128)(2,1)S(1)}, u32[]{:S(2)}, u32[]{:S(2)}) collective-permute-start(bf16[1024,1024]{1,0:T(8,128)(2,1)S(1)} %collective-permute-done.7.slope_ref), channel_id=1, source_target_pairs={{0,8},{10,2},{8,16},{18,10},{16,24},{26,18},{24,28},{30,26},{28,20... | collective-permute-start | bytes 6291464 | tf_op jit(solution)/shard_map/ppermute | solution.py:63
  397.7 49.4 %collective-permute-start.12 = (bf16[1024,1024]{1,0:T(8,128)(2,1)S(1)}, bf16[1024,1024]{1,0:T(8,128)(2,1)S(1)}, u32[]{:S(2)}, u32[]{:S(2)}) collective-permute-start(bf16[1024,1024]{1,0:T(8,128)(2,1)S(1)} %collective-permute-done.10.tokens_ref), channel_id=1, source_target_pairs={{0,2},{2,0},{4,6},{6,4},{8,10},{10,8},{12,14},{14,12},{16,18},{18,... | collective-permute-start | bytes 6291464 | tf_op jit(solution)/shard_map/ppermute | solution.py:66
  398.2 48.9 %collective-permute-start.13 = (bf16[1024,1024]{1,0:T(8,128)(2,1)S(1)}, bf16[1024,1024]{1,0:T(8,128)(2,1)}, u32[]{:S(2)}, u32[]{:S(2)}) collective-permute-start(bf16[1024,1024]{1,0:T(8,128)(2,1)S(1)} %collective-permute-done.11.slope_ref), channel_id=1, source_target_pairs={{0,2},{2,0},{4,6},{6,4},{8,10},{10,8},{12,14},{14,12},{16,18},{18,... | collective-permute-start | bytes 6291464 | tf_op jit(solution)/shard_map/ppermute | solution.py:66
  399.0 69.1 %collective-permute-start.14 = (bf16[1024,1024]{1,0:T(8,128)(2,1)S(1)}, bf16[1024,1024]{1,0:T(8,128)(2,1)S(1)}, u32[]{:S(2)}, u32[]{:S(2)}) collective-permute-start(bf16[1024,1024]{1,0:T(8,128)(2,1)S(1)} %collective-permute-done.10.tokens_ref), channel_id=1, source_target_pairs={{0,8},{10,2},{8,16},{18,10},{16,24},{26,18},{24,28},{30,26},{28,20... | collective-permute-start | bytes 6291464 | tf_op jit(solution)/shard_map/ppermute | solution.py:63
  420.2 48.4 %collective-permute-start.15 = (bf16[1024,1024]{1,0:T(8,128)(2,1)S(1)}, bf16[1024,1024]{1,0:T(8,128)(2,1)S(1)}, u32[]{:S(2)}, u32[]{:S(2)}) collective-permute-start(bf16[1024,1024]{1,0:T(8,128)(2,1)S(1)} %collective-permute-done.11.slope_ref), channel_id=1, source_target_pairs={{0,8},{10,2},{8,16},{18,10},{16,24},{26,18},{24,28},{30,26},{28,20... | collective-permute-start | bytes 6291464 | tf_op jit(solution)/shard_map/ppermute | solution.py:63
  468.1 46.5 %collective-permute-start.16 = (bf16[1024,1024]{1,0:T(8,128)(2,1)S(1)}, bf16[1024,1024]{1,0:T(8,128)(2,1)}, u32[]{:S(2)}, u32[]{:S(2)}) collective-permute-start(bf16[1024,1024]{1,0:T(8,128)(2,1)S(1)} %collective-permute-done.14.tokens_ref), channel_id=1, source_target_pairs={{0,2},{2,0},{4,6},{6,4},{8,10},{10,8},{12,14},{14,12},{16,18},{18,... | collective-permute-start | bytes 6291464 | tf_op jit(solution)/shard_map/ppermute | solution.py:66
  468.6 46.0 %collective-permute-start.17 = (bf16[1024,1024]{1,0:T(8,128)(2,1)S(1)}, bf16[1024,1024]{1,0:T(8,128)(2,1)S(1)}, u32[]{:S(2)}, u32[]{:S(2)}) collective-permute-start(bf16[1024,1024]{1,0:T(8,128)(2,1)S(1)} %collective-permute-done.15.slope_ref), channel_id=1, source_target_pairs={{0,2},{2,0},{4,6},{6,4},{8,10},{10,8},{12,14},{14,12},{16,18},{18,... | collective-permute-start | bytes 6291464 | tf_op jit(solution)/shard_map/ppermute | solution.py:66
  470.0 65.9 %collective-permute-start.18 = (bf16[1024,1024]{1,0:T(8,128)(2,1)S(1)}, bf16[1024,1024]{1,0:T(8,128)(2,1)S(1)}, u32[]{:S(2)}, u32[]{:S(2)}) collective-permute-start(bf16[1024,1024]{1,0:T(8,128)(2,1)S(1)} %collective-permute-done.14.tokens_ref), channel_id=1, source_target_pairs={{0,8},{10,2},{8,16},{18,10},{16,24},{26,18},{24,28},{30,26},{28,20... | collective-permute-start | bytes 6291464 | tf_op jit(solution)/shard_map/ppermute | solution.py:63
  487.6 48.8 %collective-permute-start.19 = (bf16[1024,1024]{1,0:T(8,128)(2,1)S(1)}, bf16[1024,1024]{1,0:T(8,128)(2,1)S(1)}, u32[]{:S(2)}, u32[]{:S(2)}) collective-permute-start(bf16[1024,1024]{1,0:T(8,128)(2,1)S(1)} %collective-permute-done.15.slope_ref), channel_id=1, source_target_pairs={{0,8},{10,2},{8,16},{18,10},{16,24},{26,18},{24,28},{30,26},{28,20... | collective-permute-start | bytes 6291464 | tf_op jit(solution)/shard_map/ppermute | solution.py:63
  535.9 45.9 %collective-permute-start.20 = (bf16[1024,1024]{1,0:T(8,128)(2,1)S(1)}, bf16[1024,1024]{1,0:T(8,128)(2,1)S(1)}, u32[]{:S(2)}, u32[]{:S(2)}) collective-permute-start(bf16[1024,1024]{1,0:T(8,128)(2,1)S(1)} %collective-permute-done.18.tokens_ref), channel_id=1, source_target_pairs={{0,2},{2,0},{4,6},{6,4},{8,10},{10,8},{12,14},{14,12},{16,18},{18,... | collective-permute-start | bytes 6291464 | tf_op jit(solution)/shard_map/ppermute | solution.py:66
  538.0 65.0 %collective-permute-start.22 = (bf16[1024,1024]{1,0:T(8,128)(2,1)S(1)}, bf16[1024,1024]{1,0:T(8,128)(2,1)S(1)}, u32[]{:S(2)}, u32[]{:S(2)}) collective-permute-start(bf16[1024,1024]{1,0:T(8,128)(2,1)S(1)} %collective-permute-done.18.tokens_ref), channel_id=1, source_target_pairs={{0,8},{10,2},{8,16},{18,10},{16,24},{26,18},{24,28},{30,26},{28,20... | collective-permute-start | bytes 6291464 | tf_op jit(solution)/shard_map/ppermute | solution.py:63
  555.0 48.4 %collective-permute-start.23 = (bf16[1024,1024]{1,0:T(8,128)(2,1)S(1)}, bf16[1024,1024]{1,0:T(8,128)(2,1)S(1)}, u32[]{:S(2)}, u32[]{:S(2)}) collective-permute-start(bf16[1024,1024]{1,0:T(8,128)(2,1)S(1)} %collective-permute-done.19.slope_ref), channel_id=1, source_target_pairs={{0,8},{10,2},{8,16},{18,10},{16,24},{26,18},{24,28},{30,26},{28,20... | collective-permute-start | bytes 6291464 | tf_op jit(solution)/shard_map/ppermute | solution.py:63
  603.0 46.4 %collective-permute-start.24 = (bf16[1024,1024]{1,0:T(8,128)(2,1)S(1)}, bf16[1024,1024]{1,0:T(8,128)(2,1)S(1)}, u32[]{:S(2)}, u32[]{:S(2)}) collective-permute-start(bf16[1024,1024]{1,0:T(8,128)(2,1)S(1)} %collective-permute-done.22.tokens_ref), channel_id=1, source_target_pairs={{0,2},{2,0},{4,6},{6,4},{8,10},{10,8},{12,14},{14,12},{16,18},{18,... | collective-permute-start | bytes 6291464 | tf_op jit(solution)/shard_map/ppermute | solution.py:66
  603.5 45.9 %collective-permute-start.25 = (bf16[1024,1024]{1,0:T(8,128)(2,1)S(1)}, bf16[1024,1024]{1,0:T(8,128)(2,1)}, u32[]{:S(2)}, u32[]{:S(2)}) collective-permute-start(bf16[1024,1024]{1,0:T(8,128)(2,1)S(1)} %collective-permute-done.23.slope_ref), channel_id=1, source_target_pairs={{0,2},{2,0},{4,6},{6,4},{8,10},{10,8},{12,14},{14,12},{16,18},{18,... | collective-permute-start | bytes 6291464 | tf_op jit(solution)/shard_map/ppermute | solution.py:66
  604.9 65.7 %collective-permute-start.26 = (bf16[1024,1024]{1,0:T(8,128)(2,1)S(1)}, bf16[1024,1024]{1,0:T(8,128)(2,1)S(1)}, u32[]{:S(2)}, u32[]{:S(2)}) collective-permute-start(bf16[1024,1024]{1,0:T(8,128)(2,1)S(1)} %collective-permute-done.22.tokens_ref), channel_id=1, source_target_pairs={{0,8},{10,2},{8,16},{18,10},{16,24},{26,18},{24,28},{30,26},{28,20... | collective-permute-start | bytes 6291464 | tf_op jit(solution)/shard_map/ppermute | solution.py:63
  622.5 48.7 %collective-permute-start.27 = (bf16[1024,1024]{1,0:T(8,128)(2,1)S(1)}, bf16[1024,1024]{1,0:T(8,128)(2,1)S(1)}, u32[]{:S(2)}, u32[]{:S(2)}) collective-permute-start(bf16[1024,1024]{1,0:T(8,128)(2,1)S(1)} %collective-permute-done.23.slope_ref), channel_id=1, source_target_pairs={{0,8},{10,2},{8,16},{18,10},{16,24},{26,18},{24,28},{30,26},{28,20... | collective-permute-start | bytes 6291464 | tf_op jit(solution)/shard_map/ppermute | solution.py:63
  721.1 55.7 %collective-permute-start.30 = (bf16[1024,1024]{1,0:T(8,128)(2,1)}, bf16[1024,1024]{1,0:T(8,128)(2,1)}, u32[]{:S(2)}, u32[]{:S(2)}) collective-permute-start(bf16[1024,1024]{1,0:T(8,128)(2,1)} %get-tuple-element.235), channel_id=1, source_target_pairs={{0,2},{2,0},{4,6},{6,4},{8,10},{10,8},{12,14},{14,12},{16,18},{18,... | collective-permute-start | bytes 6291464 | tf_op jit(solution)/shard_map/ppermute | solution.py:66
  751.7 481.2 %reduce-scatter.5.cloned.1.call-start = ((), (), s32[]{:S(2)}) async-start(), calls=%async_computation.5 | async-start | bytes 4456448 | tf_op jit(solution)/shard_map/reduce_scatter | solution.py:524
  1131.2 179.8 %reduce-scatter.3.cloned.1.call-start = ((), (), s32[]{:S(2)}) async-start(), calls=%async_computation.4 | async-start | bytes 8912896 | tf_op jit(solution)/shard_map/reduce_scatter | solution.py:527
  1185.2 241.2 %all-reduce.7.cloned.1.call-start = ((), (), s32[]{:S(2)}) async-start(), calls=%async_computation.8 | async-start | bytes 1572864 | tf_op jit(solution)/shard_map/psum | solution.py:526
  1214.9 153.7 %collective-permute-start.60 = (bf16[2,1024,1024]{2,1,0:T(8,128)(2,1)}, bf16[2,1024,1024]{2,1,0:T(8,128)(2,1)}, u32[]{:S(2)}, u32[]{:S(2)}) collective-permute-start(bf16[2,1024,1024]{2,1,0:T(8,128)(2,1)} %convolution_convert_fusion), channel_id=1, source_target_pairs={{0,1},{1,0},{2,3},{3,2},{4,5},{5,4},{6,7},{7,6},{8,9},{9,8},{10,11... | collective-permute-start | bytes 12582920 | tf_op jit(solution)/shard_map/ppermute | solution.py:512
  1232.5 131.5 %collective-permute-start.61 = (bf16[2,512,1024]{2,1,0:T(8,128)(2,1)}, bf16[2,512,1024]{2,1,0:T(8,128)(2,1)}, u32[]{:S(2)}, u32[]{:S(2)}) collective-permute-start(bf16[2,512,1024]{2,1,0:T(8,128)(2,1)} %convolution_convert_fusion.1), channel_id=1, source_target_pairs={{0,1},{1,0},{2,3},{3,2},{4,5},{5,4},{6,7},{7,6},{8,9},{9,8},{10,11... | collective-permute-start | bytes 6291464 | tf_op jit(solution)/shard_map/ppermute | solution.py:512
  1311.0 178.2 %all-reduce.5.cloned.1.call-start = ((), (), s32[]{:S(2)}) async-start(), calls=%async_computation.6 | async-start | bytes 262144 | tf_op jit(solution)/shard_map/psum | solution.py:519
  (139 other events, 3692.0 us)
Sparse Core Ops, SparseCore 0:
  10.9 64.5 all-gather.3
  78.2 39.9 all-gather.5
  1131.3 71.5 reduce-scatter.4
  1207.4 103.5 reduce-scatter.2
  1313.4 47.8 all-reduce.6
  1367.2 121.9 all-reduce.4

commit v2 on v1

v2 whole, which is shorter than its diff:
```python
import functools

import jax
import jax.numpy as jnp
import numpy as np
from jax import lax
from jax.experimental import pallas as pl
from jax.experimental.pallas import tpu as pltpu
from jax.sharding import PartitionSpec as P

D = 1024
HEADS = 16
KV = 8
HD = 64
EXPERTS = 32
TOP = 8
CAP = 288
ABSENT = -100000


epsilon = 1e-06
masked_score = -1e30
rotary_base = 10000.0


def chip_cycle(count):
    if count % 4 == 0 and count >= 8:
        wide = count // 4
        tall = 4
    else:
        return list(range(count))
    if wide == 1:
        return list(range(count))
    order = [row * wide for row in range(tall)]
    for step, row in enumerate(reversed(range(tall))):
        columns = range(1, wide) if step % 2 == 0 else reversed(range(1, wide))
        order += [row * wide + column for column in columns]
    return order


class Ring:
    def __init__(self, shards):
        chips = chip_cycle(shards // 2)
        count = len(chips)
        self.steps = count
        self.forward = []
        for place in range(count):
            here, there = chips[place], chips[(place + 1) % count]
            self.forward += [(2 * here, 2 * there), (2 * there + 1, 2 * here + 1)]
        self.swap = [(s, s ^ 1) for s in range(shards)]
        near = np.zeros((shards, count), np.int32)
        far = np.zeros((shards, count), np.int32)
        for place in range(count):
            for core in range(2):
                way = 1 - 2 * core
                for step in range(count):
                    me = 2 * chips[place] + core
                    near[me, step] = 2 * chips[(place - way * step) % count] + core
                    far[me, step] = 2 * chips[(place + way * step) % count] + 1 - core
        self.near, self.far = near, far

    def hop(self, array):
        return lax.ppermute(array, "shard", self.forward)

    def cross(self, array):
        return lax.ppermute(array, "shard", self.swap)

    def part_sum(self, near, far):
        return near.astype(jnp.float32) + self.cross(far).astype(jnp.float32)

    def scatter_sum(self, array, me):
        rows, columns = array.shape
        count = self.steps
        blocks = array.reshape(count, 2, rows // (2 * count), columns)
        core = lax.rem(me, 2)
        mine = lax.dynamic_index_in_dim(blocks, core, axis=1, keepdims=False)
        other = lax.dynamic_index_in_dim(blocks, 1 - core, axis=1, keepdims=False)
        parts = self.part_sum(mine, other.astype(jnp.bfloat16))
        chips = jnp.asarray(self.near // 2)[me]

        def part(step):
            return lax.dynamic_index_in_dim(parts, chips[step], axis=0, keepdims=False)

        total = None
        for step in range(1, count):
            here = part(step) if total is None else part(step) + total.astype(jnp.float32)
            total = self.hop(here.astype(jnp.bfloat16))
        return part(0) + total.astype(jnp.float32)

    def gather(self, array):
        near, far = [array], [self.cross(array)]
        for _ in range(self.steps - 1):
            near.append(self.hop(near[-1]))
            far.append(self.cross(near[-1]))
        return near, far


def rope_tables(tokens):
    halfway = HD // 2
    index_float = jnp.arange(halfway, dtype=jnp.float32)
    frequency = jnp.exp(-jnp.log(rotary_base) * index_float * 2.0 / HD)
    angle = jnp.arange(tokens, dtype=jnp.float32)[:, None] * frequency[None, :]
    cosine, sine = jnp.cos(angle), jnp.sin(angle)
    return (
        jnp.concatenate([cosine] * 4, axis=1),
        jnp.concatenate([-sine, sine, -sine, sine], axis=1),
    )


def dot(l,r): return jnp.dot(l,r,preferred_element_type=jnp.float32)
def dot_nt(l,r): return lax.dot_general(l,r,(((1,),(1,)),((),())),preferred_element_type=jnp.float32)
def dot_tn(l,r): return lax.dot_general(l,r,(((0,),(0,)),((),())),preferred_element_type=jnp.float32)

def swap_halves(values):
    parts=[]
    for start in range(0, values.shape[1], 128):
        part=values[:,start:start+128]
        lane=lax.broadcasted_iota(jnp.int32,part.shape,1)
        parts.append(jnp.where(lane % HD < HD//2, pltpu.roll(part,128-HD//2,1), pltpu.roll(part,HD//2,1)))
    return parts[0] if len(parts)==1 else jnp.concatenate(parts,axis=1)

def tile(table,width):
    return table if width==128 else jnp.concatenate([table]*(width//128),axis=1)

def forward_kernel(block, length_ref, normed_ref, wq_ref, wk_ref, wv_ref, cos_ref, sin_ref,
                   q_ref,k_ref,v_ref,out_ref,total_ref):
    tokens=normed_ref.shape[0]
    length=length_ref[0]
    cos,sin=cos_ref[...],sin_ref[...]
    bf16=jnp.bfloat16
    x=normed_ref[...]
    q=dot(x,wq_ref[...])
    q=q*tile(cos,q.shape[1])+swap_halves(q)*tile(sin,q.shape[1])
    q_ref[...]=(q.astype(bf16).astype(jnp.float32)*(HD**-0.5)).astype(bf16)
    k=dot(x,wk_ref[...])
    k_ref[...]=(k*cos+swap_halves(k)*sin).astype(bf16)
    v_ref[...]=dot(x,wv_ref[...]).astype(bf16)
    groups=HEADS//KV
    for head in range(2):
        for i in range(tokens//block):
            rows=slice(i*block,(i+1)*block)
            span=(i+1)*block
            keys=k_ref[:span,head*HD:(head+1)*HD]
            vals=v_ref[:span,head*HD:(head+1)*HD]
            qs=jnp.concatenate([q_ref[rows,(head*groups+h)*HD:(head*groups+h+1)*HD] for h in range(groups)],axis=0)
            s=dot_nt(keys,qs)
            key_place=lax.broadcasted_iota(jnp.int32,s.shape,0)
            query_place=lax.broadcasted_iota(jnp.int32,s.shape,1) % block + i*block
            s=jnp.where(key_place<=jnp.minimum(query_place,length-1),s,masked_score)
            top=jnp.max(s,axis=0,keepdims=True)
            p=jnp.exp(s-top)
            total=jnp.sum(p,axis=0,keepdims=True)
            p=(p*(1.0/total)).astype(bf16)
            o=dot_tn(p,vals)
            log_total=top+jnp.log(total)
            for h in range(groups):
                at=head*groups+h
                out_ref[rows,at*HD:(at+1)*HD]=o[h*block:(h+1)*block].astype(bf16)
                total_ref[0,at:at+1,rows]=log_total[:,h*block:(h+1)*block]

def attention_forward(length, normed, packed, cos, sin, part, block=256):
    tokens,width=normed.shape
    qw=HEADS*HD//4; kw=KV*HD//4
    bf16=jnp.bfloat16
    qb=HEADS*HD//kw; vb=(HEADS+KV)*HD//kw
    return pl.pallas_call(
        functools.partial(forward_kernel,block),
        out_shape=[jax.ShapeDtypeStruct((tokens,2*qw),bf16),jax.ShapeDtypeStruct((tokens,2*kw),bf16),jax.ShapeDtypeStruct((tokens,2*kw),bf16),
                   jax.ShapeDtypeStruct((tokens,2*qw),bf16),jax.ShapeDtypeStruct((2,HEADS//4,tokens),jnp.float32)],
        grid_spec=pltpu.PrefetchScalarGridSpec(num_scalar_prefetch=1,grid=(2,),
            in_specs=[pl.BlockSpec((tokens,width),lambda g,l:(0,0)),
                      pl.BlockSpec((width,qw),lambda g,l:(0,g+2*part)),
                      pl.BlockSpec((width,kw),lambda g,l:(0,qb+g+2*part)),
                      pl.BlockSpec((width,kw),lambda g,l:(0,vb+g+2*part)),
                      pl.BlockSpec((tokens,128),lambda g,l:(0,0)),pl.BlockSpec((tokens,128),lambda g,l:(0,0))],
            out_specs=[pl.BlockSpec((tokens,qw),lambda g,l:(0,g)),pl.BlockSpec((tokens,kw),lambda g,l:(0,g)),pl.BlockSpec((tokens,kw),lambda g,l:(0,g)),
                       pl.BlockSpec((tokens,qw),lambda g,l:(0,g)),pl.BlockSpec((1,HEADS//4,tokens),lambda g,l:(g,0,0))]),
        compiler_params=pltpu.CompilerParams(vmem_limit_bytes=40*1024*1024),
        cost_estimate=pl.CostEstimate(flops=30*10**9,bytes_accessed=20*1024*1024,transcendentals=0),
    )(length,normed,packed,packed,packed,cos,sin)

def backward_kernel(block,length_ref,q_ref,k_ref,v_ref,slope_ref,total_ref,cos_ref,sin_ref,dq_ref,dk_ref,dv_ref,dq_s,dk_s,dv_s):
    tokens=q_ref.shape[0]
    length=length_ref[0]
    bf16=jnp.bfloat16
    groups=HEADS//KV
    for head in range(2):
        lanes=slice(head*HD,(head+1)*HD)
        for i in reversed(range(tokens//block)):
            rows=slice(i*block,(i+1)*block)
            span=(i+1)*block
            keys=k_ref[:span,lanes]; vals=v_ref[:span,lanes]
            heads=[slice((head*groups+h)*HD,(head*groups+h+1)*HD) for h in range(groups)]
            qs=jnp.concatenate([q_ref[rows,at] for at in heads],axis=0)
            slopes=jnp.concatenate([slope_ref[rows,at] for at in heads],axis=0)
            log_total=jnp.concatenate([total_ref[0,head*groups+h:head*groups+h+1,rows] for h in range(groups)],axis=1)
            s=dot_nt(keys,qs)
            key_place=lax.broadcasted_iota(jnp.int32,s.shape,0)
            query_place=lax.broadcasted_iota(jnp.int32,s.shape,1) % block + i*block
            s=jnp.where(key_place<=jnp.minimum(query_place,length-1),s,masked_score)
            w=jnp.exp(s-log_total)
            ps=dot_nt(vals,slopes)
            centre=jnp.sum(w*ps,axis=0,keepdims=True)
            ds=(w*(ps-centre)).astype(bf16)
            dq=dot_tn(ds,keys)
            dk=dot(ds,qs)
            dv=dot(w.astype(bf16),slopes)
            for h in range(groups):
                dq_s[rows,heads[h]]=dq[h*block:(h+1)*block]*(HD**-0.5)
            if i==tokens//block-1:
                dk_s[:,lanes]=dk; dv_s[:,lanes]=dv
            else:
                dk_s[:span,lanes]+=dk; dv_s[:span,lanes]+=dv
    cos,sin=cos_ref[...],sin_ref[...]
    dq=dq_s[...]
    dq_ref[...]=(dq*tile(cos,dq.shape[1])-swap_halves(dq)*tile(sin,dq.shape[1])).astype(bf16)
    dk=dk_s[...]
    dk_ref[...]=(dk*cos-swap_halves(dk)*sin).astype(bf16)
    dv_ref[...]=dv_s[...].astype(bf16)

def attention_backward(length,q,k,v,slope,total,cos,sin,part,block=256):
    tokens=q.shape[0]
    qw=HEADS*HD//4; kw=KV*HD//4
    bf16=jnp.bfloat16
    qs=pl.BlockSpec((tokens,qw),lambda g,l:(0,g)); ks=pl.BlockSpec((tokens,kw),lambda g,l:(0,g)); cs=pl.BlockSpec((tokens,128),lambda g,l:(0,0))
    return pl.pallas_call(
        functools.partial(backward_kernel,block),
        out_shape=[jax.ShapeDtypeStruct((tokens,2*qw),bf16),jax.ShapeDtypeStruct((tokens,2*kw),bf16),jax.ShapeDtypeStruct((tokens,2*kw),bf16)],
        grid_spec=pltpu.PrefetchScalarGridSpec(num_scalar_prefetch=1,grid=(2,),
            in_specs=[qs,ks,ks,pl.BlockSpec((tokens,qw),lambda g,l:(0,g+2*part)),pl.BlockSpec((1,HEADS//4,tokens),lambda g,l:(g,0,0)),cs,cs],
            out_specs=[qs,ks,ks],
            scratch_shapes=[pltpu.VMEM((tokens,qw),jnp.float32),pltpu.VMEM((tokens,kw),jnp.float32),pltpu.VMEM((tokens,kw),jnp.float32)]),
        compiler_params=pltpu.CompilerParams(vmem_limit_bytes=40*1024*1024),
        cost_estimate=pl.CostEstimate(flops=20*10**9,bytes_accessed=10*1024*1024,transcendentals=0),
    )(length,q,k,v,slope,total,cos,sin)

def pair_kernel(local_experts, chained, where_ref, tokens_a, tokens_b, slope_a, slope_b, row_a, row_b, mask_a, mask_b,
                router_ref, gate_ref, up_ref, down_ref, *rest):
    rest = rest[4:] if chained else rest
    (back_a, back_b, mix_a, mix_b, rows_ref, routed_ref, hidden_ref, slopes_ref, gate_slope_ref, mixed_rows, back_rows, raw_slopes) = rest
    expert = pl.program_id(0)
    tokens = tokens_a.shape[0]
    half = hidden_ref.shape[-1]
    bf16 = jnp.bfloat16
    sides = ((tokens_a, slope_a, row_a, mask_a), (tokens_b, slope_b, row_b, mask_b))
    taken, chosen = [], []
    for side, (tokens_ref, slope_ref, row_ref, mask_ref) in enumerate(sides):
        place = lax.broadcasted_iota(jnp.int32, (CAP, tokens), 0)
        hit = row_ref[0, pl.ds(expert, 1)] == place
        taken.append(hit)
        pick = jnp.where(hit, 1.0, 0.0).astype(bf16)
        rows_ref[0, side * CAP : (side + 1) * CAP] = dot(pick, tokens_ref[...]).astype(bf16)
        raw_slopes[side * CAP : (side + 1) * CAP] = dot(pick, slope_ref[...]).astype(bf16)
        chosen.append(dot_nt(pick, mask_ref[0]))
    rows = rows_ref[0]
    chosen = jnp.concatenate(chosen, axis=0)
    logits = dot(rows, router_ref[...])
    kept = jnp.where(chosen > 0.5, logits, masked_score)
    top = jnp.max(kept, axis=-1, keepdims=True)
    powered = jnp.exp(kept - top) * chosen
    total = jnp.sum(powered, axis=-1, keepdims=True)
    lane = lax.broadcasted_iota(jnp.int32, powered.shape, 1)
    mine = lane == where_ref[2] * local_experts + expert
    gate = jnp.sum(jnp.where(mine, powered, 0.0), axis=-1, keepdims=True) / jnp.where(total > 0.0, total, 1.0)
    gate_part = dot(rows, gate_ref[0])
    up_part = dot(rows, up_ref[0])
    sigma = 1.0 / (1.0 + jnp.exp(-gate_part))
    silu = gate_part * sigma
    hidden = (silu * up_part).astype(bf16)
    hidden_ref[0] = hidden
    slope_rows = raw_slopes[...].astype(jnp.float32)
    routed = (gate * slope_rows).astype(bf16)
    routed_ref[0] = routed
    out = dot(hidden, down_ref[0]).astype(bf16).astype(jnp.float32)
    gate_slope = jnp.sum(out * slope_rows, axis=-1, keepdims=True)
    for side in range(2):
        part = gate_slope[side * CAP : (side + 1) * CAP]
        gate_slope_ref[side, 0] = jnp.sum(jnp.where(taken[side], part, 0.0), axis=0, keepdims=True)
    mixed = (gate * out).astype(bf16)
    hidden_slope = dot_nt(routed, down_ref[0])
    gate_back = (hidden_slope * up_part * sigma * (1.0 + gate_part * (1.0 - sigma))).astype(bf16)
    up_back = (hidden_slope * silu).astype(bf16)
    slopes_ref[0, :, :half] = gate_back
    slopes_ref[0, :, half:] = up_back
    back = (dot_nt(gate_back, gate_ref[0]) + dot_nt(up_back, up_ref[0])).astype(bf16)
    start = pl.multiple_of(expert * CAP, CAP)
    for side in range(2):
        mixed_rows[side, pl.ds(start, CAP), :] = mixed[side * CAP : (side + 1) * CAP]
        back_rows[side, pl.ds(start, CAP), :] = back[side * CAP : (side + 1) * CAP]

    @pl.when(expert == local_experts - 1)
    def _():
        for side, (column_ref, back_ref, mix_ref) in enumerate(((row_a, back_a, mix_a), (row_b, back_b, mix_b))):
            column = lax.broadcasted_iota(jnp.int32, (tokens, local_experts * CAP), 1)
            slots = jnp.transpose(column_ref[0])
            spread = jnp.zeros(column.shape, jnp.float32)
            for e in range(local_experts):
                spread = jnp.where(column - e * CAP == slots[:, e : e + 1], 1.0, spread)
            spread = spread.astype(bf16)
            back_ref[...] = dot(spread, back_rows[side]).astype(bf16)
            mix_ref[...] = dot(spread, mixed_rows[side]).astype(bf16)

def experts_pair(step, steps, where, ta, tb, sa, sb, plan, weights, kept):
    slot_row, mask = plan
    router, gate, up, down = weights
    tokens, width = ta.shape
    local_experts, half = down.shape[0], down.shape[1]
    bf16 = jnp.bfloat16
    chained = kept is not None
    once = pl.Buffered(1)
    block = lambda: pl.BlockSpec((tokens, width), lambda e, w: (0, 0), pipeline_mode=once)
    in_specs = [block(), block(), block(), block()]
    in_specs += [pl.BlockSpec((1, local_experts, tokens), lambda e, w, i=i: (w[i], 0, 0), pipeline_mode=once) for i in range(2)]
    in_specs += [pl.BlockSpec((1, EXPERTS, tokens), lambda e, w, i=i: (w[i], 0, 0), pipeline_mode=once) for i in range(2)]
    in_specs += [
        pl.BlockSpec((width, EXPERTS), lambda e, w: (0, 0), pipeline_mode=once),
        pl.BlockSpec((1, width, half), lambda e, w: (e, 0, 0)),
        pl.BlockSpec((1, width, half), lambda e, w: (e, 0, 0)),
        pl.BlockSpec((1, half, width), lambda e, w: (e, 0, 0)),
    ]
    S = jax.ShapeDtypeStruct
    R = 2 * CAP
    shapes = [S((tokens, width), bf16)] * 4 + [
        S((local_experts, steps * R, width), bf16), S((local_experts, steps * R, width), bf16),
        S((local_experts, steps * R, half), bf16), S((local_experts, steps * R, 2 * half), bf16),
        S((2, local_experts, 1, tokens), jnp.float32)]
    out_specs = [block(), block(), block(), block(),
        pl.BlockSpec((1, R, width), lambda e, w: (e, step, 0)),
        pl.BlockSpec((1, R, width), lambda e, w: (e, step, 0)),
        pl.BlockSpec((1, R, half), lambda e, w: (e, step, 0)),
        pl.BlockSpec((1, R, 2 * half), lambda e, w: (e, step, 0)),
        pl.BlockSpec((2, 1, 1, tokens), lambda e, w: (0, e, 0, 0))]
    operands = [ta, tb, sa, sb, slot_row, slot_row, mask, mask, router, gate, up, down]
    aliases = {}
    if chained:
        first = 1 + len(operands)
        operands += list(kept)
        in_specs += [pl.BlockSpec(memory_space=pl.ANY)] * 4
        aliases = {first + p: 4 + p for p in range(4)}
    flops = local_experts * 4 * CAP * (2 * tokens * width + 6 * width * half + 2 * tokens * width)
    return pl.pallas_call(
        functools.partial(pair_kernel, local_experts, chained),
        out_shape=shapes,
        grid_spec=pltpu.PrefetchScalarGridSpec(num_scalar_prefetch=1, grid=(local_experts,), in_specs=in_specs, out_specs=out_specs,
            scratch_shapes=[pltpu.VMEM((2, local_experts * CAP, width), bf16), pltpu.VMEM((2, local_experts * CAP, width), bf16), pltpu.VMEM((R, width), bf16)]),
        input_output_aliases=aliases,
        compiler_params=pltpu.CompilerParams(vmem_limit_bytes=60 * 1024 * 1024),
        cost_estimate=pl.CostEstimate(flops=flops, bytes_accessed=40 * 1024 * 1024, transcendentals=0),
    )(where, *operands)


def on_device(
    shards,
    reps,
    layer_input,
    attention_gain,
    query_weight,
    key_weight,
    value_weight,
    output_weight,
    expert_gain,
    router_weight,
    gate_weight,
    up_weight,
    down_weight,
    lengths,
    routes,
    cotangent,
):
    ring = Ring(shards)
    me = lax.axis_index("shard")
    tokens = layer_input.shape[0]
    local_experts, half = down_weight.shape[0], down_weight.shape[1]
    length = lengths[0]
    bf16 = jnp.bfloat16
    heads_width = (HEADS + 2 * KV) * HD

    expert_ids = jnp.arange(EXPERTS, dtype=jnp.int32)
    routes_turned = routes.T
    picks = functools.reduce(
        jnp.logical_or, [routes_turned[k][None, :] == expert_ids[:, None] for k in range(TOP)]
    )
    weight_rows = query_weight.shape[0]
    packed = jnp.concatenate(
        [query_weight, key_weight, value_weight, picks.astype(bf16).reshape(weight_rows, -1)],
        axis=1,
    )
    packed_full = lax.all_gather(packed, "shard", axis=0, tiled=True)
    packed_full, output_weight = lax.optimization_barrier((packed_full, output_weight))
    output_full = lax.all_gather(output_weight, "shard", axis=0, tiled=True)
    input_full = packed_full[:, :heads_width]

    valid = (jnp.arange(tokens, dtype=jnp.int32) < length)[:, None]
    slope_low = jnp.where(valid, cotangent, jnp.zeros_like(cotangent))
    slope = slope_low.astype(jnp.float32)
    slope_near = [slope_low]
    for _ in range(2):
        slope_near.append(ring.hop(slope_near[-1]))

    inputs_f = layer_input.astype(jnp.float32)
    first_scale = lax.rsqrt(jnp.mean(inputs_f * inputs_f, axis=-1, keepdims=True) + epsilon)
    base_one = inputs_f * first_scale
    normed_one = (base_one * attention_gain).astype(bf16)
    cosine, sine = rope_tables(tokens)
    packed_full, slope_near[-1] = lax.optimization_barrier((packed_full, slope_near[-1]))
    heads = []
    for part in range(2):
        heads.append(
            attention_forward(lengths, normed_one, packed_full, cosine, sine, part)
        )
        slope_near.append(ring.hop(slope_near[-1]))
        heads[-1], slope_near[-1], packed_full = lax.optimization_barrier(
            (heads[-1], slope_near[-1], packed_full)
        )
    attended = jnp.concatenate([heads[part][3] for part in range(2)], axis=1)
    residual = inputs_f + dot(attended, output_full)
    second_scale = lax.rsqrt(jnp.mean(residual * residual, axis=-1, keepdims=True) + epsilon)
    base_two = residual * second_scale
    normed_two = (base_two * expert_gain).astype(bf16)

    mask_all = packed_full[:, heads_width:].reshape(shards, EXPERTS, tokens)
    mask_mine = lax.dynamic_slice_in_dim(mask_all, me * local_experts, local_experts, axis=1)
    earlier = jnp.triu(jnp.ones((tokens, tokens), bf16), k=1)
    ranks = dot(mask_mine.reshape(shards * local_experts, tokens), earlier).astype(jnp.int32)
    slot_row = jnp.where(mask_mine > 0, ranks.reshape(mask_mine.shape), ABSENT)
    plan = (slot_row, mask_all)

    near = [normed_two]
    near_table, far_table = jnp.asarray(ring.near)[me], jnp.asarray(ring.far)[me]
    weights = (router_weight, gate_weight, up_weight, down_weight)
    kept, gate_slopes, total = None, [], None
    mix_near, mix_far, back_home = [], [], None
    for step in range(ring.steps):
        if step + 1 < ring.steps:
            near.append(ring.hop(near[-1]))
        if step > 0 and len(slope_near) < ring.steps:
            slope_near.append(ring.hop(slope_near[-1]))
            if step + 1 < ring.steps:
                near[-1], slope_near[-1] = lax.optimization_barrier((near[-1], slope_near[-1]))
        results = experts_pair(
            step,
            ring.steps,
            jnp.stack([near_table[step], far_table[step], me]).astype(jnp.int32),
            near[step],
            ring.cross(near[step]),
            slope_near[step],
            ring.cross(slope_near[step]),
            plan,
            weights,
            kept,
        )
        kept = results[4:8]
        mix_near.append(results[2])
        mix_far.append(results[3])
        gate_slopes.append(results[8])
        part = ring.part_sum(results[0], results[1])
        if step == 0:
            back_home = part
        else:
            total = part if total is None else part + total.astype(jnp.float32)
            total = ring.hop(total.astype(bf16))
    rows_all, routed_all, hidden_all, slopes_all = kept
    in_grad = [
        lax.dot_general(
            rows_all[e], slopes_all[e], (((0,), (0,)), ((), ())), preferred_element_type=jnp.float32
        ).astype(bf16)
        for e in range(local_experts)
    ]

    places = np.zeros((shards, shards), np.int32)
    for step in range(ring.steps):
        for shard in range(shards):
            places[shard, ring.near[shard, step]] = 2 * step
            places[shard, ring.far[shard, step]] = 2 * step + 1
    gate_slopes = jnp.concatenate(gate_slopes, axis=0)[:, :, 0, :]
    gate_slopes = jnp.take(gate_slopes, jnp.asarray(places)[me], axis=0)
    gate_slope = lax.all_to_all(
        gate_slopes, "shard", split_axis=0, concat_axis=0, tiled=True
    ).reshape(EXPERTS, tokens)
    logits = lax.dot_general(
        router_weight, normed_two, (((0,), (1,)), ((), ())), preferred_element_type=jnp.float32
    )
    kept_logits = jnp.where(picks, logits, masked_score)
    powered = jnp.where(
        picks, jnp.exp(kept_logits - jnp.max(kept_logits, axis=0, keepdims=True)), 0.0
    )
    gates = powered / jnp.sum(powered, axis=0, keepdims=True)
    mean_slope = jnp.sum(gates * gate_slope, axis=0, keepdims=True)
    logit_slope = (gates * (gate_slope - mean_slope)).astype(bf16)
    router_grad = dot(logit_slope, normed_two)
    normed_slope = (
        back_home
        + total.astype(jnp.float32)
        + lax.dot_general(
            logit_slope, router_weight, (((0,), (1,)), ((), ())), preferred_element_type=jnp.float32
        )
    )
    normed_slope, in_grad, mix_near, mix_far = lax.optimization_barrier(
        (normed_slope, in_grad, mix_near, mix_far)
    )

    def across(array):
        return lax.ppermute(array, "rep", [(0, 1), (1, 0)])

    def mix_hop(step, total):
        part = ring.part_sum(mix_near[step], mix_far[step])
        if total is not None:
            part = part + total.astype(jnp.float32)
        return ring.hop(part.astype(bf16))

    pair = reps == 2
    in_other = [across(in_grad[0])] if pair else []
    mix = mix_hop(1, None)
    expert_gain_grad = jnp.sum(normed_slope * base_two, axis=0)
    scaled_two = normed_slope * expert_gain
    residual_slope = (
        slope
        + second_scale * scaled_two
        - base_two
        * second_scale
        * second_scale
        * jnp.mean(scaled_two * residual, axis=-1, keepdims=True)
    )
    branch_slope = residual_slope.astype(bf16)
    output_grad = lax.dot_general(
        attended, branch_slope, (((0,), (0,)), ((), ())), preferred_element_type=jnp.float32
    ).astype(bf16)
    attended_slope = jnp.einsum(
        "sd,cd->sc", branch_slope, output_full, preferred_element_type=jnp.float32
    ).astype(bf16)
    output_owned = lax.psum_scatter(output_grad, "shard", scatter_dimension=0, tiled=True)

    slopes_out = []
    mix_step = 2
    for part in range(2):
        attended_slope, mix = lax.optimization_barrier((attended_slope, mix))
        if mix_step < ring.steps:
            mix = mix_hop(mix_step, mix)
            mix_step += 1
        queries, keys, values, _, log_totals = heads[part]
        slopes_out.append(
            attention_backward(
                lengths, queries, keys, values, attended_slope, log_totals, cosine, sine, part
            )
        )
        if part == 0:
            attended_slope, slopes_out[0], in_other = lax.optimization_barrier(
                (attended_slope, slopes_out[0], in_other)
            )
            if pair and local_experts > 1:
                in_other.append(across(in_grad[1]))
    pre_slopes = jnp.concatenate(
        [slopes_out[part][which] for which in range(3) for part in range(2)], axis=1
    )
    pre_slopes, mix = lax.optimization_barrier((pre_slopes, mix))
    if mix_step < ring.steps:
        mix = mix_hop(mix_step, mix)
        mix_step += 1
    input_grad = lax.dot_general(
        normed_one, pre_slopes, (((0,), (0,)), ((), ())), preferred_element_type=jnp.float32
    ).astype(bf16)
    input_owned = lax.psum_scatter(input_grad, "shard", scatter_dimension=0, tiled=True)
    normed_one_slope = jnp.einsum(
        "sc,dc->sd", pre_slopes, input_full, preferred_element_type=jnp.float32
    )
    hidden_all, normed_one_slope = lax.optimization_barrier((hidden_all, normed_one_slope))
    down_grad = jnp.einsum(
        "erf,erd->efd", hidden_all, routed_all, preferred_element_type=jnp.float32
    ).astype(bf16)
    attention_gain_grad = jnp.sum(normed_one_slope * base_one, axis=0)
    scaled_one = normed_one_slope * attention_gain
    input_slope = (
        residual_slope
        + first_scale * scaled_one
        - base_one
        * first_scale
        * first_scale
        * jnp.mean(scaled_one * inputs_f, axis=-1, keepdims=True)
    )
    input_gradient = input_slope.astype(bf16)
    if pair:
        in_other, down_grad = lax.optimization_barrier((in_other, down_grad))
    mix, down_grad = lax.optimization_barrier((mix, down_grad))
    if pair:
        down_other = across(down_grad)
    while mix_step < ring.steps:
        mix = mix_hop(mix_step, mix)
        if pair and mix_step == ring.steps - 2:
            mix, down_other = lax.optimization_barrier((mix, down_other))
        mix_step += 1
    layer_output = (
        residual + ring.part_sum(mix_near[0], mix_far[0]) + mix.astype(jnp.float32)
    ).astype(bf16)

    def rep_sum(*arrays):
        if not pair:
            return lax.psum(tuple(array.astype(jnp.float32) for array in arrays), "rep")
        low = [array.astype(bf16) for array in arrays]
        return tuple(a.astype(jnp.float32) + across(a).astype(jnp.float32) for a in low)

    if pair:
        in_sum = jnp.stack(
            [a.astype(jnp.float32) + b.astype(jnp.float32) for a, b in zip(in_grad, in_other)]
        )
        down_sum = down_grad.astype(jnp.float32) + down_other.astype(jnp.float32)
    else:
        in_sum, down_sum = rep_sum(jnp.stack(in_grad), down_grad)
    gain_sum = jnp.concatenate(
        [attention_gain_grad[None], expert_gain_grad[None], router_grad], axis=0
    )
    for axis, size in (("rep", reps), ("shard", shards)):
        far_bit = 1
        while far_bit < size:
            gain_sum = gain_sum + lax.ppermute(
                gain_sum, axis, [(place, place ^ far_bit) for place in range(size)]
            )
            far_bit *= 2
    output_sum, input_sum = rep_sum(output_owned, input_owned)
    return (
        layer_output,
        input_gradient,
        gain_sum[0],
        input_sum[:, : HEADS * HD],
        input_sum[:, HEADS * HD : (HEADS + KV) * HD],
        input_sum[:, (HEADS + KV) * HD :],
        output_sum,
        gain_sum[1],
        gain_sum[2:].T,
        in_sum[..., :half],
        in_sum[..., half:],
        down_sum,
    )


def solution(mesh):
    return jax.shard_map(
        functools.partial(on_device, mesh.shape["shard"], mesh.shape["rep"]),
        mesh=mesh,
        in_specs=(
            P(("shard", "rep"), None),
            P(),
            P("shard", None),
            P("shard", None),
            P("shard", None),
            P("shard", None),
            P(),
            P(),
            P("shard", None, None),
            P("shard", None, None),
            P("shard", None, None),
            P(("shard", "rep")),
            P(("shard", "rep"), None),
            P(("shard", "rep"), None),
        ),
        out_specs=(
            P(("shard", "rep"), None),
            P(("shard", "rep"), None),
            P(),
            P("shard", None),
            P("shard", None),
            P("shard", None),
            P("shard", None),
            P(),
            P(),
            P("shard", None, None),
            P("shard", None, None),
            P("shard", None, None),
        ),
        check_vma=False,
    )
```

time: 1500 us -> 944 us (0.63)
  waiting for transfers between devices: 549 us -> 256 us
  matrix products: 264 us -> 85.5 us
  other arithmetic: 188 us -> 119 us
  local copies, waits for them, and re-layouts: 92.5 us -> 42 us
  blocking collectives: 38.5 us -> 0 us
  starting transfers between devices: 35.4 us -> 72.7 us
  Pallas kernels: 315 us -> 342 us
    dot_general x19 -> x7, matrix products: 232 us -> 52.5 us  [the longest x2 32.8 us: on_device(): lax.dot_general(rows_all[e], slopes_all[e], (((0,), (0,)), ((), ())), pre...]
    reduce_scatter x1, waiting for transfers between devices: 78.2 us -> 0.01 us  [on_device(): lax.psum_scatter(input_grad, 'shard', scatter_dimension=0, tiled=True)]
    psum x2 -> x0, waiting for transfers between devices: 59.5 us -> none  [the longest x1 59.5 us: on_device(): early = lax.psum((expert_gain_grad, router_grad), ('shard', 'rep'))]
    ppermute x28, waiting for transfers between devices: 245 us -> 185 us  [hop(): return lax.ppermute(array, 'shard', self.forward)]
    all_gather x1, waiting for transfers between devices: 58.4 us -> 2.24 us  [on_device(): packed_full = lax.all_gather(packed, 'shard', axis=0, tiled=True)]
    convert_element_type x17, other arithmetic: 102 us -> 61.1 us  [the longest x7 33.5 us: on_device(): total = ring.hop(total.astype(bf16))]
    psum x1 -> x0, blocking collectives: 38.5 us -> none  [on_device(): gain_sum = lax.psum(attention_gain_grad, ('shard', 'rep'))]
    all_gather x1, waiting for transfers between devices: 31.4 us -> 0.01 us  [on_device(): output_full = lax.all_gather(output_weight, 'shard', axis=0, tiled=True)]
  transfers between devices with their start and end apart: 69 -> 75, of which waited for: 19 -> 25; matrix products, arithmetic and copies ran while one was open for 18% -> 23% of each run, Pallas kernels for 21% -> 37%
where the time goes in v2:
time: 944 us; the launch traced here: 934 us
  Pallas kernels  342 us (36%)
  waiting for transfers between devices  256 us (27%)
  other arithmetic  119 us (13%)
  matrix products  85.5 us (9%)
  starting transfers between devices  72.7 us (8%)
  local copies, waits for them, and re-layouts  42 us (4%)
  between operations  16.3 us (2%)
    pallas_call x8, Pallas kernels, experts_pair(): pl.pallas_call(functools.partial(pair_kernel, local_experts, chained), ou...  263 us
    ppermute x28, waiting for transfers between devices, hop(): return lax.ppermute(array, 'shard', self.forward)  185 us
    ppermute x5, waiting for transfers between devices, on_device(): lax.ppermute(gain_sum, axis, [(place, place ^ far_bit) for place in range...  58.4 us
    ppermute x28, starting transfers between devices, hop(): return lax.ppermute(array, 'shard', self.forward)  50 us
    pallas_call x2, Pallas kernels, attention_backward(): pl.pallas_call(functools.partial(backward_kernel, block), out_shape=[jax....  40.4 us
    pallas_call x2, Pallas kernels, attention_forward(): pl.pallas_call(functools.partial(forward_kernel, block), out_shape=[jax.S...  38 us
    convert_element_type x7, other arithmetic, on_device(): total = ring.hop(total.astype(bf16))  33.5 us
    dot_general x2, matrix products, on_device(): lax.dot_general(rows_all[e], slopes_all[e], (((0,), (0,)), ((), ())), pre...  32.8 us
  transfers between devices with their start and end apart: 75, of which 25 were waited for; matrix products, arithmetic and copies ran while one was open for 23% of the time, Pallas kernels for 37%

profile of v2, /device:TPU:0, one launch (start us, length us, event | category | flops | bytes accessed | tf_op | source)
XLA Modules:
  0.0 933.9 jit_solution(29601623170864341)
XLA Ops:
  16.7 43.0 %collective-permute-done.slope_a = bf16[1024,1024]{1,0:T(8,128)(2,1)} collective-permute-done((bf16[1024,1024]{1,0:T(8,128)(2,1)}, bf16[1024,1024]{1,0:T(8,128)(2,1)}, u32[]{:S(2)}, u32[]{:S(2)}) %collective-permute-start) | collective-permute-done | bytes 2097184 | tf_op jit(solution)/shard_map/ppermute | solution.py:63
  59.8 9.9 %collective-permute-start.1 = (bf16[1024,1024]{1,0:T(8,128)(2,1)}, bf16[1024,1024]{1,0:T(8,128)(2,1)}, u32[]{:S(2)}, u32[]{:S(2)}) collective-permute-start(bf16[1024,1024]{1,0:T(8,128)(2,1)} %collective-permute-done.slope_a), channel_id=1, source_target_pairs={{0,8},{10,2},{8,16},{18,10},{16,24},{26,18},{24,28},{30,26},{28,20... | collective-permute-start | bytes 6291464 | tf_op jit(solution)/shard_map/ppermute | solution.py:63
  76.4 18.2 %collective-permute-done.1.slope_a = bf16[1024,1024]{1,0:T(8,128)(2,1)} collective-permute-done((bf16[1024,1024]{1,0:T(8,128)(2,1)}, bf16[1024,1024]{1,0:T(8,128)(2,1)}, u32[]{:S(2)}, u32[]{:S(2)}) %collective-permute-start.1) | collective-permute-done | bytes 2097184 | tf_op jit(solution)/shard_map/ppermute | solution.py:63
  99.9 19.0 %shard_map.256 = (bf16[1024,512]{1,0:T(8,128)(2,1)S(1)}, bf16[1024,256]{1,0:T(8,128)(2,1)S(1)}, bf16[1024,256]{1,0:T(8,128)(2,1)S(1)}, bf16[1024,512]{1,0:T(8,128)(2,1)S(1)}, f32[2,4,1024]{2,1,0:T(4,128)S(1)}) custom-call(s32[1]{0:T(128)} %copy.123.length_ref, bf16[1024,1024]{1,0:T(8,128)(2,1)S(1)} %fusion.13.normed_ref, bf16[1024,2560]{1,0:T(8,128)(2,1)S(1)} %copy-done, ...), custom_call_target="tpu_custom_call" | custom-call | flops 30000001024 | bytes 20971520 | tf_op jit(solution)/shard_map/pallas_call | solution.py:166
  121.5 7.5 collective-permute-done.2.slope_a
  132.9 19.0 %shard_map.257 = (bf16[1024,512]{1,0:T(8,128)(2,1)S(1)}, bf16[1024,256]{1,0:T(8,128)(2,1)S(1)}, bf16[1024,256]{1,0:T(8,128)(2,1)S(1)}, bf16[1024,512]{1,0:T(8,128)(2,1)S(1)}, f32[2,4,1024]{2,1,0:T(4,128)S(1)}) custom-call(s32[1]{0:T(128)} %copy.123.length_ref, bf16[1024,1024]{1,0:T(8,128)(2,1)S(1)} %fusion.13.normed_ref, bf16[1024,2560]{1,0:T(8,128)(2,1)S(1)} %copy-done, ...), custom_call_target="tpu_custom_call" | custom-call | flops 30000001024 | bytes 20971520 | tf_op jit(solution)/shard_map/pallas_call | solution.py:166
  181.6 13.3 %collective-permute-done.7.tokens_a = bf16[1024,1024]{1,0:T(8,128)(2,1)} collective-permute-done((bf16[1024,1024]{1,0:T(8,128)(2,1)}, bf16[1024,1024]{1,0:T(8,128)(2,1)}, u32[]{:S(2)}, u32[]{:S(2)}) %collective-permute-start.7) | collective-permute-done | bytes 2097184 | tf_op jit(solution)/shard_map/ppermute | solution.py:63
  201.8 33.0 %shard_map.258 = (bf16[1024,1024]{1,0:T(8,128)(2,1)}, bf16[1024,1024]{1,0:T(8,128)(2,1)}, bf16[1024,1024]{1,0:T(8,128)(2,1)}, bf16[1024,1024]{1,0:T(8,128)(2,1)}...) custom-call(s32[3]{0:T(128)} %add_add_fusion.1.where_ref, ...), custom_call_target="tpu_custom_call" | custom-call | flops 16911433728 | bytes 41943040 | tf_op jit(solution)/shard_map/pallas_call | solution.py:341
  234.8 32.8 %shard_map.259 = (bf16[1024,1024]{1,0:T(8,128)(2,1)}, bf16[1024,1024]{1,0:T(8,128)(2,1)}, bf16[1024,1024]{1,0:T(8,128)(2,1)}, bf16[1024,1024]{1,0:T(8,128)(2,1)}...) custom-call(s32[3]{0:T(128)} %add_add_fusion.8.where_ref, ...), custom_call_target="tpu_custom_call", output_to_operand_aliasing={{4}: (13, {}), {5}: (14, {}), {6}: (15, {}), {7}: (16, {})} | custom-call | flops 16911433728 | bytes 41943040 | tf_op jit(solution)/shard_map/pallas_call | solution.py:341
  279.3 33.0 %shard_map.260 = (bf16[1024,1024]{1,0:T(8,128)(2,1)}, bf16[1024,1024]{1,0:T(8,128)(2,1)}, bf16[1024,1024]{1,0:T(8,128)(2,1)}, bf16[1024,1024]{1,0:T(8,128)(2,1)}...) custom-call(s32[3]{0:T(128)} %add_add_fusion.7.where_ref, ...), custom_call_target="tpu_custom_call", output_to_operand_aliasing={{4}: (13, {}), {5}: (14, {}), {6}: (15, {}), {7}: (16, {})} | custom-call | flops 16911433728 | bytes 41943040 | tf_op jit(solution)/shard_map/pallas_call | solution.py:341
  312.9 6.1 collective-permute-done.11.slope_a
  321.9 19.6 %collective-permute-done.38 = bf16[1024,1024]{1,0:T(8,128)(2,1)} collective-permute-done((bf16[1024,1024]{1,0:T(8,128)(2,1)}, bf16[1024,1024]{1,0:T(8,128)(2,1)}, u32[]{:S(2)}, u32[]{:S(2)}) %collective-permute-start.38) | collective-permute-done | bytes 2097184 | tf_op jit(solution)/shard_map/ppermute | solution.py:63
  347.7 32.8 %shard_map.261 = (bf16[1024,1024]{1,0:T(8,128)(2,1)}, bf16[1024,1024]{1,0:T(8,128)(2,1)}, bf16[1024,1024]{1,0:T(8,128)(2,1)}, bf16[1024,1024]{1,0:T(8,128)(2,1)}...) custom-call(s32[3]{0:T(128)} %add_add_fusion.6.where_ref, ...), custom_call_target="tpu_custom_call", output_to_operand_aliasing={{4}: (13, {}), {5}: (14, {}), {6}: (15, {}), {7}: (16, {})} | custom-call | flops 16911433728 | bytes 41943040 | tf_op jit(solution)/shard_map/pallas_call | solution.py:341
  389.4 19.5 %collective-permute-done.39 = bf16[1024,1024]{1,0:T(8,128)(2,1)} collective-permute-done((bf16[1024,1024]{1,0:T(8,128)(2,1)}, bf16[1024,1024]{1,0:T(8,128)(2,1)}, u32[]{:S(2)}, u32[]{:S(2)}) %collective-permute-start.39) | collective-permute-done | bytes 2097184 | tf_op jit(solution)/shard_map/ppermute | solution.py:63
  415.1 33.0 %shard_map.262 = (bf16[1024,1024]{1,0:T(8,128)(2,1)}, bf16[1024,1024]{1,0:T(8,128)(2,1)}, bf16[1024,1024]{1,0:T(8,128)(2,1)}, bf16[1024,1024]{1,0:T(8,128)(2,1)}...) custom-call(s32[3]{0:T(128)} %add_add_fusion.5.where_ref, ...), custom_call_target="tpu_custom_call", output_to_operand_aliasing={{4}: (13, {}), {5}: (14, {}), {6}: (15, {}), {7}: (16, {})} | custom-call | flops 16911433728 | bytes 41943040 | tf_op jit(solution)/shard_map/pallas_call | solution.py:341
  460.0 32.8 %shard_map.263 = (bf16[1024,1024]{1,0:T(8,128)(2,1)}, bf16[1024,1024]{1,0:T(8,128)(2,1)}, bf16[1024,1024]{1,0:T(8,128)(2,1)}, bf16[1024,1024]{1,0:T(8,128)(2,1)}...) custom-call(s32[3]{0:T(128)} %add_add_fusion.4.where_ref, ...), custom_call_target="tpu_custom_call", output_to_operand_aliasing={{4}: (13, {}), {5}: (14, {}), {6}: (15, {}), {7}: (16, {})} | custom-call | flops 16911433728 | bytes 41943040 | tf_op jit(solution)/shard_map/pallas_call | solution.py:341
  505.4 33.2 %shard_map.264 = (bf16[1024,1024]{1,0:T(8,128)(2,1)}, bf16[1024,1024]{1,0:T(8,128)(2,1)}, bf16[1024,1024]{1,0:T(8,128)(2,1)}, bf16[1024,1024]{1,0:T(8,128)(2,1)}...) custom-call(s32[3]{0:T(128)} %add_add_fusion.3.where_ref, ...), custom_call_target="tpu_custom_call", output_to_operand_aliasing={{4}: (13, {}), {5}: (14, {}), {6}: (15, {}), {7}: (16, {})} | custom-call | flops 16911433728 | bytes 41943040 | tf_op jit(solution)/shard_map/pallas_call | solution.py:341
  554.3 32.8 %shard_map.265 = (bf16[1024,1024]{1,0:T(8,128)(2,1)}, bf16[1024,1024]{1,0:T(8,128)(2,1)}, bf16[1024,1024]{1,0:T(8,128)(2,1)}, bf16[1024,1024]{1,0:T(8,128)(2,1)}...) custom-call(s32[3]{0:T(128)} %add_add_fusion.2.where_ref, ...), custom_call_target="tpu_custom_call", output_to_operand_aliasing={{4}: (13, {}), {5}: (14, {}), {6}: (15, {}), {7}: (16, {})} | custom-call | flops 16911433728 | bytes 41943040 | tf_op jit(solution)/shard_map/pallas_call | solution.py:341
  596.0 16.4 %fusion.32 = bf16[1024,1024]{1,0:T(8,128)(2,1)} fusion(bf16[2,4608,1024]{2,1,0:T(8,128)(2,1)} %get-tuple-element.242, bf16[2,4608,1024]{2,1,0:T(8,128)(2,1)} %get-tuple-element.241), kind=kOutput, calls=%fused_computation.62 | convolution fusion | flops 9664724992 | bytes 20971520 | tf_op jit(solution)/shard_map/dot_general | solution.py:464
  619.2 16.4 %fusion.27 = bf16[1024,1024]{1,0:T(8,128)(2,1)} fusion(bf16[2,4608,1024]{2,1,0:T(8,128)(2,1)} %get-tuple-element.242, bf16[2,4608,1024]{2,1,0:T(8,128)(2,1)} %get-tuple-element.241), kind=kOutput, calls=%fused_computation.61 | convolution fusion | flops 9664724992 | bytes 20971520 | tf_op jit(solution)/shard_map/dot_general | solution.py:464
  663.7 15.5 %collective-permute-done.51 = bf16[1024,1024]{1,0:T(8,128)(2,1)S(1)} collective-permute-done((bf16[1024,1024]{1,0:T(8,128)(2,1)S(1)}, bf16[1024,1024]{1,0:T(8,128)(2,1)S(1)}, u32[]{:S(2)}, u32[]{:S(2)}) %collective-permute-start.51) | collective-permute-done | bytes 2097184 | tf_op jit(solution)/shard_map/ppermute | solution.py:63
  695.7 20.3 %shard_map.266 = (bf16[1024,512]{1,0:T(8,128)(2,1)S(1)}, bf16[1024,256]{1,0:T(8,128)(2,1)S(1)}, bf16[1024,256]{1,0:T(8,128)(2,1)S(1)}) custom-call(s32[1]{0:T(128)} %copy.123.length_ref, bf16[1024,512]{1,0:T(8,128)(2,1)S(1)} %copy-done.6, bf16[1024,256]{1,0:T(8,128)(2,1)S(1)} %copy-done.12, bf16[1024,256]{1,0:T(8,128)(2,1)S(1)} %copy-done.14, ...), custom_call_target="tpu_custom_call" | custom-call | flops 20000000000 | bytes 10485760 | tf_op jit(solution)/shard_map/pallas_call | solution.py:226
  723.3 20.1 %shard_map.267 = (bf16[1024,512]{1,0:T(8,128)(2,1)S(1)}, bf16[1024,256]{1,0:T(8,128)(2,1)S(1)}, bf16[1024,256]{1,0:T(8,128)(2,1)S(1)}) custom-call(s32[1]{0:T(128)} %copy.123.length_ref, bf16[1024,512]{1,0:T(8,128)(2,1)S(1)} %copy-done.4, bf16[1024,256]{1,0:T(8,128)(2,1)S(1)} %copy-done.8, bf16[1024,256]{1,0:T(8,128)(2,1)S(1)} %copy-done.10, ...), custom_call_target="tpu_custom_call" | custom-call | flops 20000000000 | bytes 10485760 | tf_op jit(solution)/shard_map/pallas_call | solution.py:226
  747.8 7.8 collective-permute-done.56
  755.6 8.4 fusion.22
  770.9 17.1 %convolution_convert_fusion.1 = bf16[2,512,1024]{2,1,0:T(8,128)(2,1)} fusion(bf16[2,4608,512]{2,1,0:T(8,128)(2,1)} %get-tuple-element.304, bf16[2,4608,1024]{2,1,0:T(8,128)(2,1)} %get-tuple-element.305), kind=kOutput, calls=%fused_computation.63 | convolution fusion | flops 9664724992 | bytes 30408704 | tf_op jit(solution)/shard_map/erf,erd->efd/dot_general | solution.py:567
  788.0 6.8 collective-permute-done.57
  800.0 6.5 convolution_convert_fusion
  814.4 9.6 %collective-permute-done.59 = bf16[1024,1024]{1,0:T(8,128)(2,1)} collective-permute-done((bf16[1024,1024]{1,0:T(8,128)(2,1)}, bf16[1024,1024]{1,0:T(8,128)(2,1)}, u32[]{:S(2)}, u32[]{:S(2)}) %collective-permute-start.59) | collective-permute-done | bytes 2097184 | tf_op jit(solution)/shard_map/ppermute | solution.py:63
  832.7 30.5 %collective-permute-done.63 = f32[34,1024]{1,0:T(8,128)S(1)} collective-permute-done((f32[34,1024]{1,0:T(8,128)S(1)}, f32[34,1024]{1,0:T(8,128)S(1)}, u32[]{:S(2)}, u32[]{:S(2)}) %collective-permute-start.63) | collective-permute-done | bytes 139296 | tf_op jit(solution)/shard_map/ppermute | solution.py:614
  886.7 25.1 %collective-permute-done.67 = f32[34,1024]{1,0:T(8,128)S(1)} collective-permute-done((f32[34,1024]{1,0:T(8,128)S(1)}, f32[34,1024]{1,0:T(8,128)S(1)}, u32[]{:S(2)}, u32[]{:S(2)}) %collective-permute-start.67) | collective-permute-done | bytes 139296 | tf_op jit(solution)/shard_map/ppermute | solution.py:614
  914.4 5.7 convert_add_fusion.1
  (433 shorter events, 272.7 us)
Async XLA Ops:
  7.2 69.2 %all-gather.3.cloned.1.call-start = ((), (), s32[]{:S(2)}) async-start(), calls=%async_computation.3 | async-start | bytes 5570560 | tf_op jit(solution)/shard_map/all_gather | solution.py:388
  11.4 146.9 %all-gather.5.cloned.1.call-start = ((), (), s32[]{:S(2)}) async-start(), calls=%async_computation.4 | async-start | bytes 2228224 | tf_op jit(solution)/shard_map/all_gather | solution.py:390
  13.7 46.0 %collective-permute-start = (bf16[1024,1024]{1,0:T(8,128)(2,1)}, bf16[1024,1024]{1,0:T(8,128)(2,1)}, u32[]{:S(2)}, u32[]{:S(2)}) collective-permute-start(bf16[1024,1024]{1,0:T(8,128)(2,1)} %broadcast_select_fusion.slope_a), channel_id=1, source_target_pairs={{0,8},{10,2},{8,16},{18,10},{16,24},{26,18},{24,28},{30,26},{28,20... | collective-permute-start | bytes 6291464 | tf_op jit(solution)/shard_map/ppermute | solution.py:63
  177.1 57.7 %collective-permute-start.30 = (bf16[1024,1024]{1,0:T(8,128)(2,1)}, bf16[1024,1024]{1,0:T(8,128)(2,1)}, u32[]{:S(2)}, u32[]{:S(2)}) collective-permute-start(bf16[1024,1024]{1,0:T(8,128)(2,1)} %collective-permute-done.slope_a), channel_id=1, source_target_pairs={{0,2},{2,0},{4,6},{6,4},{8,10},{10,8},{12,14},{14,12},{16,18},{18,... | collective-permute-start | bytes 6291464 | tf_op jit(solution)/shard_map/ppermute | solution.py:66
  196.3 71.9 %collective-permute-start.9 = (bf16[1024,1024]{1,0:T(8,128)(2,1)}, bf16[1024,1024]{1,0:T(8,128)(2,1)}, u32[]{:S(2)}, u32[]{:S(2)}) collective-permute-start(bf16[1024,1024]{1,0:T(8,128)(2,1)} %collective-permute-done.3.slope_a), channel_id=1, source_target_pairs={{0,8},{10,2},{8,16},{18,10},{16,24},{26,18},{24,28},{30,26},{28,20... | collective-permute-start | bytes 6291464 | tf_op jit(solution)/shard_map/ppermute | solution.py:63
  199.5 68.7 %collective-permute-start.8 = (bf16[1024,1024]{1,0:T(8,128)(2,1)}, bf16[1024,1024]{1,0:T(8,128)(2,1)}, u32[]{:S(2)}, u32[]{:S(2)}) collective-permute-start(bf16[1024,1024]{1,0:T(8,128)(2,1)} %collective-permute-done.7.tokens_a), channel_id=1, source_target_pairs={{0,8},{10,2},{8,16},{18,10},{16,24},{26,18},{24,28},{30,26},{28,20... | collective-permute-start | bytes 6291464 | tf_op jit(solution)/shard_map/ppermute | solution.py:63
  270.2 42.7 %collective-permute-start.10 = (bf16[1024,1024]{1,0:T(8,128)(2,1)}, bf16[1024,1024]{1,0:T(8,128)(2,1)}, u32[]{:S(2)}, u32[]{:S(2)}) collective-permute-start(bf16[1024,1024]{1,0:T(8,128)(2,1)} %collective-permute-done.8.tokens_a), channel_id=1, source_target_pairs={{0,8},{10,2},{8,16},{18,10},{16,24},{26,18},{24,28},{30,26},{28,20... | collective-permute-start | bytes 6291464 | tf_op jit(solution)/shard_map/ppermute | solution.py:63
  271.3 47.6 %collective-permute-start.11 = (bf16[1024,1024]{1,0:T(8,128)(2,1)}, bf16[1024,1024]{1,0:T(8,128)(2,1)}, u32[]{:S(2)}, u32[]{:S(2)}) collective-permute-start(bf16[1024,1024]{1,0:T(8,128)(2,1)} %collective-permute-done.9.slope_a), channel_id=1, source_target_pairs={{0,8},{10,2},{8,16},{18,10},{16,24},{26,18},{24,28},{30,26},{28,20... | collective-permute-start | bytes 6291464 | tf_op jit(solution)/shard_map/ppermute | solution.py:63
  278.1 63.3 %collective-permute-start.38 = (bf16[1024,1024]{1,0:T(8,128)(2,1)}, bf16[1024,1024]{1,0:T(8,128)(2,1)}, u32[]{:S(2)}, u32[]{:S(2)}) collective-permute-start(bf16[1024,1024]{1,0:T(8,128)(2,1)} %add_convert_fusion.14), channel_id=1, source_target_pairs={{0,8},{10,2},{8,16},{18,10},{16,24},{26,18},{24,28},{30,26},{28,20... | collective-permute-start | bytes 6291464 | tf_op jit(solution)/shard_map/ppermute | solution.py:63
  320.7 60.3 %collective-permute-start.12 = (bf16[1024,1024]{1,0:T(8,128)(2,1)}, bf16[1024,1024]{1,0:T(8,128)(2,1)}, u32[]{:S(2)}, u32[]{:S(2)}) collective-permute-start(bf16[1024,1024]{1,0:T(8,128)(2,1)} %collective-permute-done.10.tokens_a), channel_id=1, source_target_pairs={{0,8},{10,2},{8,16},{18,10},{16,24},{26,18},{24,28},{30,26},{28,20... | collective-permute-start | bytes 6291464 | tf_op jit(solution)/shard_map/ppermute | solution.py:63
  341.5 44.9 %collective-permute-start.13 = (bf16[1024,1024]{1,0:T(8,128)(2,1)}, bf16[1024,1024]{1,0:T(8,128)(2,1)}, u32[]{:S(2)}, u32[]{:S(2)}) collective-permute-start(bf16[1024,1024]{1,0:T(8,128)(2,1)} %collective-permute-done.11.slope_a), channel_id=1, source_target_pairs={{0,8},{10,2},{8,16},{18,10},{16,24},{26,18},{24,28},{30,26},{28,20... | collective-permute-start | bytes 6291464 | tf_op jit(solution)/shard_map/ppermute | solution.py:63
  347.6 61.2 %collective-permute-start.39 = (bf16[1024,1024]{1,0:T(8,128)(2,1)}, bf16[1024,1024]{1,0:T(8,128)(2,1)}, u32[]{:S(2)}, u32[]{:S(2)}) collective-permute-start(bf16[1024,1024]{1,0:T(8,128)(2,1)} %add_convert_fusion.13), channel_id=1, source_target_pairs={{0,8},{10,2},{8,16},{18,10},{16,24},{26,18},{24,28},{30,26},{28,20... | collective-permute-start | bytes 6291464 | tf_op jit(solution)/shard_map/ppermute | solution.py:63
  388.2 60.5 %collective-permute-start.14 = (bf16[1024,1024]{1,0:T(8,128)(2,1)}, bf16[1024,1024]{1,0:T(8,128)(2,1)}, u32[]{:S(2)}, u32[]{:S(2)}) collective-permute-start(bf16[1024,1024]{1,0:T(8,128)(2,1)} %collective-permute-done.12.tokens_a), channel_id=1, source_target_pairs={{0,8},{10,2},{8,16},{18,10},{16,24},{26,18},{24,28},{30,26},{28,20... | collective-permute-start | bytes 6291464 | tf_op jit(solution)/shard_map/ppermute | solution.py:63
  450.5 42.9 %collective-permute-start.15 = (bf16[1024,1024]{1,0:T(8,128)(2,1)}, bf16[1024,1024]{1,0:T(8,128)(2,1)}, u32[]{:S(2)}, u32[]{:S(2)}) collective-permute-start(bf16[1024,1024]{1,0:T(8,128)(2,1)} %collective-permute-done.14.tokens_a), channel_id=1, source_target_pairs={{0,8},{10,2},{8,16},{18,10},{16,24},{26,18},{24,28},{30,26},{28,20... | collective-permute-start | bytes 6291464 | tf_op jit(solution)/shard_map/ppermute | solution.py:63
  495.8 43.9 %collective-permute-start.16 = (bf16[1024,1024]{1,0:T(8,128)(2,1)}, bf16[1024,1024]{1,0:T(8,128)(2,1)}, u32[]{:S(2)}, u32[]{:S(2)}) collective-permute-start(bf16[1024,1024]{1,0:T(8,128)(2,1)} %collective-permute-done.15.tokens_a), channel_id=1, source_target_pairs={{0,8},{10,2},{8,16},{18,10},{16,24},{26,18},{24,28},{30,26},{28,20... | collective-permute-start | bytes 6291464 | tf_op jit(solution)/shard_map/ppermute | solution.py:63
  504.6 43.9 %collective-permute-start.42 = (bf16[1024,1024]{1,0:T(8,128)(2,1)}, bf16[1024,1024]{1,0:T(8,128)(2,1)}, u32[]{:S(2)}, u32[]{:S(2)}) collective-permute-start(bf16[1024,1024]{1,0:T(8,128)(2,1)} %add_convert_fusion.10), channel_id=1, source_target_pairs={{0,8},{10,2},{8,16},{18,10},{16,24},{26,18},{24,28},{30,26},{28,20... | collective-permute-start | bytes 6291464 | tf_op jit(solution)/shard_map/ppermute | solution.py:63
  547.6 91.5 %collective-permute-start.6 = (bf16[1024,1024]{1,0:T(8,128)(2,1)}, bf16[1024,1024]{1,0:T(8,128)(2,1)}, u32[]{:S(2)}, u32[]{:S(2)}) collective-permute-start(bf16[1024,1024]{1,0:T(8,128)(2,1)} %get-tuple-element.183), channel_id=1, source_target_pairs={{0,2},{2,0},{4,6},{6,4},{8,10},{10,8},{12,14},{14,12},{16,18},{18,... | collective-permute-start | bytes 6291464 | tf_op jit(solution)/shard_map/ppermute | solution.py:66
  553.0 59.4 %collective-permute-start.43 = (bf16[1024,1024]{1,0:T(8,128)(2,1)}, bf16[1024,1024]{1,0:T(8,128)(2,1)}, u32[]{:S(2)}, u32[]{:S(2)}) collective-permute-start(bf16[1024,1024]{1,0:T(8,128)(2,1)} %add_convert_fusion.9), channel_id=1, source_target_pairs={{0,8},{10,2},{8,16},{18,10},{16,24},{26,18},{24,28},{30,26},{28,20... | collective-permute-start | bytes 6291464 | tf_op jit(solution)/shard_map/ppermute | solution.py:63
  591.7 43.9 %all-to-all-start = ((f32[16,2,1024]{2,1,0:T(2,128)}), f32[16,2,1024]{2,1,0:T(2,128)}, u32[]{:S(2)}, u32[]{:S(2)}) async-start(f32[16,2,1024]{2,1,0:T(2,128)} %broadcast_select_fusion.1), calls=%async_computation | async-start | bytes 262144 | tf_op jit(solution)/shard_map/all_to_all | solution.py:477
  595.9 210.8 %reduce-scatter.5.cloned.1.call-start = ((), (), s32[]{:S(2)}) async-start(), calls=%async_computation.6 | async-start | bytes 2228224 | tf_op jit(solution)/shard_map/reduce_scatter | solution.py:531
  655.0 61.0 %collective-permute-start.52 = (bf16[1024,1024]{1,0:T(8,128)(2,1)}, bf16[1024,1024]{1,0:T(8,128)(2,1)}, u32[]{:S(2)}, u32[]{:S(2)}) collective-permute-start(bf16[1024,1024]{1,0:T(8,128)(2,1)} %fusion.27), channel_id=1, source_target_pairs={{0,1},{1,0},{2,3},{3,2},{4,5},{5,4},{6,7},{7,6},{8,9},{9,8},{10,11... | collective-permute-start | bytes 6291464 | tf_op jit(solution)/shard_map/ppermute | solution.py:503
  656.4 61.3 %collective-permute-start.55 = (bf16[1024,1024]{1,0:T(8,128)(2,1)}, bf16[1024,1024]{1,0:T(8,128)(2,1)}, u32[]{:S(2)}, u32[]{:S(2)}) collective-permute-start(bf16[1024,1024]{1,0:T(8,128)(2,1)} %get-tuple-element.297), channel_id=1, source_target_pairs={{0,2},{2,0},{4,6},{6,4},{8,10},{10,8},{12,14},{14,12},{16,18},{18,... | collective-permute-start | bytes 6291464 | tf_op jit(solution)/shard_map/ppermute | solution.py:66
  689.2 98.9 %collective-permute-start.58 = (bf16[1024,1024]{1,0:T(8,128)(2,1)}, bf16[1024,1024]{1,0:T(8,128)(2,1)}, u32[]{:S(2)}, u32[]{:S(2)}) collective-permute-start(bf16[1024,1024]{1,0:T(8,128)(2,1)} %fusion.32), channel_id=1, source_target_pairs={{0,1},{1,0},{2,3},{3,2},{4,5},{5,4},{6,7},{7,6},{8,9},{9,8},{10,11... | collective-permute-start | bytes 6291464 | tf_op jit(solution)/shard_map/ppermute | solution.py:503
  690.6 73.4 %collective-permute-start.49 = (bf16[1024,1024]{1,0:T(8,128)(2,1)}, bf16[1024,1024]{1,0:T(8,128)(2,1)}, u32[]{:S(2)}, u32[]{:S(2)}) collective-permute-start(bf16[1024,1024]{1,0:T(8,128)(2,1)} %get-tuple-element.268), channel_id=1, source_target_pairs={{0,2},{2,0},{4,6},{6,4},{8,10},{10,8},{12,14},{14,12},{16,18},{18,... | collective-permute-start | bytes 6291464 | tf_op jit(solution)/shard_map/ppermute | solution.py:66
  690.7 222.5 %reduce-scatter.3.cloned.1.call-start = ((), (), s32[]{:S(2)}) async-start(), calls=%async_computation.5 | async-start | bytes 4456448 | tf_op jit(solution)/shard_map/reduce_scatter | solution.py:562
  716.0 78.8 %collective-permute-start.48 = (bf16[1024,1024]{1,0:T(8,128)(2,1)}, bf16[1024,1024]{1,0:T(8,128)(2,1)S(1)}, u32[]{:S(2)}, u32[]{:S(2)}) collective-permute-start(bf16[1024,1024]{1,0:T(8,128)(2,1)} %get-tuple-element.266), channel_id=1, source_target_pairs={{0,2},{2,0},{4,6},{6,4},{8,10},{10,8},{12,14},{14,12},{16,18},{18,... | collective-permute-start | bytes 6291464 | tf_op jit(solution)/shard_map/ppermute | solution.py:66
  717.6 96.8 %collective-permute-start.47 = (bf16[1024,1024]{1,0:T(8,128)(2,1)}, bf16[1024,1024]{1,0:T(8,128)(2,1)}, u32[]{:S(2)}, u32[]{:S(2)}) collective-permute-start(bf16[1024,1024]{1,0:T(8,128)(2,1)} %get-tuple-element.264), channel_id=1, source_target_pairs={{0,2},{2,0},{4,6},{6,4},{8,10},{10,8},{12,14},{14,12},{16,18},{18,... | collective-permute-start | bytes 6291464 | tf_op jit(solution)/shard_map/ppermute | solution.py:66
  809.6 64.5 %collective-permute-start.46 = (bf16[1024,1024]{1,0:T(8,128)(2,1)}, bf16[1024,1024]{1,0:T(8,128)(2,1)S(1)}, u32[]{:S(2)}, u32[]{:S(2)}) collective-permute-start(bf16[1024,1024]{1,0:T(8,128)(2,1)} %get-tuple-element.262), channel_id=1, source_target_pairs={{0,2},{2,0},{4,6},{6,4},{8,10},{10,8},{12,14},{14,12},{16,18},{18,... | collective-permute-start | bytes 6291464 | tf_op jit(solution)/shard_map/ppermute | solution.py:66
  809.6 112.1 %collective-permute-start.45 = (bf16[1024,1024]{1,0:T(8,128)(2,1)}, bf16[1024,1024]{1,0:T(8,128)(2,1)}, u32[]{:S(2)}, u32[]{:S(2)}) collective-permute-start(bf16[1024,1024]{1,0:T(8,128)(2,1)} %get-tuple-element.260), channel_id=1, source_target_pairs={{0,2},{2,0},{4,6},{6,4},{8,10},{10,8},{12,14},{14,12},{16,18},{18,... | collective-permute-start | bytes 6291464 | tf_op jit(solution)/shard_map/ppermute | solution.py:66
  813.6 60.5 %collective-permute-start.61 = (bf16[2,512,1024]{2,1,0:T(8,128)(2,1)}, bf16[2,512,1024]{2,1,0:T(8,128)(2,1)S(1)}, u32[]{:S(2)}, u32[]{:S(2)}) collective-permute-start(bf16[2,512,1024]{2,1,0:T(8,128)(2,1)} %convolution_convert_fusion.1), channel_id=1, source_target_pairs={{0,1},{1,0},{2,3},{3,2},{4,5},{5,4},{6,7},{7,6},{8,9},{9,8},{10,11... | collective-permute-start | bytes 6291464 | tf_op jit(solution)/shard_map/ppermute | solution.py:503
  828.0 46.2 %collective-permute-start.60 = (bf16[1024,1024]{1,0:T(8,128)(2,1)S(1)}, bf16[1024,1024]{1,0:T(8,128)(2,1)S(1)}, u32[]{:S(2)}, u32[]{:S(2)}) collective-permute-start(bf16[1024,1024]{1,0:T(8,128)(2,1)S(1)} %add_convert_fusion.2), channel_id=1, source_target_pairs={{0,8},{10,2},{8,16},{18,10},{16,24},{26,18},{24,28},{30,26},{28,20... | collective-permute-start | bytes 6291464 | tf_op jit(solution)/shard_map/ppermute | solution.py:63
  877.0 44.7 %collective-permute-start.62 = (bf16[1024,1024]{1,0:T(8,128)(2,1)}, bf16[1024,1024]{1,0:T(8,128)(2,1)}, u32[]{:S(2)}, u32[]{:S(2)}) collective-permute-start(bf16[1024,1024]{1,0:T(8,128)(2,1)} %add_convert_fusion.1), channel_id=1, source_target_pairs={{0,8},{10,2},{8,16},{18,10},{16,24},{26,18},{24,28},{30,26},{28,20... | collective-permute-start | bytes 6291464 | tf_op jit(solution)/shard_map/ppermute | solution.py:63
  (126 other events, 2254.4 us)
Sparse Core Ops, SparseCore 0:
  11.5 64.8 all-gather.2
  97.5 44.5 all-gather.4
  690.8 62.5 reduce-scatter.4
  806.8 88.0 reduce-scatter.2

commit v3 on v2

v3 whole, which is shorter than its diff:
```python
import functools

import jax
import jax.numpy as jnp
import numpy as np
from jax import lax
from jax.experimental import pallas as pl
from jax.experimental.pallas import tpu as pltpu
from jax.sharding import PartitionSpec as P

D = 1024
HEADS = 16
KV = 8
HD = 64
EXPERTS = 32
TOP = 8
CAP = 288
ABSENT = -100000


epsilon = 1e-06
masked_score = -1e30
rotary_base = 10000.0


def chip_cycle(count):
    if count % 4 == 0 and count >= 8:
        wide = count // 4
        tall = 4
    else:
        return list(range(count))
    if wide == 1:
        return list(range(count))
    order = [row * wide for row in range(tall)]
    for step, row in enumerate(reversed(range(tall))):
        columns = range(1, wide) if step % 2 == 0 else reversed(range(1, wide))
        order += [row * wide + column for column in columns]
    return order


class Ring:
    def __init__(self, shards, reps, layers):
        if layers > 1:
            wide = shards // (2 * layers)
            cells = [
                [(layer * wide + x, y) for y in range(reps) for x in (range(wide) if y % 2 == 0 else reversed(range(wide)))]
                for layer in range(layers)
            ]
        else:
            cells = [[(chip, rep) for chip in chip_cycle(shards // 2)] for rep in range(reps)]
        self.steps = len(cells[0])
        self.forward, self.swap = [], []

        def device(chip, core):
            return (2 * chip[0] + core) * reps + chip[1]

        for cell in cells:
            for place, here in enumerate(cell):
                there = cell[(place + 1) % len(cell)]
                self.forward += [
                    (device(here, 0), device(there, 0)),
                    (device(there, 1), device(here, 1)),
                ]
                self.swap += [(device(here, 0), device(here, 1)), (device(here, 1), device(here, 0))]

    def hop(self, array):
        return lax.ppermute(array, ("shard", "rep"), self.forward)

    def cross(self, array):
        return lax.ppermute(array, ("shard", "rep"), self.swap)

    def part_sum(self, near, far, *more):
        far = far[0] if len(far) == 1 else sum(part.astype(jnp.float32) for part in far)
        parts = [*near, self.cross(far.astype(jnp.bfloat16)), *more]
        return sum(part.astype(jnp.float32) for part in parts)


def rope_tables(tokens):
    halfway = HD // 2
    index_float = jnp.arange(halfway, dtype=jnp.float32)
    frequency = jnp.exp(-jnp.log(rotary_base) * index_float * 2.0 / HD)
    angle = jnp.arange(tokens, dtype=jnp.float32)[:, None] * frequency[None, :]
    cosine, sine = jnp.cos(angle), jnp.sin(angle)
    return (
        jnp.concatenate([cosine] * 4, axis=1),
        jnp.concatenate([-sine, sine, -sine, sine], axis=1),
    )


def dot(l,r): return jnp.dot(l,r,preferred_element_type=jnp.float32)
def dot_nt(l,r): return lax.dot_general(l,r,(((1,),(1,)),((),())),preferred_element_type=jnp.float32)
def dot_tn(l,r): return lax.dot_general(l,r,(((0,),(0,)),((),())),preferred_element_type=jnp.float32)

def swap_halves(values):
    parts=[]
    for start in range(0, values.shape[1], 128):
        part=values[:,start:start+128]
        lane=lax.broadcasted_iota(jnp.int32,part.shape,1)
        parts.append(jnp.where(lane % HD < HD//2, pltpu.roll(part,128-HD//2,1), pltpu.roll(part,HD//2,1)))
    return parts[0] if len(parts)==1 else jnp.concatenate(parts,axis=1)

def tile(table,width):
    return table if width==128 else jnp.concatenate([table]*(width//128),axis=1)

def forward_kernel(block, length_ref, normed_ref, wq_ref, wk_ref, wv_ref, cos_ref, sin_ref,
                   q_ref,k_ref,v_ref,out_ref,total_ref):
    tokens=normed_ref.shape[0]
    length=length_ref[0]
    cos,sin=cos_ref[...],sin_ref[...]
    bf16=jnp.bfloat16
    x=normed_ref[...]
    q=dot(x,wq_ref[...])
    q=q*tile(cos,q.shape[1])+swap_halves(q)*tile(sin,q.shape[1])
    q_ref[...]=(q.astype(bf16).astype(jnp.float32)*(HD**-0.5)).astype(bf16)
    k=dot(x,wk_ref[...])
    k_ref[...]=(k*cos+swap_halves(k)*sin).astype(bf16)
    v_ref[...]=dot(x,wv_ref[...]).astype(bf16)
    groups=HEADS//KV
    for head in range(2):
        for i in range(tokens//block):
            rows=slice(i*block,(i+1)*block)
            span=(i+1)*block
            keys=k_ref[:span,head*HD:(head+1)*HD]
            vals=v_ref[:span,head*HD:(head+1)*HD]
            qs=jnp.concatenate([q_ref[rows,(head*groups+h)*HD:(head*groups+h+1)*HD] for h in range(groups)],axis=0)
            s=dot_nt(keys,qs)
            key_place=lax.broadcasted_iota(jnp.int32,s.shape,0)
            query_place=lax.broadcasted_iota(jnp.int32,s.shape,1) % block + i*block
            s=jnp.where(key_place<=jnp.minimum(query_place,length-1),s,masked_score)
            top=jnp.max(s,axis=0,keepdims=True)
            p=jnp.exp(s-top)
            total=jnp.sum(p,axis=0,keepdims=True)
            p=(p*(1.0/total)).astype(bf16)
            o=dot_tn(p,vals)
            log_total=top+jnp.log(total)
            for h in range(groups):
                at=head*groups+h
                out_ref[rows,at*HD:(at+1)*HD]=o[h*block:(h+1)*block].astype(bf16)
                total_ref[0,at:at+1,rows]=log_total[:,h*block:(h+1)*block]

def attention_forward(length, normed, packed, cos, sin, part, block=256):
    tokens,width=normed.shape
    qw=HEADS*HD//4; kw=KV*HD//4
    bf16=jnp.bfloat16
    qb=HEADS*HD//kw; vb=(HEADS+KV)*HD//kw
    return pl.pallas_call(
        functools.partial(forward_kernel,block),
        out_shape=[jax.ShapeDtypeStruct((tokens,2*qw),bf16),jax.ShapeDtypeStruct((tokens,2*kw),bf16),jax.ShapeDtypeStruct((tokens,2*kw),bf16),
                   jax.ShapeDtypeStruct((tokens,2*qw),bf16),jax.ShapeDtypeStruct((2,HEADS//4,tokens),jnp.float32)],
        grid_spec=pltpu.PrefetchScalarGridSpec(num_scalar_prefetch=1,grid=(2,),
            in_specs=[pl.BlockSpec((tokens,width),lambda g,l:(0,0)),
                      pl.BlockSpec((width,qw),lambda g,l:(0,g+2*part)),
                      pl.BlockSpec((width,kw),lambda g,l:(0,qb+g+2*part)),
                      pl.BlockSpec((width,kw),lambda g,l:(0,vb+g+2*part)),
                      pl.BlockSpec((tokens,128),lambda g,l:(0,0)),pl.BlockSpec((tokens,128),lambda g,l:(0,0))],
            out_specs=[pl.BlockSpec((tokens,qw),lambda g,l:(0,g)),pl.BlockSpec((tokens,kw),lambda g,l:(0,g)),pl.BlockSpec((tokens,kw),lambda g,l:(0,g)),
                       pl.BlockSpec((tokens,qw),lambda g,l:(0,g)),pl.BlockSpec((1,HEADS//4,tokens),lambda g,l:(g,0,0))]),
        compiler_params=pltpu.CompilerParams(vmem_limit_bytes=40*1024*1024),
        cost_estimate=pl.CostEstimate(flops=30*10**9,bytes_accessed=20*1024*1024,transcendentals=0),
    )(length,normed,packed,packed,packed,cos,sin)

def backward_kernel(block,length_ref,q_ref,k_ref,v_ref,slope_ref,total_ref,cos_ref,sin_ref,dq_ref,dk_ref,dv_ref,dq_s,dk_s,dv_s):
    tokens=q_ref.shape[0]
    length=length_ref[0]
    bf16=jnp.bfloat16
    groups=HEADS//KV
    for head in range(2):
        lanes=slice(head*HD,(head+1)*HD)
        for i in reversed(range(tokens//block)):
            rows=slice(i*block,(i+1)*block)
            span=(i+1)*block
            keys=k_ref[:span,lanes]; vals=v_ref[:span,lanes]
            heads=[slice((head*groups+h)*HD,(head*groups+h+1)*HD) for h in range(groups)]
            qs=jnp.concatenate([q_ref[rows,at] for at in heads],axis=0)
            slopes=jnp.concatenate([slope_ref[rows,at] for at in heads],axis=0)
            log_total=jnp.concatenate([total_ref[0,head*groups+h:head*groups+h+1,rows] for h in range(groups)],axis=1)
            s=dot_nt(keys,qs)
            key_place=lax.broadcasted_iota(jnp.int32,s.shape,0)
            query_place=lax.broadcasted_iota(jnp.int32,s.shape,1) % block + i*block
            s=jnp.where(key_place<=jnp.minimum(query_place,length-1),s,masked_score)
            w=jnp.exp(s-log_total)
            ps=dot_nt(vals,slopes)
            centre=jnp.sum(w*ps,axis=0,keepdims=True)
            ds=(w*(ps-centre)).astype(bf16)
            dq=dot_tn(ds,keys)
            dk=dot(ds,qs)
            dv=dot(w.astype(bf16),slopes)
            for h in range(groups):
                dq_s[rows,heads[h]]=dq[h*block:(h+1)*block]*(HD**-0.5)
            if i==tokens//block-1:
                dk_s[:,lanes]=dk; dv_s[:,lanes]=dv
            else:
                dk_s[:span,lanes]+=dk; dv_s[:span,lanes]+=dv
    cos,sin=cos_ref[...],sin_ref[...]
    dq=dq_s[...]
    dq_ref[...]=(dq*tile(cos,dq.shape[1])-swap_halves(dq)*tile(sin,dq.shape[1])).astype(bf16)
    dk=dk_s[...]
    dk_ref[...]=(dk*cos-swap_halves(dk)*sin).astype(bf16)
    dv_ref[...]=dv_s[...].astype(bf16)

def attention_backward(length,q,k,v,slope,total,cos,sin,part,block=256):
    tokens=q.shape[0]
    qw=HEADS*HD//4; kw=KV*HD//4
    bf16=jnp.bfloat16
    qs=pl.BlockSpec((tokens,qw),lambda g,l:(0,g)); ks=pl.BlockSpec((tokens,kw),lambda g,l:(0,g)); cs=pl.BlockSpec((tokens,128),lambda g,l:(0,0))
    return pl.pallas_call(
        functools.partial(backward_kernel,block),
        out_shape=[jax.ShapeDtypeStruct((tokens,2*qw),bf16),jax.ShapeDtypeStruct((tokens,2*kw),bf16),jax.ShapeDtypeStruct((tokens,2*kw),bf16)],
        grid_spec=pltpu.PrefetchScalarGridSpec(num_scalar_prefetch=1,grid=(2,),
            in_specs=[qs,ks,ks,pl.BlockSpec((tokens,qw),lambda g,l:(0,g+2*part)),pl.BlockSpec((1,HEADS//4,tokens),lambda g,l:(g,0,0)),cs,cs],
            out_specs=[qs,ks,ks],
            scratch_shapes=[pltpu.VMEM((tokens,qw),jnp.float32),pltpu.VMEM((tokens,kw),jnp.float32),pltpu.VMEM((tokens,kw),jnp.float32)]),
        compiler_params=pltpu.CompilerParams(vmem_limit_bytes=40*1024*1024),
        cost_estimate=pl.CostEstimate(flops=20*10**9,bytes_accessed=10*1024*1024,transcendentals=0),
    )(length,q,k,v,slope,total,cos,sin)

def pair_kernel(
    count,
    step,
    chained,
    ids_ref,
    tokens_a,
    tokens_b,
    slope_a,
    slope_b,
    row_a,
    row_b,
    mask_a,
    mask_b,
    router_ref,
    *rest,
):
    weights, rest = rest[: 3 * count], rest[3 * count :]
    rest = rest[4:] if chained else rest
    back_out, mix_out, kept_out, rest = rest[0:2], rest[2:4], rest[4:8], rest[8:]
    blocks, backs, mixes, gates_in, ups_in, downs_in, rest = *rest[:6], rest[6:]
    rows_buf, routed_buf, hidden_buf, slopes_buf, raw_buf, mixed_rows, back_rows, rest = (
        *rest[:7],
        rest[7:],
    )
    load_sems, weight_sems, back_sems, mix_sems, kept_sems = rest
    tokens = blocks.shape[1]
    pair_rows = 2 * CAP
    bf16, f32 = jnp.bfloat16, jnp.float32
    sources = (tokens_a, slope_a, tokens_b, slope_b)

    def load(which):
        return pltpu.make_async_copy(
            sources[which].at[pl.ds(0, tokens)], blocks.at[which], load_sems.at[which]
        )

    def load_weight(e, which):
        target = (gates_in, ups_in, downs_in)[which].at[e]
        return pltpu.make_async_copy(weights[3 * e + which], target, weight_sems.at[e, which])

    stores = []

    def store(source, target, sem):
        stores.append(pltpu.make_async_copy(source, target, sem))
        stores[-1].start()

    def keep(e, which):
        source = (rows_buf, routed_buf, hidden_buf, slopes_buf)[which].at[e]
        target = kept_out[which].at[e, pl.ds(step * pair_rows, pair_rows)]
        store(source, target, kept_sems.at[e, which])

    for which in (0, 2, 1, 3):
        load(which).start()
    for e in range(count):
        for which in range(3):
            load_weight(e, which).start()

    taken, picks, chosen = [], [], []
    for side, (row_ref, mask_ref) in enumerate(((row_a, mask_a), (row_b, mask_b))):
        place = lax.broadcasted_iota(jnp.int32, (CAP, tokens), 0)
        taken.append([row_ref[0, e : e + 1] == place for e in range(count)])
        hits = [jnp.where(hit, 1.0, 0.0).astype(bf16) for hit in taken[side]]
        picks.append(hits[0] if count == 1 else jnp.concatenate(hits, axis=0))
        chosen.append(dot_nt(picks[side], mask_ref[...]))
        load(2 * side).wait()
        rows = dot(picks[side], blocks[2 * side]).astype(bf16)
        for e in range(count):
            rows_buf[e, side * CAP : (side + 1) * CAP] = rows[e * CAP : (e + 1) * CAP]
    for e in range(count):
        keep(e, 0)
    for side in range(2):
        load(2 * side + 1).wait()
        rows = dot(picks[side], blocks[2 * side + 1]).astype(bf16)
        for e in range(count):
            raw_buf[e, side * CAP : (side + 1) * CAP] = rows[e * CAP : (e + 1) * CAP]
    homeward = [[], []]
    for e in range(count):
        rows = rows_buf[e]
        marks = jnp.concatenate([chosen[side][e * CAP : (e + 1) * CAP] for side in range(2)], axis=0)
        logits = dot(rows, router_ref[...])
        kept = jnp.where(marks > 0.5, logits, masked_score)
        top = jnp.max(kept, axis=-1, keepdims=True)
        powered = jnp.exp(kept - top) * marks
        total = jnp.sum(powered, axis=-1, keepdims=True)
        lane = lax.broadcasted_iota(jnp.int32, powered.shape, 1)
        mine = lane == ids_ref[e]
        gate = jnp.sum(jnp.where(mine, powered, 0.0), axis=-1, keepdims=True) / jnp.where(
            total > 0.0, total, 1.0
        )
        slope_rows = raw_buf[e].astype(f32)
        routed = (gate * slope_rows).astype(bf16)
        routed_buf[e] = routed
        keep(e, 1)
        for which in range(3):
            load_weight(e, which).wait()
        gate_part = dot(rows, gates_in[e])
        up_part = dot(rows, ups_in[e])
        hidden_slope = dot_nt(routed, downs_in[e])
        sigma = 1.0 / (1.0 + jnp.exp(-gate_part))
        silu = gate_part * sigma
        hidden = (silu * up_part).astype(bf16)
        hidden_buf[e] = hidden
        keep(e, 2)
        gate_back = (hidden_slope * up_part * sigma * (1.0 + gate_part * (1.0 - sigma))).astype(bf16)
        up_back = (hidden_slope * silu).astype(bf16)
        half = gate_back.shape[1]
        slopes_buf[e, :, :half] = gate_back
        slopes_buf[e, :, half:] = up_back
        keep(e, 3)
        out = dot(hidden, downs_in[e]).astype(bf16).astype(f32)
        back = (dot_nt(gate_back, gates_in[e]) + dot_nt(up_back, ups_in[e])).astype(bf16)
        gate_slope = jnp.sum(out * slope_rows, axis=-1, keepdims=True)
        mixed = (gate * out).astype(bf16)
        for side in range(2):
            part = slice(side * CAP, (side + 1) * CAP)
            homeward[side].append(
                jnp.sum(jnp.where(taken[side][e], gate_slope[part], 0.0), axis=0, keepdims=True)
            )
            mixed_rows[side, e * CAP : (e + 1) * CAP] = mixed[part]
            back_rows[side, e * CAP : (e + 1) * CAP] = back[part]
    for side, row_ref in enumerate((row_a, row_b)):
        backs[side, :tokens] = dot_tn(picks[side], back_rows[side]).astype(bf16)
        row = lax.broadcasted_iota(jnp.int32, (EXPERTS, tokens), 0)
        whole = jnp.zeros(row.shape, f32)
        for e in range(count):
            whole = jnp.where(row == ids_ref[e], homeward[side][e], whole)
        high = whole.astype(bf16)
        backs[side, tokens : tokens + EXPERTS] = high
        backs[side, tokens + EXPERTS :] = (whole - high.astype(f32)).astype(bf16)
        store(backs.at[side], back_out[side], back_sems.at[side])
        mixes[side] = dot_tn(picks[side], mixed_rows[side]).astype(bf16)
        store(mixes.at[side], mix_out[side], mix_sems.at[side])
    for copy in stores:
        copy.wait()


def experts_pair(step, steps, expert_ids, ta, tb, sa, sb, slots, weights, kept):
    router, *weights = weights
    tokens, width = ta.shape
    count, half = len(weights) // 3, weights[2].shape[0]
    bf16 = jnp.bfloat16
    chained = kept is not None
    once = pl.Buffered(1)
    back_rows = tokens + 2 * EXPERTS

    def block(rows, at=0):
        return pl.BlockSpec((rows, width), lambda e, w: (at, 0), pipeline_mode=once)

    anywhere = pl.BlockSpec(memory_space=pl.ANY)
    in_specs = [anywhere] * 4
    in_specs += [
        pl.BlockSpec((1, count, tokens), lambda e, w, i=i: (2 * step + i, 0, 0), pipeline_mode=once)
        for i in range(2)
    ]
    in_specs += [block(EXPERTS, tokens // EXPERTS)] * 2
    in_specs += [pl.BlockSpec((width, EXPERTS), lambda e, w: (0, 0), pipeline_mode=once)]
    in_specs += [anywhere] * len(weights)
    rows = 2 * CAP
    columns = (width, width, half, 2 * half)
    shapes = [jax.ShapeDtypeStruct((back_rows, width), bf16)] * 2
    shapes += [jax.ShapeDtypeStruct((tokens, width), bf16)] * 2
    shapes += [jax.ShapeDtypeStruct((count, steps * rows, column), bf16) for column in columns]
    out_specs = [anywhere] * 8
    operands = [ta, tb, sa, sb, slots, slots, sa, sb, router, *weights]
    aliases = {}
    if chained:
        first = 1 + len(operands)
        operands += list(kept)
        in_specs += [anywhere] * 4
        aliases = {first + p: 4 + p for p in range(4)}
    flops = count * 2 * rows * (4 * tokens * width + 6 * width * half)
    return pl.pallas_call(
        functools.partial(pair_kernel, count, step, chained),
        out_shape=shapes,
        grid_spec=pltpu.PrefetchScalarGridSpec(
            num_scalar_prefetch=1,
            grid=(1,),
            in_specs=in_specs,
            out_specs=out_specs,
            scratch_shapes=[
                pltpu.VMEM((4, tokens, width), bf16),
                pltpu.VMEM((2, back_rows, width), bf16),
                pltpu.VMEM((2, tokens, width), bf16),
                pltpu.VMEM((count, width, half), bf16),
                pltpu.VMEM((count, width, half), bf16),
                pltpu.VMEM((count, half, width), bf16),
                *[pltpu.VMEM((count, rows, column), bf16) for column in columns],
                pltpu.VMEM((count, rows, width), bf16),
                pltpu.VMEM((2, count * CAP, width), bf16),
                pltpu.VMEM((2, count * CAP, width), bf16),
                pltpu.SemaphoreType.DMA((4,)),
                pltpu.SemaphoreType.DMA((count, 3)),
                pltpu.SemaphoreType.DMA((2,)),
                pltpu.SemaphoreType.DMA((2,)),
                pltpu.SemaphoreType.DMA((count, 4)),
            ],
        ),
        input_output_aliases=aliases,
        compiler_params=pltpu.CompilerParams(vmem_limit_bytes=60 * 1024 * 1024),
        cost_estimate=pl.CostEstimate(
            flops=2 * flops, bytes_accessed=40 * 1024 * 1024, transcendentals=0
        ),
    )(expert_ids, *operands)


def on_device(
    shards,
    reps,
    layer_input,
    attention_gain,
    query_weight,
    key_weight,
    value_weight,
    output_weight,
    expert_gain,
    router_weight,
    gate_weight,
    up_weight,
    down_weight,
    lengths,
    routes,
    cotangent,
):
    me, rep = lax.axis_index("shard"), lax.axis_index("rep")
    tokens = layer_input.shape[0]
    local_experts, half = down_weight.shape[0], down_weight.shape[1]
    length = lengths[0]
    bf16, f32 = jnp.bfloat16, jnp.float32
    heads_width = (HEADS + 2 * KV) * HD
    layers = 4 if (shards == 16 and reps == 2 and local_experts == 2) else 1
    layered = layers > 1
    ring = Ring(shards, reps, layers)
    barrier = lax.optimization_barrier

    packed = jnp.concatenate([query_weight, key_weight, value_weight], axis=1)
    packed_full = lax.all_gather(packed, "shard", axis=0, tiled=True)
    packed_full, output_weight = barrier((packed_full, output_weight))
    output_full = lax.all_gather(output_weight, "shard", axis=0, tiled=True)

    def layer_swap(array, bit):
        stride = bit * (shards // layers)
        return lax.ppermute(array, "shard", [(s, s ^ stride) for s in range(shards)])

    if layered:
        own = [
            lax.dynamic_index_in_dim(weight, rep, axis=0, keepdims=False)
            for weight in (gate_weight, up_weight, down_weight)
        ]

        def owned(bits):
            return 2 * (me ^ (bits * (shards // layers))) + rep

        half_ids = [
            jnp.stack([owned(0), owned(1)]).astype(jnp.int32),
            jnp.stack([owned(2), owned(3)]).astype(jnp.int32),
        ]
    else:
        half_ids = [(me * local_experts + jnp.arange(local_experts)).astype(jnp.int32)]

    expert_ids = jnp.arange(EXPERTS, dtype=jnp.int32)
    routes_turned = routes.T
    picks = functools.reduce(
        jnp.logical_or, [routes_turned[k][None, :] == expert_ids[:, None] for k in range(TOP)]
    )
    valid = (jnp.arange(tokens, dtype=jnp.int32) < length)[:, None]
    slope_low = jnp.where(valid, cotangent, jnp.zeros_like(cotangent))
    slope = slope_low.astype(f32)
    slope_near = [jnp.concatenate([slope_low, picks.astype(bf16)], axis=0)]

    def slope_hop(*tie):
        if len(slope_near) == ring.steps:
            return tie
        arrived = ring.hop(slope_near[-1])
        arrived, *tie = barrier((arrived, *tie))
        slope_near.append(arrived)
        return tie

    inputs_f = layer_input.astype(f32)
    first_scale = lax.rsqrt(jnp.mean(inputs_f * inputs_f, axis=-1, keepdims=True) + epsilon)
    base_one = inputs_f * first_scale
    normed_one = (base_one * attention_gain).astype(bf16)
    cosine, sine = rope_tables(tokens)
    (normed_one,) = slope_hop(normed_one)
    normed_one, packed_full = slope_hop(normed_one, packed_full)
    if layered:
        packed_full, own = barrier((packed_full, own))
        next_one = [layer_swap(own[0], 1)]
        across_two = [layer_swap(own[0], 2)]
    heads = []
    for part in range(2):
        result = attention_forward(lengths, normed_one, packed_full, cosine, sine, part)
        if part == 0:
            result, packed_full = slope_hop(result, packed_full)
            if layered:
                result, packed_full, own, next_one[0] = barrier(
                    (result, packed_full, own, next_one[0])
                )
                next_one.append(layer_swap(own[1], 1))
        elif layered:
            result, own, next_one[1], across_two[0] = barrier(
                (result, own, next_one[1], across_two[0])
            )
            next_one.append(layer_swap(own[2], 1))
            across_two.append(layer_swap(own[1], 2))
        heads.append(result)
    attended = jnp.concatenate([heads[part][3] for part in range(2)], axis=1)
    residual = inputs_f + dot(attended, output_full)
    second_scale = lax.rsqrt(jnp.mean(residual * residual, axis=-1, keepdims=True) + epsilon)
    base_two = residual * second_scale
    normed_two = (base_two * expert_gain).astype(bf16)

    across_three = []
    if layered:
        normed_two, next_one[2], across_two[0], own = barrier(
            (normed_two, next_one[2], across_two[0], own)
        )
        across_two.append(layer_swap(own[2], 2))
        across_three.append(layer_swap(across_two[0], 1))

    near = [normed_two]
    while len(near) < ring.steps:
        near.append(ring.hop(near[-1]))
        if len(slope_near) < ring.steps:
            near[-1], *_ = slope_hop(near[-1])
    far = [ring.cross(block) for block in near]
    slope_far = [ring.cross(block) for block in slope_near]

    masks = jnp.stack(
        [block[tokens:] for step in range(ring.steps) for block in (slope_near[step], slope_far[step])]
    )
    earlier = jnp.triu(jnp.ones((tokens, tokens), bf16), k=1)
    all_ids = jnp.concatenate(half_ids)
    mine = jnp.take(masks.astype(f32), all_ids, axis=1, mode="clip")
    ranks = dot(mine.reshape(-1, tokens).astype(bf16), earlier).astype(jnp.int32).reshape(mine.shape)
    slots = jnp.where(mine > 0.5, ranks, ABSENT)
    count = half_ids[0].shape[0]
    half_slots = [slots[:, h * count : (h + 1) * count] for h in range(len(half_ids))]

    if layered:
        order = [(0, step) for step in range(1, ring.steps)]
        order += [(1, step % ring.steps) for step in range(1, ring.steps + 1)] + [(0, 0)]
    else:
        half_weights = [
            [w[e] for e in range(local_experts) for w in (gate_weight, up_weight, down_weight)]
        ]
        order = [(0, step) for step in range(ring.steps)]

    def expert_grads(kept):
        rows, routed, hidden, slopes = kept
        turned = (((0,), (0,)), ((), ()))
        return [
            (
                lax.dot_general(rows[e], slopes[e], turned, preferred_element_type=f32).astype(bf16),
                lax.dot_general(hidden[e], routed[e], turned, preferred_element_type=f32).astype(bf16),
            )
            for e in range(count)
        ]

    def thirds(pair):
        middle = pair[0].shape[0] // 2
        return [pair[0][:middle], pair[0][middle:], pair[1]]

    def to_owner(which):
        both = far_grads[0][which].astype(f32) + three_sum[which].astype(f32)
        return layer_swap(both.astype(bf16), 2)

    def across(array):
        return lax.ppermute(array, "rep", [(0, 1), (1, 0)])

    def finish(which):
        parts = (near_grads[0][which], two_sum[which], next_sum[which])
        sums.append(sum(g.astype(f32) for g in parts).astype(bf16))
        others.append(across(sums[-1]))

    three_sum, next_sum, two_sum, sums, others = [], [], [], [], []
    kept = [None] * len(half_ids)
    back_parts = [([], []) for _ in range(ring.steps)]
    mix_parts = [([], []) for _ in range(ring.steps)]
    total, next_step, last = None, 1, None
    for turn, (which, step) in enumerate(order):
        tokens_now = near[step]
        if last is not None:
            tokens_now, last = barrier((tokens_now, last))
        if layered:
            now = [*own, *next_one] if which == 0 else [*across_two, *across_three]
        else:
            now = half_weights[0]
        results = experts_pair(
            step,
            ring.steps,
            half_ids[which],
            tokens_now,
            far[step],
            slope_near[step],
            slope_far[step],
            half_slots[which],
            (router_weight, *now),
            kept[which],
        )
        kept[which] = results[4:8]
        for side in range(2):
            back_parts[step][side].append(results[side])
            mix_parts[step][side].append(results[2 + side])
        last = results[2]
        if layered and turn == 0:
            last, across_two[1], across_three[0] = barrier((last, across_two[1], across_three[0]))
            across_three.append(layer_swap(across_two[1], 1))
        elif layered and turn == 1:
            last, across_two[2], across_three[1] = barrier((last, across_two[2], across_three[1]))
            across_three.append(layer_swap(across_two[2], 1))
        if layered and (which, step) == (1, 0):
            far_grads = [thirds(pair) for pair in expert_grads(kept[1])]
            last, far_grads = barrier((last, far_grads))
            three_sum.append(layer_swap(far_grads[1][0], 1))
        elif layered and (which, step) == (0, 0):
            last, kept[0], three_sum[0] = barrier((last, kept[0], three_sum[0]))
            two_sum.append(to_owner(0))
            three_sum += [layer_swap(far_grads[1][at], 1) for at in (1, 2)]
        mix_parts[step][0][-1] = last
        while next_step < ring.steps and len(back_parts[next_step][0]) == len(half_ids):
            more = () if total is None else (total,)
            total = ring.hop(ring.part_sum(*back_parts[next_step], *more).astype(bf16))
            next_step += 1

    if layered:
        near_grads = [thirds(pair) for pair in expert_grads(kept[0])]
        total, near_grads, three_sum[1], three_sum[2] = barrier(
            (total, near_grads, three_sum[1], three_sum[2])
        )
        two_sum += [to_owner(1), to_owner(2)]
        next_sum += [layer_swap(near_grads[1][which], 1) for which in range(3)]
        back = ring.part_sum(*back_parts[0], total)
    else:
        back = ring.part_sum(*back_parts[0], total)
        whole_grads = expert_grads(kept[0])
        back, whole_grads = barrier((back, whole_grads))
    normed_slope = back[:tokens]
    gate_slope = back[tokens : tokens + EXPERTS] + back[tokens + EXPERTS :]

    logits = lax.dot_general(
        router_weight, normed_two, (((0,), (1,)), ((), ())), preferred_element_type=f32
    )
    kept_logits = jnp.where(picks, logits, masked_score)
    powered = jnp.where(
        picks, jnp.exp(kept_logits - jnp.max(kept_logits, axis=0, keepdims=True)), 0.0
    )
    gates = powered / jnp.sum(powered, axis=0, keepdims=True)
    mean_slope = jnp.sum(gates * gate_slope, axis=0, keepdims=True)
    logit_slope = (gates * (gate_slope - mean_slope)).astype(bf16)
    router_grad = dot(logit_slope, normed_two)
    normed_slope = normed_slope + lax.dot_general(
        logit_slope, router_weight, (((0,), (1,)), ((), ())), preferred_element_type=f32
    )

    def mix_hop(step, total):
        more = () if total is None else (total,)
        return ring.hop(ring.part_sum(*mix_parts[step], *more).astype(bf16))

    expert_gain_grad = jnp.sum(normed_slope * base_two, axis=0)
    scaled_two = normed_slope * expert_gain
    residual_slope = (
        slope
        + second_scale * scaled_two
        - base_two
        * second_scale
        * second_scale
        * jnp.mean(scaled_two * residual, axis=-1, keepdims=True)
    )
    branch_slope = residual_slope.astype(bf16)
    output_grad = lax.dot_general(
        attended, branch_slope, (((0,), (0,)), ((), ())), preferred_element_type=f32
    ).astype(bf16)
    attended_slope = jnp.einsum(
        "sd,cd->sc", branch_slope, output_full, preferred_element_type=f32
    ).astype(bf16)
    output_owned = lax.psum_scatter(output_grad, "shard", scatter_dimension=0, tiled=True)

    attended_slope, mix_parts = barrier((attended_slope, mix_parts))
    mix = mix_hop(1, None)
    slopes_out = []
    mix_step = 2
    for part in range(2):
        if part > 0:
            attended_slope, mix = barrier((attended_slope, mix))
            if mix_step < ring.steps:
                mix = mix_hop(mix_step, mix)
                mix_step += 1
        if layered:
            attended_slope, next_sum[part] = barrier((attended_slope, next_sum[part]))
            if part == 1:
                attended_slope, two_sum[0] = barrier((attended_slope, two_sum[0]))
                finish(0)
        queries, keys, values, _, log_totals = heads[part]
        slopes_out.append(
            attention_backward(
                lengths, queries, keys, values, attended_slope, log_totals, cosine, sine, part
            )
        )
        if part == 0:
            attended_slope, slopes_out[0] = barrier((attended_slope, slopes_out[0]))
    pre_slopes = jnp.concatenate(
        [slopes_out[part][which] for which in range(3) for part in range(2)], axis=1
    )
    pre_slopes, mix = barrier((pre_slopes, mix))
    if layered:
        pre_slopes, next_sum[2] = barrier((pre_slopes, next_sum[2]))
    while mix_step < ring.steps:
        mix = mix_hop(mix_step, mix)
        mix_step += 1
    input_grad = lax.dot_general(
        normed_one, pre_slopes, (((0,), (0,)), ((), ())), preferred_element_type=f32
    ).astype(bf16)
    input_owned = lax.psum_scatter(input_grad, "shard", scatter_dimension=0, tiled=True)
    normed_one_slope = jnp.einsum(
        "sc,dc->sd", pre_slopes, packed_full, preferred_element_type=f32
    )
    attention_gain_grad = jnp.sum(normed_one_slope * base_one, axis=0)
    gain_sum = jnp.concatenate(
        [attention_gain_grad[None], expert_gain_grad[None], router_grad], axis=0
    )
    for axis, size in (("rep", reps), ("shard", shards)):
        far_bit = 1
        while far_bit < size:
            gain_sum = gain_sum + lax.ppermute(
                gain_sum, axis, [(place, place ^ far_bit) for place in range(size)]
            )
            far_bit *= 2
    scaled_one = normed_one_slope * attention_gain
    input_slope = (
        residual_slope
        + first_scale * scaled_one
        - base_one
        * first_scale
        * first_scale
        * jnp.mean(scaled_one * inputs_f, axis=-1, keepdims=True)
    )
    input_gradient = input_slope.astype(bf16)
    if layered:
        input_gradient, two_sum[1] = barrier((input_gradient, two_sum[1]))
        finish(1)
        gain_sum, two_sum[2] = barrier((gain_sum, two_sum[2]))
        finish(2)
    layer_output = (residual + ring.part_sum(*mix_parts[0], mix)).astype(bf16)

    def rep_sum(*arrays):
        if reps != 2:
            return lax.psum(tuple(array.astype(f32) for array in arrays), "rep")
        low = [array.astype(bf16) for array in arrays]
        return tuple(a.astype(f32) + across(a).astype(f32) for a in low)

    if layered:
        whole = [
            jnp.stack([jnp.where(rep == 0, a, b), jnp.where(rep == 0, b, a)])
            for a, b in zip([x.astype(f32) for x in sums], [x.astype(f32) for x in others])
        ]
        in_sum, down_sum = jnp.concatenate(whole[:2], axis=1), whole[2]
    else:
        in_sum, down_sum = rep_sum(
            jnp.stack([g[0] for g in whole_grads]), jnp.stack([g[1] for g in whole_grads])
        )
    gain_sum, output_owned, input_owned = barrier((gain_sum, output_owned, input_owned))
    output_sum, input_sum = rep_sum(output_owned, input_owned)
    return (
        layer_output,
        input_gradient,
        gain_sum[0],
        input_sum[:, : HEADS * HD],
        input_sum[:, HEADS * HD : (HEADS + KV) * HD],
        input_sum[:, (HEADS + KV) * HD :],
        output_sum,
        gain_sum[1],
        gain_sum[2:].T,
        in_sum[..., :half],
        in_sum[..., half:],
        down_sum,
    )


def solution(mesh):
    return jax.shard_map(
        functools.partial(on_device, mesh.shape["shard"], mesh.shape["rep"]),
        mesh=mesh,
        in_specs=(
            P(("shard", "rep"), None),
            P(),
            P("shard", None),
            P("shard", None),
            P("shard", None),
            P("shard", None),
            P(),
            P(),
            P("shard", None, None),
            P("shard", None, None),
            P("shard", None, None),
            P(("shard", "rep")),
            P(("shard", "rep"), None),
            P(("shard", "rep"), None),
        ),
        out_specs=(
            P(("shard", "rep"), None),
            P(("shard", "rep"), None),
            P(),
            P("shard", None),
            P("shard", None),
            P("shard", None),
            P("shard", None),
            P(),
            P(),
            P("shard", None, None),
            P("shard", None, None),
            P("shard", None, None),
        ),
        check_vma=False,
    )
```

time: 944 us -> 901 us (0.954)
  Pallas kernels: 342 us -> 311 us
  waiting for transfers between devices: 256 us -> 286 us
  other arithmetic: 119 us -> 94.9 us
  starting transfers between devices: 72.7 us -> 50.5 us
    pallas_call x8, Pallas kernels: 263 us -> 232 us  [experts_pair(): pl.pallas_call(functools.partial(pair_kernel, count, step, chained), out_...]
    ppermute x5, waiting for transfers between devices: 1.8 us -> 26 us  [across(): return lax.ppermute(array, 'rep', [(0, 1), (1, 0)])]
    another operation x11 -> x6, other arithmetic: 24.7 us -> 6.47 us  [the longest x4 5.26 us: on_device(): jnp.stack([jnp.where(rep == 0, a, b), jnp.where(rep == 0, b, a)])]
    ppermute x60 -> x46, starting transfers between devices: 57 us -> 42.2 us  [the longest x12 19.9 us: hop(): return lax.ppermute(array, ('shard', 'rep'), self.forward)]
    ppermute x60 -> x46, waiting for transfers between devices: 194 us -> 180 us  [the longest x12 94.1 us: hop(): return lax.ppermute(array, ('shard', 'rep'), self.forward)]
    ppermute x5, waiting for transfers between devices: 58.4 us -> 71.6 us  [on_device(): lax.ppermute(gain_sum, axis, [(place, place ^ far_bit) for place in range...]
    convert_element_type x16 -> x23, other arithmetic: 60.6 us -> 63.8 us  [the longest x8 20.9 us: part_sum(): parts = [*near, self.cross(far.astype(jnp.bfloat16)), *more]]
    dot_general x4 -> x9, matrix products: 58.4 us -> 61.5 us  [the longest x4 33.4 us: expert_grads(): lax.dot_general(rows[e], slopes[e], turned, preferred_element_type=f32)]
  transfers between devices with their start and end apart: 75 -> 60, of which waited for: 25 -> 23; matrix products, arithmetic and copies ran while one was open for 23% -> 22% of each run, Pallas kernels for 37% -> 31%
where the time goes in v3:
time: 901 us; the launch traced here: 895 us
  Pallas kernels  311 us (35%)
  waiting for transfers between devices  286 us (32%)
  other arithmetic  94.9 us (11%)
  matrix products  89.6 us (10%)
  starting transfers between devices  50.5 us (6%)
  local copies, waits for them, and re-layouts  46.9 us (5%)
  between operations  16.3 us (2%)
    pallas_call x8, Pallas kernels, experts_pair(): pl.pallas_call(functools.partial(pair_kernel, count, step, chained), out_...  232 us
    ppermute x12, waiting for transfers between devices, hop(): return lax.ppermute(array, ('shard', 'rep'), self.forward)  94.1 us
    ppermute x18, waiting for transfers between devices, layer_swap(): lax.ppermute(array, 'shard', [(s, s ^ stride) for s in range(shards)])  85.7 us
    ppermute x5, waiting for transfers between devices, on_device(): lax.ppermute(gain_sum, axis, [(place, place ^ far_bit) for place in range...  71.6 us
    pallas_call x2, Pallas kernels, attention_backward(): pl.pallas_call(functools.partial(backward_kernel, block), out_shape=[jax....  40.1 us
    pallas_call x2, Pallas kernels, attention_forward(): pl.pallas_call(functools.partial(forward_kernel, block), out_shape=[jax.S...  38.9 us
    dot_general x4, matrix products, expert_grads(): lax.dot_general(rows[e], slopes[e], turned, preferred_element_type=f32)  33.4 us
    ppermute x5, waiting for transfers between devices, across(): return lax.ppermute(array, 'rep', [(0, 1), (1, 0)])  26 us
  transfers between devices with their start and end apart: 60, of which 23 were waited for; matrix products, arithmetic and copies ran while one was open for 22% of the time, Pallas kernels for 31%

profile of v3, /device:TPU:0, one launch (start us, length us, event | category | flops | bytes accessed | tf_op | source)
XLA Modules:
  0.0 895.1 jit_solution(5553872462447159039)
XLA Ops:
  19.9 32.2 %collective-permute-done.slope_a.mask_a = bf16[1056,1024]{1,0:T(8,128)(2,1)} collective-permute-done((bf16[1056,1024]{1,0:T(8,128)(2,1)}, bf16[1056,1024]{1,0:T(8,128)(2,1)}, u32[]{:S(2)}, u32[]{:S(2)}) %collective-permute-start) | collective-permute-done | bytes 2162720 | tf_op jit(solution)/shard_map/ppermute | solution.py:67
  60.7 8.7 all-gather.3.cloned.1.call-done.wq_ref.wk_ref.wv_ref
  69.4 10.0 %collective-permute-done.1.slope_a.mask_a = bf16[1056,1024]{1,0:T(8,128)(2,1)} collective-permute-done((bf16[1056,1024]{1,0:T(8,128)(2,1)}, bf16[1056,1024]{1,0:T(8,128)(2,1)}, u32[]{:S(2)}, u32[]{:S(2)}) %collective-permute-start.1) | collective-permute-done | bytes 2162720 | tf_op jit(solution)/shard_map/ppermute | solution.py:67
  88.6 19.2 %shard_map.229 = (bf16[1024,512]{1,0:T(8,128)(2,1)S(1)}, bf16[1024,256]{1,0:T(8,128)(2,1)S(1)}, bf16[1024,256]{1,0:T(8,128)(2,1)S(1)}, bf16[1024,512]{1,0:T(8,128)(2,1)S(1)}, f32[2,4,1024]{2,1,0:T(4,128)S(1)}) custom-call(s32[1]{0:T(128)} %copy.137.length_ref, bf16[1024,1024]{1,0:T(8,128)(2,1)S(1)} %copy-done.2, bf16[1024,2048]{1,0:T(8,128)(2,1)S(1)} %copy-done.3, ...), custom_call_target="tpu_custom_call" | custom-call | flops 30000001024 | bytes 20971520 | tf_op jit(solution)/shard_map/pallas_call | solution.py:146
  112.0 18.9 %collective-permute-done.3.rest_3_ = bf16[1024,512]{1,0:T(8,128)(2,1)} collective-permute-done((bf16[1024,512]{1,0:T(8,128)(2,1)}, bf16[1024,512]{1,0:T(8,128)(2,1)}, u32[]{:S(2)}, u32[]{:S(2)}) %collective-permute-start.3) | collective-permute-done | bytes 1048608 | tf_op jit(solution)/shard_map/ppermute | solution.py:457
  130.8 19.8 %shard_map.230 = (bf16[1024,512]{1,0:T(8,128)(2,1)S(1)}, bf16[1024,256]{1,0:T(8,128)(2,1)S(1)}, bf16[1024,256]{1,0:T(8,128)(2,1)S(1)}, bf16[1024,512]{1,0:T(8,128)(2,1)S(1)}, f32[2,4,1024]{2,1,0:T(4,128)S(1)}) custom-call(s32[1]{0:T(128)} %copy.137.length_ref, bf16[1024,1024]{1,0:T(8,128)(2,1)S(1)} %copy-done.2, bf16[1024,2048]{1,0:T(8,128)(2,1)S(1)} %copy-done.4, ...), custom_call_target="tpu_custom_call" | custom-call | flops 30000001024 | bytes 20971520 | tf_op jit(solution)/shard_map/pallas_call | solution.py:146
  152.1 11.3 %collective-permute-done.4.rest_4_ = bf16[1024,512]{1,0:T(8,128)(2,1)S(1)} collective-permute-done((bf16[1024,512]{1,0:T(8,128)(2,1)S(1)}, bf16[1024,512]{1,0:T(8,128)(2,1)S(1)}, u32[]{:S(2)}, u32[]{:S(2)}) %collective-permute-start.4) | collective-permute-done | bytes 1048608 | tf_op jit(solution)/shard_map/ppermute | solution.py:457
  174.5 12.5 %collective-permute-done.6.rest_5_ = bf16[512,1024]{1,0:T(8,128)(2,1)} collective-permute-done((bf16[512,1024]{1,0:T(8,128)(2,1)}, bf16[512,1024]{1,0:T(8,128)(2,1)}, u32[]{:S(2)}, u32[]{:S(2)}) %collective-permute-start.6) | collective-permute-done | bytes 1048608 | tf_op jit(solution)/shard_map/ppermute | solution.py:457
  192.7 20.7 %collective-permute-done.7.tokens_a = bf16[1024,1024]{1,0:T(8,128)(2,1)} collective-permute-done((bf16[1024,1024]{1,0:T(8,128)(2,1)}, bf16[1024,1024]{1,0:T(8,128)(2,1)}, u32[]{:S(2)}, u32[]{:S(2)}) %collective-permute-start.7) | collective-permute-done | bytes 2097184 | tf_op jit(solution)/shard_map/ppermute | solution.py:67
  230.6 9.4 %collective-permute-done.8.tokens_a = bf16[1024,1024]{1,0:T(8,128)(2,1)} collective-permute-done((bf16[1024,1024]{1,0:T(8,128)(2,1)}, bf16[1024,1024]{1,0:T(8,128)(2,1)}, u32[]{:S(2)}, u32[]{:S(2)}) %collective-permute-start.8) | collective-permute-done | bytes 2097184 | tf_op jit(solution)/shard_map/ppermute | solution.py:67
  241.7 28.7 %shard_map.231 = (bf16[1088,1024]{1,0:T(8,128)(2,1)}, bf16[1088,1024]{1,0:T(8,128)(2,1)}, bf16[1024,1024]{1,0:T(8,128)(2,1)}, bf16[1024,1024]{1,0:T(8,128)(2,1)}...) custom-call(s32[2]{0:T(128)} %pad_add_fusion.1.ids_ref, ...), custom_call_target="tpu_custom_call" | custom-call | flops 33822867456 | bytes 41943040 | tf_op jit(solution)/shard_map/pallas_call | solution.py:387
  271.2 29.1 %shard_map.232 = (bf16[1088,1024]{1,0:T(8,128)(2,1)}, bf16[1088,1024]{1,0:T(8,128)(2,1)}, bf16[1024,1024]{1,0:T(8,128)(2,1)}, bf16[1024,1024]{1,0:T(8,128)(2,1)}...) custom-call(s32[2]{0:T(128)} %pad_add_fusion.1.ids_ref, ...), custom_call_target="tpu_custom_call", output_to_operand_aliasing={{4}: (16, {}), {5}: (17, {}), {6}: (18, {}), {7}: (19, {})} | custom-call | flops 33822867456 | bytes 41943040 | tf_op jit(solution)/shard_map/pallas_call | solution.py:387
  300.4 10.7 %collective-permute-done.18.rest_2_ = bf16[512,1024]{1,0:T(8,128)(2,1)} collective-permute-done((bf16[512,1024]{1,0:T(8,128)(2,1)}, bf16[512,1024]{1,0:T(8,128)(2,1)}, u32[]{:S(2)}, u32[]{:S(2)}) %collective-permute-start.18) | collective-permute-done | bytes 1048608 | tf_op jit(solution)/shard_map/ppermute | solution.py:457
  311.0 7.8 collective-permute-done.19.rest_4_
  318.8 28.7 %shard_map.233 = (bf16[1088,1024]{1,0:T(8,128)(2,1)}, bf16[1088,1024]{1,0:T(8,128)(2,1)}, bf16[1024,1024]{1,0:T(8,128)(2,1)}, bf16[1024,1024]{1,0:T(8,128)(2,1)}...) custom-call(s32[2]{0:T(128)} %pad_add_fusion.1.ids_ref, ...), custom_call_target="tpu_custom_call", output_to_operand_aliasing={{4}: (16, {}), {5}: (17, {}), {6}: (18, {}), {7}: (19, {})} | custom-call | flops 33822867456 | bytes 41943040 | tf_op jit(solution)/shard_map/pallas_call | solution.py:387
  347.6 29.2 %shard_map.234 = (bf16[1088,1024]{1,0:T(8,128)(2,1)}, bf16[1088,1024]{1,0:T(8,128)(2,1)}, bf16[1024,1024]{1,0:T(8,128)(2,1)}, bf16[1024,1024]{1,0:T(8,128)(2,1)}...) custom-call(s32[2]{0:T(128)} %pad_add_fusion.ids_ref, ...), custom_call_target="tpu_custom_call" | custom-call | flops 33822867456 | bytes 41943040 | tf_op jit(solution)/shard_map/pallas_call | solution.py:387
  376.7 29.1 %shard_map.235 = (bf16[1088,1024]{1,0:T(8,128)(2,1)}, bf16[1088,1024]{1,0:T(8,128)(2,1)}, bf16[1024,1024]{1,0:T(8,128)(2,1)}, bf16[1024,1024]{1,0:T(8,128)(2,1)}...) custom-call(s32[2]{0:T(128)} %pad_add_fusion.ids_ref, ...), custom_call_target="tpu_custom_call", output_to_operand_aliasing={{4}: (16, {}), {5}: (17, {}), {6}: (18, {}), {7}: (19, {})} | custom-call | flops 33822867456 | bytes 41943040 | tf_op jit(solution)/shard_map/pallas_call | solution.py:387
  405.9 28.7 %shard_map.236 = (bf16[1088,1024]{1,0:T(8,128)(2,1)}, bf16[1088,1024]{1,0:T(8,128)(2,1)}, bf16[1024,1024]{1,0:T(8,128)(2,1)}, bf16[1024,1024]{1,0:T(8,128)(2,1)}...) custom-call(s32[2]{0:T(128)} %pad_add_fusion.ids_ref, ...), custom_call_target="tpu_custom_call", output_to_operand_aliasing={{4}: (16, {}), {5}: (17, {}), {6}: (18, {}), {7}: (19, {})} | custom-call | flops 33822867456 | bytes 41943040 | tf_op jit(solution)/shard_map/pallas_call | solution.py:387
  434.6 29.2 %shard_map.237 = (bf16[1088,1024]{1,0:T(8,128)(2,1)}, bf16[1088,1024]{1,0:T(8,128)(2,1)}, bf16[1024,1024]{1,0:T(8,128)(2,1)}, bf16[1024,1024]{1,0:T(8,128)(2,1)}...) custom-call(s32[2]{0:T(128)} %pad_add_fusion.ids_ref, ...), custom_call_target="tpu_custom_call", output_to_operand_aliasing={{4}: (16, {}), {5}: (17, {}), {6}: (18, {}), {7}: (19, {})} | custom-call | flops 33822867456 | bytes 41943040 | tf_op jit(solution)/shard_map/pallas_call | solution.py:387
  463.8 8.5 fusion.60
  472.4 8.0 fusion.65
  506.2 28.9 %shard_map.238 = (bf16[1088,1024]{1,0:T(8,128)(2,1)}, bf16[1088,1024]{1,0:T(8,128)(2,1)}, bf16[1024,1024]{1,0:T(8,128)(2,1)}, bf16[1024,1024]{1,0:T(8,128)(2,1)}...) custom-call(s32[2]{0:T(128)} %pad_add_fusion.1.ids_ref, ...), custom_call_target="tpu_custom_call", output_to_operand_aliasing={{4}: (16, {}), {5}: (17, {}), {6}: (18, {}), {7}: (19, {})} | custom-call | flops 33822867456 | bytes 41943040 | tf_op jit(solution)/shard_map/pallas_call | solution.py:387
  545.5 8.4 fusion.70
  553.9 8.5 fusion.75
  562.4 10.4 %collective-permute-done.28 = bf16[1088,1024]{1,0:T(8,128)(2,1)S(1)} collective-permute-done((bf16[1088,1024]{1,0:T(8,128)(2,1)S(1)}, bf16[1088,1024]{1,0:T(8,128)(2,1)S(1)}, u32[]{:S(2)}, u32[]{:S(2)}) %collective-permute-start.28) | collective-permute-done | bytes 2228256 | tf_op jit(solution)/shard_map/ppermute | solution.py:67
  650.5 20.0 %shard_map.239 = (bf16[1024,512]{1,0:T(8,128)(2,1)S(1)}, bf16[1024,256]{1,0:T(8,128)(2,1)S(1)}, bf16[1024,256]{1,0:T(8,128)(2,1)S(1)}) custom-call(s32[1]{0:T(128)} %copy.137.length_ref, bf16[1024,512]{1,0:T(8,128)(2,1)S(1)} %copy-done.9, bf16[1024,256]{1,0:T(8,128)(2,1)S(1)} %copy-done.15, bf16[1024,256]{1,0:T(8,128)(2,1)S(1)} %copy-done.17, ...), custom_call_target="tpu_custom_call" | custom-call | flops 20000000000 | bytes 10485760 | tf_op jit(solution)/shard_map/pallas_call | solution.py:206
  689.1 20.2 %shard_map.240 = (bf16[1024,512]{1,0:T(8,128)(2,1)S(1)}, bf16[1024,256]{1,0:T(8,128)(2,1)S(1)}, bf16[1024,256]{1,0:T(8,128)(2,1)S(1)}) custom-call(s32[1]{0:T(128)} %copy.137.length_ref, bf16[1024,512]{1,0:T(8,128)(2,1)S(1)} %copy-done.7, bf16[1024,256]{1,0:T(8,128)(2,1)S(1)} %copy-done.11, bf16[1024,256]{1,0:T(8,128)(2,1)S(1)} %copy-done.13, ...), custom_call_target="tpu_custom_call" | custom-call | flops 20000000000 | bytes 10485760 | tf_op jit(solution)/shard_map/pallas_call | solution.py:206
  714.3 16.4 %collective-permute-done.43 = bf16[512,1024]{1,0:T(8,128)(2,1)S(1)} collective-permute-done((bf16[512,1024]{1,0:T(8,128)(2,1)S(1)}, bf16[512,1024]{1,0:T(8,128)(2,1)S(1)}, u32[]{:S(2)}, u32[]{:S(2)}) %collective-permute-start.43) | collective-permute-done | bytes 1048608 | tf_op jit(solution)/shard_map/ppermute | solution.py:457
  739.9 8.4 fusion.40
  767.6 25.3 %collective-permute-done.48 = f32[34,1024]{1,0:T(8,128)S(1)} collective-permute-done((f32[34,1024]{1,0:T(8,128)S(1)}, f32[34,1024]{1,0:T(8,128)S(1)}, u32[]{:S(2)}, u32[]{:S(2)}) %collective-permute-start.48) | collective-permute-done | bytes 139296 | tf_op jit(solution)/shard_map/ppermute | solution.py:739
  800.1 36.9 %collective-permute-done.49 = f32[34,1024]{1,0:T(8,128)S(1)} collective-permute-done((f32[34,1024]{1,0:T(8,128)S(1)}, f32[34,1024]{1,0:T(8,128)S(1)}, u32[]{:S(2)}, u32[]{:S(2)}) %collective-permute-start.49) | collective-permute-done | bytes 139296 | tf_op jit(solution)/shard_map/ppermute | solution.py:739
  844.1 18.8 %collective-permute-done.55 = bf16[512,1024]{1,0:T(8,128)(2,1)S(1)} collective-permute-done((bf16[512,1024]{1,0:T(8,128)(2,1)S(1)}, bf16[512,1024]{1,0:T(8,128)(2,1)S(1)}, u32[]{:S(2)}, u32[]{:S(2)}) %collective-permute-start.55) | collective-permute-done | bytes 1048608 | tf_op jit(solution)/shard_map/ppermute | solution.py:583
  (448 shorter events, 276.4 us)
Async XLA Ops:
  7.2 62.2 %all-gather.3.cloned.1.call-start = ((), (), s32[]{:S(2)}) async-start(), calls=%async_computation.2 | async-start | bytes 4456448 | tf_op jit(solution)/shard_map/all_gather | solution.py:451
  9.1 156.4 %all-gather.5.cloned.1.call-start = ((), (), s32[]{:S(2)}) async-start(), calls=%async_computation.3 | async-start | bytes 2228224 | tf_op jit(solution)/shard_map/all_gather | solution.py:453
  54.6 134.7 %collective-permute-start.12 = (bf16[1056,1024]{1,0:T(8,128)(2,1)}, bf16[1056,1024]{1,0:T(8,128)(2,1)}, u32[]{:S(2)}, u32[]{:S(2)}) collective-permute-start(bf16[1056,1024]{1,0:T(8,128)(2,1)} %pad_maximum_fusion.1.slope_a.mask_a), channel_id=1, source_target_pairs={{0,2},{2,0},{4,6},{6,4},{5,7},{7,5},{1,3},{3,1},{8,10},{10,8},{12,... | collective-permute-start | bytes 6488072 | tf_op jit(solution)/shard_map/ppermute | solution.py:70
  60.2 130.8 %collective-permute-start.11 = (bf16[1056,1024]{1,0:T(8,128)(2,1)}, bf16[1056,1024]{1,0:T(8,128)(2,1)}, u32[]{:S(2)}, u32[]{:S(2)}) collective-permute-start(bf16[1056,1024]{1,0:T(8,128)(2,1)} %collective-permute-done.slope_a.mask_a), channel_id=1, source_target_pairs={{0,2},{2,0},{4,6},{6,4},{5,7},{7,5},{1,3},{3,1},{8,10},{10,8},{12,... | collective-permute-start | bytes 6488072 | tf_op jit(solution)/shard_map/ppermute | solution.py:70
  79.3 51.5 %collective-permute-start.3 = (bf16[1024,512]{1,0:T(8,128)(2,1)}, bf16[1024,512]{1,0:T(8,128)(2,1)}, u32[]{:S(2)}, u32[]{:S(2)}) collective-permute-start(bf16[1024,512]{1,0:T(8,128)(2,1)} %get-tuple-element.250.rest_0_), channel_id=1, source_target_pairs={{0,8},{2,10},{4,12},{6,14},{8,0},{10,2},{12,4},{14,6},{16,24},{18,... | collective-permute-start | bytes 3145736 | tf_op jit(solution)/shard_map/ppermute | solution.py:457
  80.9 71.0 %collective-permute-start.5 = (bf16[1024,512]{1,0:T(8,128)(2,1)}, bf16[1024,512]{1,0:T(8,128)(2,1)}, u32[]{:S(2)}, u32[]{:S(2)}) collective-permute-start(bf16[1024,512]{1,0:T(8,128)(2,1)} %get-tuple-element.250.rest_0_), channel_id=1, source_target_pairs={{0,16},{2,18},{4,20},{6,22},{8,24},{10,26},{12,28},{14,30},{16,0},... | collective-permute-start | bytes 3145736 | tf_op jit(solution)/shard_map/ppermute | solution.py:457
  86.0 787.9 %reduce-scatter.3.cloned.1.call-start = ((), (), s32[]{:S(2)}) async-start(), calls=%async_computation.4 | async-start | bytes 2228224 | tf_op jit(solution)/shard_map/reduce_scatter | solution.py:691
  112.0 103.2 %collective-permute-start.13 = (bf16[1056,1024]{1,0:T(8,128)(2,1)}, bf16[1056,1024]{1,0:T(8,128)(2,1)}, u32[]{:S(2)}, u32[]{:S(2)}) collective-permute-start(bf16[1056,1024]{1,0:T(8,128)(2,1)} %collective-permute-done.1.slope_a.mask_a), channel_id=1, source_target_pairs={{0,2},{2,0},{4,6},{6,4},{5,7},{7,5},{1,3},{3,1},{8,10},{10,8},{12,... | collective-permute-start | bytes 6488072 | tf_op jit(solution)/shard_map/ppermute | solution.py:70
  216.8 53.5 %collective-permute-start.15 = (bf16[1024,512]{1,0:T(8,128)(2,1)}, bf16[1024,512]{1,0:T(8,128)(2,1)}, u32[]{:S(2)}, u32[]{:S(2)}) collective-permute-start(bf16[1024,512]{1,0:T(8,128)(2,1)} %get-tuple-element.251.rest_1_), channel_id=1, source_target_pairs={{0,16},{2,18},{4,20},{6,22},{8,24},{10,26},{12,28},{14,30},{16,0},... | collective-permute-start | bytes 3145736 | tf_op jit(solution)/shard_map/ppermute | solution.py:457
  218.1 52.8 %collective-permute-start.16 = (bf16[1024,512]{1,0:T(8,128)(2,1)}, bf16[1024,512]{1,0:T(8,128)(2,1)}, u32[]{:S(2)}, u32[]{:S(2)}) collective-permute-start(bf16[1024,512]{1,0:T(8,128)(2,1)} %collective-permute-done.5.rest_0_), channel_id=1, source_target_pairs={{0,8},{2,10},{4,12},{6,14},{8,0},{10,2},{12,4},{14,6},{16,24},{18,... | collective-permute-start | bytes 3145736 | tf_op jit(solution)/shard_map/ppermute | solution.py:457
  223.6 87.4 %collective-permute-start.18 = (bf16[512,1024]{1,0:T(8,128)(2,1)}, bf16[512,1024]{1,0:T(8,128)(2,1)}, u32[]{:S(2)}, u32[]{:S(2)}) collective-permute-start(bf16[512,1024]{1,0:T(8,128)(2,1)} %dynamic-slice_bitcast_fusion.rest_2_), channel_id=1, source_target_pairs={{0,16},{2,18},{4,20},{6,22},{8,24},{10,26},{12,28},{14,30},{16,0},... | collective-permute-start | bytes 3145736 | tf_op jit(solution)/shard_map/ppermute | solution.py:457
  270.4 164.2 %collective-permute-start.22 = (bf16[1024,1024]{1,0:T(8,128)(2,1)}, bf16[1024,1024]{1,0:T(8,128)(2,1)}, u32[]{:S(2)}, u32[]{:S(2)}) collective-permute-start(bf16[1024,1024]{1,0:T(8,128)(2,1)} %multiply_convert_fusion.tokens_a), channel_id=1, source_target_pairs={{0,2},{2,0},{4,6},{6,4},{5,7},{7,5},{1,3},{3,1},{8,10},{10,8},{12,... | collective-permute-start | bytes 6291464 | tf_op jit(solution)/shard_map/ppermute | solution.py:70
  271.0 47.8 %collective-permute-start.19 = (bf16[1024,512]{1,0:T(8,128)(2,1)}, bf16[1024,512]{1,0:T(8,128)(2,1)}, u32[]{:S(2)}, u32[]{:S(2)}) collective-permute-start(bf16[1024,512]{1,0:T(8,128)(2,1)} %collective-permute-done.15.rest_1_), channel_id=1, source_target_pairs={{0,8},{2,10},{4,12},{6,14},{8,0},{10,2},{12,4},{14,6},{16,24},{18,... | collective-permute-start | bytes 3145736 | tf_op jit(solution)/shard_map/ppermute | solution.py:457
  271.2 47.6 %collective-permute-start.20 = (bf16[1024,1024]{1,0:T(8,128)(2,1)}, bf16[1024,1024]{1,0:T(8,128)(2,1)}, u32[]{:S(2)}, u32[]{:S(2)}) collective-permute-start(bf16[1024,1024]{1,0:T(8,128)(2,1)} %collective-permute-done.9.tokens_a), channel_id=1, source_target_pairs={{0,2},{2,0},{4,6},{6,4},{5,7},{7,5},{1,3},{3,1},{8,10},{10,8},{12,... | collective-permute-start | bytes 6291464 | tf_op jit(solution)/shard_map/ppermute | solution.py:70
  485.2 55.5 %collective-permute-start.25 = (bf16[1088,1024]{1,0:T(8,128)(2,1)}, bf16[1088,1024]{1,0:T(8,128)(2,1)}, u32[]{:S(2)}, u32[]{:S(2)}) collective-permute-start(bf16[1088,1024]{1,0:T(8,128)(2,1)} %add_convert_fusion.4), channel_id=1, source_target_pairs={{0,2},{2,0},{4,6},{6,4},{5,7},{7,5},{1,3},{3,1},{8,10},{10,8},{12,... | collective-permute-start | bytes 6684680 | tf_op jit(solution)/shard_map/ppermute | solution.py:70
  487.7 74.8 %collective-permute-start.24 = (bf16[1088,1024]{1,0:T(8,128)(2,1)}, bf16[1088,1024]{1,0:T(8,128)(2,1)}, u32[]{:S(2)}, u32[]{:S(2)}) collective-permute-start(bf16[1088,1024]{1,0:T(8,128)(2,1)} %add_convert_fusion.5), channel_id=1, source_target_pairs={{0,2},{2,0},{4,6},{6,4},{5,7},{7,5},{1,3},{3,1},{8,10},{10,8},{12,... | collective-permute-start | bytes 6684680 | tf_op jit(solution)/shard_map/ppermute | solution.py:70
  500.5 96.3 %collective-permute-start.31 = (bf16[512,1024]{1,0:T(8,128)(2,1)}, bf16[512,1024]{1,0:T(8,128)(2,1)}, u32[]{:S(2)}, u32[]{:S(2)}) collective-permute-start(bf16[512,1024]{1,0:T(8,128)(2,1)} %get-tuple-element.332), channel_id=1, source_target_pairs={{0,8},{2,10},{4,12},{6,14},{8,0},{10,2},{12,4},{14,6},{16,24},{18,... | collective-permute-start | bytes 3145736 | tf_op jit(solution)/shard_map/ppermute | solution.py:457
  538.6 58.1 %collective-permute-start.32 = (bf16[512,1024]{1,0:T(8,128)(2,1)S(1)}, bf16[512,1024]{1,0:T(8,128)(2,1)S(1)}, u32[]{:S(2)}, u32[]{:S(2)}) collective-permute-start(bf16[512,1024]{1,0:T(8,128)(2,1)S(1)} %copy-done.104), channel_id=1, source_target_pairs={{0,8},{2,10},{4,12},{6,14},{8,0},{10,2},{12,4},{14,6},{16,24},{18,... | collective-permute-start | bytes 3145736 | tf_op jit(solution)/shard_map/ppermute | solution.py:457
  540.7 63.8 %collective-permute-start.23 = (bf16[1088,1024]{1,0:T(8,128)(2,1)S(1)}, bf16[1088,1024]{1,0:T(8,128)(2,1)S(1)}, u32[]{:S(2)}, u32[]{:S(2)}) collective-permute-start(bf16[1088,1024]{1,0:T(8,128)(2,1)S(1)} %add_convert_fusion.6), channel_id=1, source_target_pairs={{0,2},{2,0},{4,6},{6,4},{5,7},{7,5},{1,3},{3,1},{8,10},{10,8},{12,... | collective-permute-start | bytes 6684680 | tf_op jit(solution)/shard_map/ppermute | solution.py:70
  579.8 98.4 %collective-permute-start.39 = (bf16[512,1024]{1,0:T(8,128)(2,1)}, bf16[512,1024]{1,0:T(8,128)(2,1)}, u32[]{:S(2)}, u32[]{:S(2)}) collective-permute-start(bf16[512,1024]{1,0:T(8,128)(2,1)} %add_convert_fusion.20), channel_id=1, source_target_pairs={{0,16},{2,18},{4,20},{6,22},{8,24},{10,26},{12,28},{14,30},{16,0},... | collective-permute-start | bytes 3145736 | tf_op jit(solution)/shard_map/ppermute | solution.py:457
  620.6 57.5 %collective-permute-start.38 = (bf16[512,1024]{1,0:T(8,128)(2,1)}, bf16[512,1024]{1,0:T(8,128)(2,1)}, u32[]{:S(2)}, u32[]{:S(2)}) collective-permute-start(bf16[512,1024]{1,0:T(8,128)(2,1)} %get-tuple-element.372), channel_id=1, source_target_pairs={{0,8},{2,10},{4,12},{6,14},{8,0},{10,2},{12,4},{14,6},{16,24},{18,... | collective-permute-start | bytes 3145736 | tf_op jit(solution)/shard_map/ppermute | solution.py:457
  636.8 44.9 %collective-permute-start.40 = (bf16[1024,1024]{1,0:T(8,128)(2,1)}, bf16[1024,1024]{1,0:T(8,128)(2,1)}, u32[]{:S(2)}, u32[]{:S(2)}) collective-permute-start(bf16[1024,1024]{1,0:T(8,128)(2,1)} %add_convert_fusion.10), channel_id=1, source_target_pairs={{0,2},{2,0},{4,6},{6,4},{5,7},{7,5},{1,3},{3,1},{8,10},{10,8},{12,... | collective-permute-start | bytes 6291464 | tf_op jit(solution)/shard_map/ppermute | solution.py:70
  636.8 237.0 %reduce-scatter.5.cloned.1.call-start = ((), (), s32[]{:S(2)}) async-start(), calls=%async_computation.5 | async-start | bytes 4456448 | tf_op jit(solution)/shard_map/reduce_scatter | solution.py:728
  650.4 144.8 %collective-permute-start.34 = (bf16[1024,1024]{1,0:T(8,128)(2,1)}, bf16[1024,1024]{1,0:T(8,128)(2,1)}, u32[]{:S(2)}, u32[]{:S(2)}) collective-permute-start(bf16[1024,1024]{1,0:T(8,128)(2,1)} %add_convert_fusion.13), channel_id=1, source_target_pairs={{0,2},{2,0},{4,6},{6,4},{5,7},{7,5},{1,3},{3,1},{8,10},{10,8},{12,... | collective-permute-start | bytes 6291464 | tf_op jit(solution)/shard_map/ppermute | solution.py:70
  671.7 194.3 %collective-permute-start.33 = (bf16[1024,1024]{1,0:T(8,128)(2,1)}, bf16[1024,1024]{1,0:T(8,128)(2,1)}, u32[]{:S(2)}, u32[]{:S(2)}) collective-permute-start(bf16[1024,1024]{1,0:T(8,128)(2,1)} %add_convert_fusion.14), channel_id=1, source_target_pairs={{0,2},{2,0},{4,6},{6,4},{5,7},{7,5},{1,3},{3,1},{8,10},{10,8},{12,... | collective-permute-start | bytes 6291464 | tf_op jit(solution)/shard_map/ppermute | solution.py:70
  678.2 52.5 %collective-permute-start.43 = (bf16[512,1024]{1,0:T(8,128)(2,1)S(1)}, bf16[512,1024]{1,0:T(8,128)(2,1)S(1)}, u32[]{:S(2)}, u32[]{:S(2)}) collective-permute-start(bf16[512,1024]{1,0:T(8,128)(2,1)S(1)} %copy-done.103), channel_id=1, source_target_pairs={{0,8},{2,10},{4,12},{6,14},{8,0},{10,2},{12,4},{14,6},{16,24},{18,... | collective-permute-start | bytes 3145736 | tf_op jit(solution)/shard_map/ppermute | solution.py:457
  678.2 78.9 %collective-permute-start.44 = (bf16[512,1024]{1,0:T(8,128)(2,1)}, bf16[512,1024]{1,0:T(8,128)(2,1)}, u32[]{:S(2)}, u32[]{:S(2)}) collective-permute-start(bf16[512,1024]{1,0:T(8,128)(2,1)} %add_convert_fusion.19), channel_id=1, source_target_pairs={{0,16},{2,18},{4,20},{6,22},{8,24},{10,26},{12,28},{14,30},{16,0},... | collective-permute-start | bytes 3145736 | tf_op jit(solution)/shard_map/ppermute | solution.py:457
  714.2 49.8 %collective-permute-start.53 = (bf16[512,1024]{1,0:T(8,128)(2,1)S(1)}, bf16[512,1024]{1,0:T(8,128)(2,1)}, u32[]{:S(2)}, u32[]{:S(2)}) collective-permute-start(bf16[512,1024]{1,0:T(8,128)(2,1)S(1)} %add_convert_fusion.17), channel_id=1, source_target_pairs={{0,1},{1,0},{2,3},{3,2},{4,5},{5,4},{6,7},{7,6},{8,9},{9,8},{10,11... | collective-permute-start | bytes 3145736 | tf_op jit(solution)/shard_map/ppermute | solution.py:583
  757.0 80.0 %collective-permute-start.50 = (bf16[512,1024]{1,0:T(8,128)(2,1)S(1)}, bf16[512,1024]{1,0:T(8,128)(2,1)S(1)}, u32[]{:S(2)}, u32[]{:S(2)}) collective-permute-start(bf16[512,1024]{1,0:T(8,128)(2,1)S(1)} %copy-done.62), channel_id=1, source_target_pairs={{0,16},{2,18},{4,20},{6,22},{8,24},{10,26},{12,28},{14,30},{16,0},... | collective-permute-start | bytes 3145736 | tf_op jit(solution)/shard_map/ppermute | solution.py:457
  763.7 74.3 %collective-permute-start.54 = (bf16[512,1024]{1,0:T(8,128)(2,1)S(1)}, bf16[512,1024]{1,0:T(8,128)(2,1)S(1)}, u32[]{:S(2)}, u32[]{:S(2)}) collective-permute-start(bf16[512,1024]{1,0:T(8,128)(2,1)S(1)} %add_convert_fusion.16), channel_id=1, source_target_pairs={{0,1},{1,0},{2,3},{3,2},{4,5},{5,4},{6,7},{7,6},{8,9},{9,8},{10,11... | collective-permute-start | bytes 3145736 | tf_op jit(solution)/shard_map/ppermute | solution.py:583
  793.0 44.0 %collective-permute-start.49 = (f32[34,1024]{1,0:T(8,128)S(1)}, f32[34,1024]{1,0:T(8,128)S(1)}, u32[]{:S(2)}, u32[]{:S(2)}) collective-permute-start(f32[34,1024]{1,0:T(8,128)S(1)} %add.243), channel_id=1, source_target_pairs={{0,16},{2,18},{4,20},{6,22},{8,24},{10,26},{12,28},{14,30},{16,0},... | collective-permute-start | bytes 417800 | tf_op jit(solution)/shard_map/ppermute | solution.py:739
  798.9 67.1 %collective-permute-start.42 = (bf16[1024,1024]{1,0:T(8,128)(2,1)S(1)}, bf16[1024,1024]{1,0:T(8,128)(2,1)S(1)}, u32[]{:S(2)}, u32[]{:S(2)}) collective-permute-start(bf16[1024,1024]{1,0:T(8,128)(2,1)S(1)} %add_convert_fusion.8), channel_id=1, source_target_pairs={{0,4},{6,2},{4,5},{7,6},{5,1},{3,7},{1,0},{2,3},{8,12},{14,10},{12... | collective-permute-start | bytes 6291464 | tf_op jit(solution)/shard_map/ppermute | solution.py:67
  (142 other events, 3526.4 us)
Sparse Core Ops, SparseCore 0:
  10.8 58.5 all-gather.2
  86.1 71.4 all-gather.4
  637.0 95.9 reduce-scatter.2
  738.4 95.1 reduce-scatter.4

commit v4 on v3

--- a/solution.py
+++ b/solution.py
@@ -552,8 +552,9 @@
     half_slots = [slots[:, h * count : (h + 1) * count] for h in range(len(half_ids))]
 
     if layered:
-        order = [(0, step) for step in range(1, ring.steps)]
-        order += [(1, step % ring.steps) for step in range(1, ring.steps + 1)] + [(0, 0)]
+        order = [(0, step) for step in range(ring.steps - 1)]
+        order += [(1, step % ring.steps) for step in range(1, ring.steps + 1)]
+        order += [(0, ring.steps - 1)]
     else:
         half_weights = [
             [w[e] for e in range(local_experts) for w in (gate_weight, up_weight, down_weight)]
@@ -591,7 +592,7 @@
     kept = [None] * len(half_ids)
     back_parts = [([], []) for _ in range(ring.steps)]
     mix_parts = [([], []) for _ in range(ring.steps)]
-    total, next_step, last = None, 1, None
+    total, totals, next_step, last = None, [], 1, None
     for turn, (which, step) in enumerate(order):
         tokens_now = near[step]
         if last is not None:
@@ -627,14 +628,20 @@
             far_grads = [thirds(pair) for pair in expert_grads(kept[1])]
             last, far_grads = barrier((last, far_grads))
             three_sum.append(layer_swap(far_grads[1][0], 1))
-        elif layered and (which, step) == (0, 0):
+        elif layered and turn == len(order) - 1:
             last, kept[0], three_sum[0] = barrier((last, kept[0], three_sum[0]))
             two_sum.append(to_owner(0))
             three_sum += [layer_swap(far_grads[1][at], 1) for at in (1, 2)]
+        if layered and 0 <= turn - ring.steps - 1 < len(totals):
+            at = turn - ring.steps - 1
+            last, totals[at] = barrier((last, totals[at]))
+            if at == len(totals) - 1:
+                total = totals[at]
         mix_parts[step][0][-1] = last
         while next_step < ring.steps and len(back_parts[next_step][0]) == len(half_ids):
             more = () if total is None else (total,)
             total = ring.hop(ring.part_sum(*back_parts[next_step], *more).astype(bf16))
+            totals.append(total)
             next_step += 1
 
     if layered:
@@ -718,7 +725,8 @@
     )
     pre_slopes, mix = barrier((pre_slopes, mix))
     if layered:
-        pre_slopes, next_sum[2] = barrier((pre_slopes, next_sum[2]))
+        pre_slopes, next_sum[2], two_sum[1] = barrier((pre_slopes, next_sum[2], two_sum[1]))
+        finish(1)
     while mix_step < ring.steps:
         mix = mix_hop(mix_step, mix)
         mix_step += 1
@@ -751,9 +759,7 @@
     )
     input_gradient = input_slope.astype(bf16)
     if layered:
-        input_gradient, two_sum[1] = barrier((input_gradient, two_sum[1]))
-        finish(1)
-        gain_sum, two_sum[2] = barrier((gain_sum, two_sum[2]))
+        input_gradient, two_sum[2] = barrier((input_gradient, two_sum[2]))
         finish(2)
     layer_output = (residual + ring.part_sum(*mix_parts[0], mix)).astype(bf16)
 

time: 901 us -> 874 us (0.970)
  waiting for transfers between devices: 286 us -> 236 us
  starting transfers between devices: 50.5 us -> 62.2 us
    ppermute x5, waiting for transfers between devices: 71.6 us -> 22.8 us  [on_device(): lax.ppermute(gain_sum, axis, [(place, place ^ far_bit) for place in range...]
    ppermute x18, waiting for transfers between devices: 85.7 us -> 106 us  [layer_swap(): lax.ppermute(array, 'shard', [(s, s ^ stride) for s in range(shards)])]
    ppermute x18, starting transfers between devices: 18.7 us -> 28.3 us  [layer_swap(): lax.ppermute(array, 'shard', [(s, s ^ stride) for s in range(shards)])]
    unnamed x241 -> x251, local copies, waits for them, and re-layouts: 23.2 us -> 26.3 us
  transfers between devices with their start and end apart: 60 -> 60, of which waited for: 23 -> 22; matrix products, arithmetic and copies ran while one was open for 22% -> 26% of each run, Pallas kernels for 31% -> 36%
where the time goes in v4:
time: 874 us; the launch traced here: 867 us
  Pallas kernels  311 us (36%)
  waiting for transfers between devices  236 us (27%)
  other arithmetic  103 us (12%)
  matrix products  86.9 us (10%)
  starting transfers between devices  62.2 us (7%)
  local copies, waits for them, and re-layouts  53 us (6%)
  between operations  16.5 us (2%)
    pallas_call x8, Pallas kernels, experts_pair(): pl.pallas_call(functools.partial(pair_kernel, count, step, chained), out_...  232 us
    ppermute x18, waiting for transfers between devices, layer_swap(): lax.ppermute(array, 'shard', [(s, s ^ stride) for s in range(shards)])  106 us
    ppermute x12, waiting for transfers between devices, hop(): return lax.ppermute(array, ('shard', 'rep'), self.forward)  87.2 us
    pallas_call x2, Pallas kernels, attention_backward(): pl.pallas_call(functools.partial(backward_kernel, block), out_shape=[jax....  40.3 us
    pallas_call x2, Pallas kernels, attention_forward(): pl.pallas_call(functools.partial(forward_kernel, block), out_shape=[jax.S...  38.6 us
    dot_general x4, matrix products, expert_grads(): lax.dot_general(rows[e], slopes[e], turned, preferred_element_type=f32)  32.8 us
    ppermute x18, starting transfers between devices, layer_swap(): lax.ppermute(array, 'shard', [(s, s ^ stride) for s in range(shards)])  28.3 us
    convert_element_type x8, other arithmetic, part_sum(): parts = [*near, self.cross(far.astype(jnp.bfloat16)), *more]  27.3 us
  transfers between devices with their start and end apart: 60, of which 22 were waited for; matrix products, arithmetic and copies ran while one was open for 26% of the time, Pallas kernels for 36%

profile of v4, /device:TPU:0, one launch (start us, length us, event | category | flops | bytes accessed | tf_op | source)
XLA Modules:
  0.0 867.4 jit_solution(16031834398843861942)
XLA Ops:
  19.9 32.3 %collective-permute-done.slope_a.mask_a = bf16[1056,1024]{1,0:T(8,128)(2,1)} collective-permute-done((bf16[1056,1024]{1,0:T(8,128)(2,1)}, bf16[1056,1024]{1,0:T(8,128)(2,1)}, u32[]{:S(2)}, u32[]{:S(2)}) %collective-permute-start) | collective-permute-done | bytes 2162720 | tf_op jit(solution)/shard_map/ppermute | solution.py:67
  67.5 12.7 %collective-permute-done.1.slope_a.mask_a = bf16[1056,1024]{1,0:T(8,128)(2,1)} collective-permute-done((bf16[1056,1024]{1,0:T(8,128)(2,1)}, bf16[1056,1024]{1,0:T(8,128)(2,1)}, u32[]{:S(2)}, u32[]{:S(2)}) %collective-permute-start.1) | collective-permute-done | bytes 2162720 | tf_op jit(solution)/shard_map/ppermute | solution.py:67
  89.6 19.2 %shard_map.229 = (bf16[1024,512]{1,0:T(8,128)(2,1)S(1)}, bf16[1024,256]{1,0:T(8,128)(2,1)S(1)}, bf16[1024,256]{1,0:T(8,128)(2,1)S(1)}, bf16[1024,512]{1,0:T(8,128)(2,1)S(1)}, f32[2,4,1024]{2,1,0:T(4,128)S(1)}) custom-call(s32[1]{0:T(128)} %copy.137.length_ref, bf16[1024,1024]{1,0:T(8,128)(2,1)S(1)} %copy-done.2, bf16[1024,2048]{1,0:T(8,128)(2,1)S(1)} %copy-done.3, ...), custom_call_target="tpu_custom_call" | custom-call | flops 30000001024 | bytes 20971520 | tf_op jit(solution)/shard_map/pallas_call | solution.py:146
  112.0 21.9 %collective-permute-done.3.rest_3_ = bf16[1024,512]{1,0:T(8,128)(2,1)} collective-permute-done((bf16[1024,512]{1,0:T(8,128)(2,1)}, bf16[1024,512]{1,0:T(8,128)(2,1)}, u32[]{:S(2)}, u32[]{:S(2)}) %collective-permute-start.3) | collective-permute-done | bytes 1048608 | tf_op jit(solution)/shard_map/ppermute | solution.py:457
  133.9 19.4 %shard_map.230 = (bf16[1024,512]{1,0:T(8,128)(2,1)S(1)}, bf16[1024,256]{1,0:T(8,128)(2,1)S(1)}, bf16[1024,256]{1,0:T(8,128)(2,1)S(1)}, bf16[1024,512]{1,0:T(8,128)(2,1)S(1)}, f32[2,4,1024]{2,1,0:T(4,128)S(1)}) custom-call(s32[1]{0:T(128)} %copy.137.length_ref, bf16[1024,1024]{1,0:T(8,128)(2,1)S(1)} %copy-done.2, bf16[1024,2048]{1,0:T(8,128)(2,1)S(1)} %copy-done.4, ...), custom_call_target="tpu_custom_call" | custom-call | flops 30000001024 | bytes 20971520 | tf_op jit(solution)/shard_map/pallas_call | solution.py:146
  154.9 11.5 %collective-permute-done.4.rest_4_ = bf16[1024,512]{1,0:T(8,128)(2,1)S(1)} collective-permute-done((bf16[1024,512]{1,0:T(8,128)(2,1)}, bf16[1024,512]{1,0:T(8,128)(2,1)S(1)}, u32[]{:S(2)}, u32[]{:S(2)}) %collective-permute-start.4) | collective-permute-done | bytes 1048608 | tf_op jit(solution)/shard_map/ppermute | solution.py:457
  175.8 13.9 %collective-permute-done.6.rest_5_ = bf16[512,1024]{1,0:T(8,128)(2,1)} collective-permute-done((bf16[512,1024]{1,0:T(8,128)(2,1)}, bf16[512,1024]{1,0:T(8,128)(2,1)}, u32[]{:S(2)}, u32[]{:S(2)}) %collective-permute-start.6) | collective-permute-done | bytes 1048608 | tf_op jit(solution)/shard_map/ppermute | solution.py:457
  219.7 28.7 %shard_map.231 = (bf16[1088,1024]{1,0:T(8,128)(2,1)}, bf16[1088,1024]{1,0:T(8,128)(2,1)}, bf16[1024,1024]{1,0:T(8,128)(2,1)}, bf16[1024,1024]{1,0:T(8,128)(2,1)}...) custom-call(s32[2]{0:T(128)} %pad_add_fusion.ids_ref, ...), custom_call_target="tpu_custom_call" | custom-call | flops 33822867456 | bytes 41943040 | tf_op jit(solution)/shard_map/pallas_call | solution.py:387
  249.1 29.1 %shard_map.232 = (bf16[1088,1024]{1,0:T(8,128)(2,1)}, bf16[1088,1024]{1,0:T(8,128)(2,1)}, bf16[1024,1024]{1,0:T(8,128)(2,1)}, bf16[1024,1024]{1,0:T(8,128)(2,1)}...) custom-call(s32[2]{0:T(128)} %pad_add_fusion.ids_ref, ...), custom_call_target="tpu_custom_call", output_to_operand_aliasing={{4}: (16, {}), {5}: (17, {}), {6}: (18, {}), {7}: (19, {})} | custom-call | flops 33822867456 | bytes 41943040 | tf_op jit(solution)/shard_map/pallas_call | solution.py:387
  278.2 11.2 %collective-permute-done.18.rest_2_ = bf16[512,1024]{1,0:T(8,128)(2,1)} collective-permute-done((bf16[512,1024]{1,0:T(8,128)(2,1)}, bf16[512,1024]{1,0:T(8,128)(2,1)}, u32[]{:S(2)}, u32[]{:S(2)}) %collective-permute-start.18) | collective-permute-done | bytes 1048608 | tf_op jit(solution)/shard_map/ppermute | solution.py:457
  289.4 7.1 collective-permute-done.19.rest_4_
  296.5 29.0 %shard_map.233 = (bf16[1088,1024]{1,0:T(8,128)(2,1)}, bf16[1088,1024]{1,0:T(8,128)(2,1)}, bf16[1024,1024]{1,0:T(8,128)(2,1)}, bf16[1024,1024]{1,0:T(8,128)(2,1)}...) custom-call(s32[2]{0:T(128)} %pad_add_fusion.ids_ref, ...), custom_call_target="tpu_custom_call", output_to_operand_aliasing={{4}: (16, {}), {5}: (17, {}), {6}: (18, {}), {7}: (19, {})} | custom-call | flops 33822867456 | bytes 41943040 | tf_op jit(solution)/shard_map/pallas_call | solution.py:387
  325.5 28.9 %shard_map.234 = (bf16[1088,1024]{1,0:T(8,128)(2,1)}, bf16[1088,1024]{1,0:T(8,128)(2,1)}, bf16[1024,1024]{1,0:T(8,128)(2,1)}, bf16[1024,1024]{1,0:T(8,128)(2,1)}...) custom-call(s32[2]{0:T(128)} %pad_add_fusion.2.ids_ref, ...), custom_call_target="tpu_custom_call" | custom-call | flops 33822867456 | bytes 41943040 | tf_op jit(solution)/shard_map/pallas_call | solution.py:387
  365.1 29.0 %shard_map.235 = (bf16[1088,1024]{1,0:T(8,128)(2,1)}, bf16[1088,1024]{1,0:T(8,128)(2,1)}, bf16[1024,1024]{1,0:T(8,128)(2,1)}, bf16[1024,1024]{1,0:T(8,128)(2,1)}...) custom-call(s32[2]{0:T(128)} %pad_add_fusion.2.ids_ref, ...), custom_call_target="tpu_custom_call", output_to_operand_aliasing={{4}: (16, {}), {5}: (17, {}), {6}: (18, {}), {7}: (19, {})} | custom-call | flops 33822867456 | bytes 41943040 | tf_op jit(solution)/shard_map/pallas_call | solution.py:387
  404.4 28.9 %shard_map.236 = (bf16[1088,1024]{1,0:T(8,128)(2,1)}, bf16[1088,1024]{1,0:T(8,128)(2,1)}, bf16[1024,1024]{1,0:T(8,128)(2,1)}, bf16[1024,1024]{1,0:T(8,128)(2,1)}...) custom-call(s32[2]{0:T(128)} %pad_add_fusion.2.ids_ref, ...), custom_call_target="tpu_custom_call", output_to_operand_aliasing={{4}: (16, {}), {5}: (17, {}), {6}: (18, {}), {7}: (19, {})} | custom-call | flops 33822867456 | bytes 41943040 | tf_op jit(solution)/shard_map/pallas_call | solution.py:387
  433.4 28.9 %shard_map.237 = (bf16[1088,1024]{1,0:T(8,128)(2,1)}, bf16[1088,1024]{1,0:T(8,128)(2,1)}, bf16[1024,1024]{1,0:T(8,128)(2,1)}, bf16[1024,1024]{1,0:T(8,128)(2,1)}...) custom-call(s32[2]{0:T(128)} %pad_add_fusion.2.ids_ref, ...), custom_call_target="tpu_custom_call", output_to_operand_aliasing={{4}: (16, {}), {5}: (17, {}), {6}: (18, {}), {7}: (19, {})} | custom-call | flops 33822867456 | bytes 41943040 | tf_op jit(solution)/shard_map/pallas_call | solution.py:387
  462.3 8.5 fusion.65
  470.9 7.9 fusion.60
  500.5 11.0 %collective-permute-done.27 = bf16[1088,1024]{1,0:T(8,128)(2,1)} collective-permute-done((bf16[1088,1024]{1,0:T(8,128)(2,1)S(1)}, bf16[1088,1024]{1,0:T(8,128)(2,1)}, u32[]{:S(2)}, u32[]{:S(2)}) %collective-permute-start.27) | collective-permute-done | bytes 2228256 | tf_op jit(solution)/shard_map/ppermute | solution.py:67
  511.5 29.0 %shard_map.238 = (bf16[1088,1024]{1,0:T(8,128)(2,1)}, bf16[1088,1024]{1,0:T(8,128)(2,1)}, bf16[1024,1024]{1,0:T(8,128)(2,1)}, bf16[1024,1024]{1,0:T(8,128)(2,1)}...) custom-call(s32[2]{0:T(128)} %pad_add_fusion.ids_ref, ...), custom_call_target="tpu_custom_call", output_to_operand_aliasing={{4}: (16, {}), {5}: (17, {}), {6}: (18, {}), {7}: (19, {})} | custom-call | flops 33822867456 | bytes 41943040 | tf_op jit(solution)/shard_map/pallas_call | solution.py:387
  544.1 8.5 fusion.75
  552.7 7.9 fusion.70
  568.9 6.8 fusion.95
  582.4 10.1 %collective-permute-done.29 = bf16[1088,1024]{1,0:T(8,128)(2,1)S(1)} collective-permute-done((bf16[1088,1024]{1,0:T(8,128)(2,1)S(1)}, bf16[1088,1024]{1,0:T(8,128)(2,1)S(1)}, u32[]{:S(2)}, u32[]{:S(2)}) %collective-permute-start.29) | collective-permute-done | bytes 2228256 | tf_op jit(solution)/shard_map/ppermute | solution.py:67
  637.4 26.2 %collective-permute-done.35 = bf16[512,1024]{1,0:T(8,128)(2,1)} collective-permute-done((bf16[512,1024]{1,0:T(8,128)(2,1)}, bf16[512,1024]{1,0:T(8,128)(2,1)}, u32[]{:S(2)}, u32[]{:S(2)}) %collective-permute-start.35) | collective-permute-done | bytes 1048608 | tf_op jit(solution)/shard_map/ppermute | solution.py:457
  666.0 20.0 %shard_map.239 = (bf16[1024,512]{1,0:T(8,128)(2,1)S(1)}, bf16[1024,256]{1,0:T(8,128)(2,1)S(1)}, bf16[1024,256]{1,0:T(8,128)(2,1)S(1)}) custom-call(s32[1]{0:T(128)} %copy.137.length_ref, bf16[1024,512]{1,0:T(8,128)(2,1)S(1)} %copy-done.9, bf16[1024,256]{1,0:T(8,128)(2,1)S(1)} %copy-done.15, bf16[1024,256]{1,0:T(8,128)(2,1)S(1)} %copy-done.17, ...), custom_call_target="tpu_custom_call" | custom-call | flops 20000000000 | bytes 10485760 | tf_op jit(solution)/shard_map/pallas_call | solution.py:206
  687.1 11.7 %collective-permute-start.44 = (bf16[512,1024]{1,0:T(8,128)(2,1)S(1)}, bf16[512,1024]{1,0:T(8,128)(2,1)S(1)}, u32[]{:S(2)}, u32[]{:S(2)}) collective-permute-start(bf16[512,1024]{1,0:T(8,128)(2,1)S(1)} %add_convert_fusion.19), channel_id=1, source_target_pairs={{0,16},{2,18},{4,20},{6,22},{8,24},{10,26},{12,28},{14,30},{16,0},... | collective-permute-start | bytes 3145736 | tf_op jit(solution)/shard_map/ppermute | solution.py:457
  706.7 20.4 %shard_map.240 = (bf16[1024,512]{1,0:T(8,128)(2,1)S(1)}, bf16[1024,256]{1,0:T(8,128)(2,1)S(1)}, bf16[1024,256]{1,0:T(8,128)(2,1)S(1)}) custom-call(s32[1]{0:T(128)} %copy.137.length_ref, bf16[1024,512]{1,0:T(8,128)(2,1)S(1)} %copy-done.7, bf16[1024,256]{1,0:T(8,128)(2,1)S(1)} %copy-done.11, bf16[1024,256]{1,0:T(8,128)(2,1)S(1)} %copy-done.13, ...), custom_call_target="tpu_custom_call" | custom-call | flops 20000000000 | bytes 10485760 | tf_op jit(solution)/shard_map/pallas_call | solution.py:206
  734.1 9.0 %collective-permute-done.44 = bf16[512,1024]{1,0:T(8,128)(2,1)S(1)} collective-permute-done((bf16[512,1024]{1,0:T(8,128)(2,1)S(1)}, bf16[512,1024]{1,0:T(8,128)(2,1)S(1)}, u32[]{:S(2)}, u32[]{:S(2)}) %collective-permute-start.44) | collective-permute-done | bytes 1048608 | tf_op jit(solution)/shard_map/ppermute | solution.py:457
  754.0 8.4 fusion.40
  805.4 14.5 %collective-permute-done.54 = bf16[512,1024]{1,0:T(8,128)(2,1)S(1)} collective-permute-done((bf16[512,1024]{1,0:T(8,128)(2,1)S(1)}, bf16[512,1024]{1,0:T(8,128)(2,1)S(1)}, u32[]{:S(2)}, u32[]{:S(2)}) %collective-permute-start.54) | collective-permute-done | bytes 1048608 | tf_op jit(solution)/shard_map/ppermute | solution.py:584
  826.9 15.7 %collective-permute-done.42 = bf16[1024,1024]{1,0:T(8,128)(2,1)} collective-permute-done((bf16[1024,1024]{1,0:T(8,128)(2,1)S(1)}, bf16[1024,1024]{1,0:T(8,128)(2,1)}, u32[]{:S(2)}, u32[]{:S(2)}) %collective-permute-start.42) | collective-permute-done | bytes 2097184 | tf_op jit(solution)/shard_map/ppermute | solution.py:67
  (460 shorter events, 283.7 us)
Async XLA Ops:
  7.2 60.3 %all-gather.3.cloned.1.call-start = ((), (), s32[]{:S(2)}) async-start(), calls=%async_computation.2 | async-start | bytes 4456448 | tf_op jit(solution)/shard_map/all_gather | solution.py:451
  9.1 159.4 %all-gather.5.cloned.1.call-start = ((), (), s32[]{:S(2)}) async-start(), calls=%async_computation.3 | async-start | bytes 2228224 | tf_op jit(solution)/shard_map/all_gather | solution.py:453
  17.6 45.5 %collective-permute-start.8 = (bf16[1056,1024]{1,0:T(8,128)(2,1)}, bf16[1056,1024]{1,0:T(8,128)(2,1)}, u32[]{:S(2)}, u32[]{:S(2)}) collective-permute-start(bf16[1056,1024]{1,0:T(8,128)(2,1)} %pad_maximum_fusion.1.slope_a.mask_a), channel_id=1, source_target_pairs={{0,2},{2,0},{4,6},{6,4},{5,7},{7,5},{1,3},{3,1},{8,10},{10,8},{12,... | collective-permute-start | bytes 6488072 | tf_op jit(solution)/shard_map/ppermute | solution.py:70
  80.1 112.4 %collective-permute-start.10 = (bf16[1056,1024]{1,0:T(8,128)(2,1)}, bf16[1056,1024]{1,0:T(8,128)(2,1)}, u32[]{:S(2)}, u32[]{:S(2)}) collective-permute-start(bf16[1056,1024]{1,0:T(8,128)(2,1)} %collective-permute-done.1.slope_a.mask_a), channel_id=1, source_target_pairs={{0,2},{2,0},{4,6},{6,4},{5,7},{7,5},{1,3},{3,1},{8,10},{10,8},{12,... | collective-permute-start | bytes 6488072 | tf_op jit(solution)/shard_map/ppermute | solution.py:70
  82.6 51.3 %collective-permute-start.3 = (bf16[1024,512]{1,0:T(8,128)(2,1)}, bf16[1024,512]{1,0:T(8,128)(2,1)}, u32[]{:S(2)}, u32[]{:S(2)}) collective-permute-start(bf16[1024,512]{1,0:T(8,128)(2,1)} %get-tuple-element.252.rest_0_), channel_id=1, source_target_pairs={{0,8},{2,10},{4,12},{6,14},{8,0},{10,2},{12,4},{14,6},{16,24},{18,... | collective-permute-start | bytes 3145736 | tf_op jit(solution)/shard_map/ppermute | solution.py:457
  83.9 70.9 %collective-permute-start.5 = (bf16[1024,512]{1,0:T(8,128)(2,1)}, bf16[1024,512]{1,0:T(8,128)(2,1)}, u32[]{:S(2)}, u32[]{:S(2)}) collective-permute-start(bf16[1024,512]{1,0:T(8,128)(2,1)} %get-tuple-element.252.rest_0_), channel_id=1, source_target_pairs={{0,16},{2,18},{4,20},{6,22},{8,24},{10,26},{12,28},{14,30},{16,0},... | collective-permute-start | bytes 3145736 | tf_op jit(solution)/shard_map/ppermute | solution.py:457
  86.9 761.7 %reduce-scatter.3.cloned.1.call-start = ((), (), s32[]{:S(2)}) async-start(), calls=%async_computation.4 | async-start | bytes 2228224 | tf_op jit(solution)/shard_map/reduce_scatter | solution.py:698
  112.0 90.3 %collective-permute-start.11 = (bf16[1056,1024]{1,0:T(8,128)(2,1)}, bf16[1056,1024]{1,0:T(8,128)(2,1)}, u32[]{:S(2)}, u32[]{:S(2)}) collective-permute-start(bf16[1056,1024]{1,0:T(8,128)(2,1)} %collective-permute-done.2.slope_a.mask_a), channel_id=1, source_target_pairs={{0,2},{2,0},{4,6},{6,4},{5,7},{7,5},{1,3},{3,1},{8,10},{10,8},{12,... | collective-permute-start | bytes 6488072 | tf_op jit(solution)/shard_map/ppermute | solution.py:70
  195.5 52.9 %collective-permute-start.15 = (bf16[1024,512]{1,0:T(8,128)(2,1)}, bf16[1024,512]{1,0:T(8,128)(2,1)}, u32[]{:S(2)}, u32[]{:S(2)}) collective-permute-start(bf16[1024,512]{1,0:T(8,128)(2,1)} %get-tuple-element.253.rest_1_), channel_id=1, source_target_pairs={{0,16},{2,18},{4,20},{6,22},{8,24},{10,26},{12,28},{14,30},{16,0},... | collective-permute-start | bytes 3145736 | tf_op jit(solution)/shard_map/ppermute | solution.py:457
  197.1 51.3 %collective-permute-start.16 = (bf16[1024,512]{1,0:T(8,128)(2,1)}, bf16[1024,512]{1,0:T(8,128)(2,1)}, u32[]{:S(2)}, u32[]{:S(2)}) collective-permute-start(bf16[1024,512]{1,0:T(8,128)(2,1)} %collective-permute-done.5.rest_0_), channel_id=1, source_target_pairs={{0,8},{2,10},{4,12},{6,14},{8,0},{10,2},{12,4},{14,6},{16,24},{18,... | collective-permute-start | bytes 3145736 | tf_op jit(solution)/shard_map/ppermute | solution.py:457
  202.3 87.1 %collective-permute-start.18 = (bf16[512,1024]{1,0:T(8,128)(2,1)}, bf16[512,1024]{1,0:T(8,128)(2,1)}, u32[]{:S(2)}, u32[]{:S(2)}) collective-permute-start(bf16[512,1024]{1,0:T(8,128)(2,1)} %dynamic-slice_bitcast_fusion.rest_2_), channel_id=1, source_target_pairs={{0,16},{2,18},{4,20},{6,22},{8,24},{10,26},{12,28},{14,30},{16,0},... | collective-permute-start | bytes 3145736 | tf_op jit(solution)/shard_map/ppermute | solution.py:457
  248.4 48.1 %collective-permute-start.19 = (bf16[1024,512]{1,0:T(8,128)(2,1)}, bf16[1024,512]{1,0:T(8,128)(2,1)}, u32[]{:S(2)}, u32[]{:S(2)}) collective-permute-start(bf16[1024,512]{1,0:T(8,128)(2,1)} %collective-permute-done.15.rest_1_), channel_id=1, source_target_pairs={{0,8},{2,10},{4,12},{6,14},{8,0},{10,2},{12,4},{14,6},{16,24},{18,... | collective-permute-start | bytes 3145736 | tf_op jit(solution)/shard_map/ppermute | solution.py:457
  249.1 47.4 %collective-permute-start.20 = (bf16[1024,1024]{1,0:T(8,128)(2,1)}, bf16[1024,1024]{1,0:T(8,128)(2,1)}, u32[]{:S(2)}, u32[]{:S(2)}) collective-permute-start(bf16[1024,1024]{1,0:T(8,128)(2,1)} %collective-permute-done.13.tokens_a), channel_id=1, source_target_pairs={{0,2},{2,0},{4,6},{6,4},{5,7},{7,5},{1,3},{3,1},{8,10},{10,8},{12,... | collective-permute-start | bytes 6291464 | tf_op jit(solution)/shard_map/ppermute | solution.py:70
  296.5 68.6 %collective-permute-start.14 = (bf16[1024,1024]{1,0:T(8,128)(2,1)}, bf16[1024,1024]{1,0:T(8,128)(2,1)}, u32[]{:S(2)}, u32[]{:S(2)}) collective-permute-start(bf16[1024,1024]{1,0:T(8,128)(2,1)} %collective-permute-done.13.tokens_a), channel_id=1, source_target_pairs={{0,4},{6,2},{4,5},{7,6},{5,1},{3,7},{1,0},{2,3},{8,12},{14,10},{12... | collective-permute-start | bytes 6291464 | tf_op jit(solution)/shard_map/ppermute | solution.py:67
  399.2 79.5 %collective-permute-start.26 = (bf16[1088,1024]{1,0:T(8,128)(2,1)}, bf16[1088,1024]{1,0:T(8,128)(2,1)}, u32[]{:S(2)}, u32[]{:S(2)}) collective-permute-start(bf16[1088,1024]{1,0:T(8,128)(2,1)} %add_convert_fusion.3), channel_id=1, source_target_pairs={{0,2},{2,0},{4,6},{6,4},{5,7},{7,5},{1,3},{3,1},{8,10},{10,8},{12,... | collective-permute-start | bytes 6684680 | tf_op jit(solution)/shard_map/ppermute | solution.py:70
  494.3 46.2 %collective-permute-start.30 = (bf16[512,1024]{1,0:T(8,128)(2,1)}, bf16[512,1024]{1,0:T(8,128)(2,1)}, u32[]{:S(2)}, u32[]{:S(2)}) collective-permute-start(bf16[512,1024]{1,0:T(8,128)(2,1)} %get-tuple-element.332), channel_id=1, source_target_pairs={{0,8},{2,10},{4,12},{6,14},{8,0},{10,2},{12,4},{14,6},{16,24},{18,... | collective-permute-start | bytes 3145736 | tf_op jit(solution)/shard_map/ppermute | solution.py:457
  496.0 86.4 %collective-permute-start.31 = (bf16[512,1024]{1,0:T(8,128)(2,1)}, bf16[512,1024]{1,0:T(8,128)(2,1)}, u32[]{:S(2)}, u32[]{:S(2)}) collective-permute-start(bf16[512,1024]{1,0:T(8,128)(2,1)} %get-tuple-element.337), channel_id=1, source_target_pairs={{0,8},{2,10},{4,12},{6,14},{8,0},{10,2},{12,4},{14,6},{16,24},{18,... | collective-permute-start | bytes 3145736 | tf_op jit(solution)/shard_map/ppermute | solution.py:457
  496.3 86.1 %collective-permute-start.32 = (bf16[512,1024]{1,0:T(8,128)(2,1)}, bf16[512,1024]{1,0:T(8,128)(2,1)}, u32[]{:S(2)}, u32[]{:S(2)}) collective-permute-start(bf16[512,1024]{1,0:T(8,128)(2,1)} %fusion.85), channel_id=1, source_target_pairs={{0,8},{2,10},{4,12},{6,14},{8,0},{10,2},{12,4},{14,6},{16,24},{18,... | collective-permute-start | bytes 3145736 | tf_op jit(solution)/shard_map/ppermute | solution.py:457
  500.5 92.0 %collective-permute-start.25 = (bf16[1088,1024]{1,0:T(8,128)(2,1)}, bf16[1088,1024]{1,0:T(8,128)(2,1)}, u32[]{:S(2)}, u32[]{:S(2)}) collective-permute-start(bf16[1088,1024]{1,0:T(8,128)(2,1)} %add_convert_fusion.4), channel_id=1, source_target_pairs={{0,2},{2,0},{4,6},{6,4},{5,7},{7,5},{1,3},{3,1},{8,10},{10,8},{12,... | collective-permute-start | bytes 6684680 | tf_op jit(solution)/shard_map/ppermute | solution.py:70
  568.9 137.7 %collective-permute-start.39 = (bf16[512,1024]{1,0:T(8,128)(2,1)}, bf16[512,1024]{1,0:T(8,128)(2,1)}, u32[]{:S(2)}, u32[]{:S(2)}) collective-permute-start(bf16[512,1024]{1,0:T(8,128)(2,1)} %add_convert_fusion.20), channel_id=1, source_target_pairs={{0,16},{2,18},{4,20},{6,22},{8,24},{10,26},{12,28},{14,30},{16,0},... | collective-permute-start | bytes 3145736 | tf_op jit(solution)/shard_map/ppermute | solution.py:457
  611.6 153.6 %collective-permute-start.45 = (bf16[512,1024]{1,0:T(8,128)(2,1)}, bf16[512,1024]{1,0:T(8,128)(2,1)}, u32[]{:S(2)}, u32[]{:S(2)}) collective-permute-start(bf16[512,1024]{1,0:T(8,128)(2,1)} %add_convert_fusion.18), channel_id=1, source_target_pairs={{0,16},{2,18},{4,20},{6,22},{8,24},{10,26},{12,28},{14,30},{16,0},... | collective-permute-start | bytes 3145736 | tf_op jit(solution)/shard_map/ppermute | solution.py:457
  613.9 88.7 %collective-permute-start.40 = (bf16[1024,1024]{1,0:T(8,128)(2,1)}, bf16[1024,1024]{1,0:T(8,128)(2,1)}, u32[]{:S(2)}, u32[]{:S(2)}) collective-permute-start(bf16[1024,1024]{1,0:T(8,128)(2,1)} %add_convert_fusion.10), channel_id=1, source_target_pairs={{0,2},{2,0},{4,6},{6,4},{5,7},{7,5},{1,3},{3,1},{8,10},{10,8},{12,... | collective-permute-start | bytes 6291464 | tf_op jit(solution)/shard_map/ppermute | solution.py:70
  614.4 49.1 %collective-permute-start.35 = (bf16[512,1024]{1,0:T(8,128)(2,1)}, bf16[512,1024]{1,0:T(8,128)(2,1)}, u32[]{:S(2)}, u32[]{:S(2)}) collective-permute-start(bf16[512,1024]{1,0:T(8,128)(2,1)} %get-tuple-element.358), channel_id=1, source_target_pairs={{0,8},{2,10},{4,12},{6,14},{8,0},{10,2},{12,4},{14,6},{16,24},{18,... | collective-permute-start | bytes 3145736 | tf_op jit(solution)/shard_map/ppermute | solution.py:457
  621.5 227.0 %reduce-scatter.5.cloned.1.call-start = ((), (), s32[]{:S(2)}) async-start(), calls=%async_computation.5 | async-start | bytes 4456448 | tf_op jit(solution)/shard_map/reduce_scatter | solution.py:736
  634.3 52.8 %collective-permute-start.37 = (bf16[1024,1024]{1,0:T(8,128)(2,1)S(1)}, bf16[1024,1024]{1,0:T(8,128)(2,1)S(1)}, u32[]{:S(2)}, u32[]{:S(2)}) collective-permute-start(bf16[1024,1024]{1,0:T(8,128)(2,1)S(1)} %add_convert_fusion.11), channel_id=1, source_target_pairs={{0,4},{6,2},{4,5},{7,6},{5,1},{3,7},{1,0},{2,3},{8,12},{14,10},{12... | collective-permute-start | bytes 6291464 | tf_op jit(solution)/shard_map/ppermute | solution.py:67
  687.1 56.0 %collective-permute-start.44 = (bf16[512,1024]{1,0:T(8,128)(2,1)S(1)}, bf16[512,1024]{1,0:T(8,128)(2,1)S(1)}, u32[]{:S(2)}, u32[]{:S(2)}) collective-permute-start(bf16[512,1024]{1,0:T(8,128)(2,1)S(1)} %add_convert_fusion.19), channel_id=1, source_target_pairs={{0,16},{2,18},{4,20},{6,22},{8,24},{10,26},{12,28},{14,30},{16,0},... | collective-permute-start | bytes 3145736 | tf_op jit(solution)/shard_map/ppermute | solution.py:457
  702.6 42.5 %collective-permute-start.43 = (bf16[512,1024]{1,0:T(8,128)(2,1)S(1)}, bf16[512,1024]{1,0:T(8,128)(2,1)S(1)}, u32[]{:S(2)}, u32[]{:S(2)}) collective-permute-start(bf16[512,1024]{1,0:T(8,128)(2,1)S(1)} %copy-done.104), channel_id=1, source_target_pairs={{0,8},{2,10},{4,12},{6,14},{8,0},{10,2},{12,4},{14,6},{16,24},{18,... | collective-permute-start | bytes 3145736 | tf_op jit(solution)/shard_map/ppermute | solution.py:457
  702.6 124.3 %collective-permute-start.33 = (bf16[1024,1024]{1,0:T(8,128)(2,1)}, bf16[1024,1024]{1,0:T(8,128)(2,1)}, u32[]{:S(2)}, u32[]{:S(2)}) collective-permute-start(bf16[1024,1024]{1,0:T(8,128)(2,1)} %add_convert_fusion.14), channel_id=1, source_target_pairs={{0,2},{2,0},{4,6},{6,4},{5,7},{7,5},{1,3},{3,1},{8,10},{10,8},{12,... | collective-permute-start | bytes 6291464 | tf_op jit(solution)/shard_map/ppermute | solution.py:70
  733.8 46.6 %collective-permute-start.34 = (bf16[1024,1024]{1,0:T(8,128)(2,1)}, bf16[1024,1024]{1,0:T(8,128)(2,1)}, u32[]{:S(2)}, u32[]{:S(2)}) collective-permute-start(bf16[1024,1024]{1,0:T(8,128)(2,1)} %add_convert_fusion.13), channel_id=1, source_target_pairs={{0,2},{2,0},{4,6},{6,4},{5,7},{7,5},{1,3},{3,1},{8,10},{10,8},{12,... | collective-permute-start | bytes 6291464 | tf_op jit(solution)/shard_map/ppermute | solution.py:70
  743.0 47.6 %collective-permute-start.53 = (bf16[512,1024]{1,0:T(8,128)(2,1)S(1)}, bf16[512,1024]{1,0:T(8,128)(2,1)}, u32[]{:S(2)}, u32[]{:S(2)}) collective-permute-start(bf16[512,1024]{1,0:T(8,128)(2,1)S(1)} %add_convert_fusion.17), channel_id=1, source_target_pairs={{0,1},{1,0},{2,3},{3,2},{4,5},{5,4},{6,7},{7,6},{8,9},{9,8},{10,11... | collective-permute-start | bytes 3145736 | tf_op jit(solution)/shard_map/ppermute | solution.py:584
  778.7 41.3 %collective-permute-start.54 = (bf16[512,1024]{1,0:T(8,128)(2,1)S(1)}, bf16[512,1024]{1,0:T(8,128)(2,1)S(1)}, u32[]{:S(2)}, u32[]{:S(2)}) collective-permute-start(bf16[512,1024]{1,0:T(8,128)(2,1)S(1)} %add_convert_fusion.16), channel_id=1, source_target_pairs={{0,1},{1,0},{2,3},{3,2},{4,5},{5,4},{6,7},{7,6},{8,9},{9,8},{10,11... | collective-permute-start | bytes 3145736 | tf_op jit(solution)/shard_map/ppermute | solution.py:584
  790.6 51.9 %collective-permute-start.42 = (bf16[1024,1024]{1,0:T(8,128)(2,1)S(1)}, bf16[1024,1024]{1,0:T(8,128)(2,1)}, u32[]{:S(2)}, u32[]{:S(2)}) collective-permute-start(bf16[1024,1024]{1,0:T(8,128)(2,1)S(1)} %add_convert_fusion.8), channel_id=1, source_target_pairs={{0,4},{6,2},{4,5},{7,6},{5,1},{3,7},{1,0},{2,3},{8,12},{14,10},{12... | collective-permute-start | bytes 6291464 | tf_op jit(solution)/shard_map/ppermute | solution.py:67
  (147 other events, 3524.4 us)
Sparse Core Ops, SparseCore 0:
  10.8 55.8 all-gather.2
  87.0 73.2 all-gather.4
  621.7 71.3 reduce-scatter.2
  752.6 79.0 reduce-scatter.4

commit v5 on v4

--- a/solution.py
+++ b/solution.py
@@ -526,9 +526,7 @@
 
     across_three = []
     if layered:
-        normed_two, next_one[2], across_two[0], own = barrier(
-            (normed_two, next_one[2], across_two[0], own)
-        )
+        normed_two, across_two[0], own = barrier((normed_two, across_two[0], own))
         across_two.append(layer_swap(own[2], 2))
         across_three.append(layer_swap(across_two[0], 1))
 
@@ -708,9 +706,10 @@
                 mix = mix_hop(mix_step, mix)
                 mix_step += 1
         if layered:
-            attended_slope, next_sum[part] = barrier((attended_slope, next_sum[part]))
             if part == 1:
-                attended_slope, two_sum[0] = barrier((attended_slope, two_sum[0]))
+                attended_slope, two_sum[0], next_sum[0] = barrier(
+                    (attended_slope, two_sum[0], next_sum[0])
+                )
                 finish(0)
         queries, keys, values, _, log_totals = heads[part]
         slopes_out.append(
@@ -725,7 +724,7 @@
     )
     pre_slopes, mix = barrier((pre_slopes, mix))
     if layered:
-        pre_slopes, next_sum[2], two_sum[1] = barrier((pre_slopes, next_sum[2], two_sum[1]))
+        pre_slopes, next_sum[1], two_sum[1] = barrier((pre_slopes, next_sum[1], two_sum[1]))
         finish(1)
     while mix_step < ring.steps:
         mix = mix_hop(mix_step, mix)
@@ -759,7 +758,9 @@
     )
     input_gradient = input_slope.astype(bf16)
     if layered:
-        input_gradient, two_sum[2] = barrier((input_gradient, two_sum[2]))
+        input_gradient, two_sum[2], next_sum[2], mix = barrier(
+            (input_gradient, two_sum[2], next_sum[2], mix)
+        )
         finish(2)
     layer_output = (residual + ring.part_sum(*mix_parts[0], mix)).astype(bf16)
 

time: 874 us -> 869 us (level)
  starting transfers between devices: 62.2 us -> 51.9 us
    ppermute x12, waiting for transfers between devices: 87.2 us -> 50.3 us  [hop(): return lax.ppermute(array, ('shard', 'rep'), self.forward)]
    ppermute x5, waiting for transfers between devices: 22.8 us -> 38.8 us  [on_device(): lax.ppermute(gain_sum, axis, [(place, place ^ far_bit) for place in range...]
    ppermute x5, waiting for transfers between devices: 19.3 us -> 30.8 us  [across(): return lax.ppermute(array, 'rep', [(0, 1), (1, 0)])]
    unnamed x251 -> x231, local copies, waits for them, and re-layouts: 26.3 us -> 28.6 us
  transfers between devices with their start and end apart: 60 -> 60, of which waited for: 22 -> 21; matrix products, arithmetic and copies ran while one was open for 26% -> 23% of each run, Pallas kernels for 36% -> 36%
where the time goes in v5:
time: 869 us; the launch traced here: 863 us
  Pallas kernels  311 us (36%)
  waiting for transfers between devices  242 us (28%)
  other arithmetic  96.5 us (11%)
  matrix products  91.1 us (10%)
  local copies, waits for them, and re-layouts  54.6 us (6%)
  starting transfers between devices  51.9 us (6%)
  between operations  16.8 us (2%)
    pallas_call x8, Pallas kernels, experts_pair(): pl.pallas_call(functools.partial(pair_kernel, count, step, chained), out_...  231 us
    ppermute x18, waiting for transfers between devices, layer_swap(): lax.ppermute(array, 'shard', [(s, s ^ stride) for s in range(shards)])  115 us
    ppermute x12, waiting for transfers between devices, hop(): return lax.ppermute(array, ('shard', 'rep'), self.forward)  50.3 us
    pallas_call x2, Pallas kernels, attention_backward(): pl.pallas_call(functools.partial(backward_kernel, block), out_shape=[jax....  40.7 us
    ppermute x5, waiting for transfers between devices, on_device(): lax.ppermute(gain_sum, axis, [(place, place ^ far_bit) for place in range...  38.8 us
    pallas_call x2, Pallas kernels, attention_forward(): pl.pallas_call(functools.partial(forward_kernel, block), out_shape=[jax.S...  38.8 us
    dot_general x4, matrix products, expert_grads(): lax.dot_general(rows[e], slopes[e], turned, preferred_element_type=f32)  34 us
    ppermute x5, waiting for transfers between devices, across(): return lax.ppermute(array, 'rep', [(0, 1), (1, 0)])  30.8 us
  transfers between devices with their start and end apart: 60, of which 21 were waited for; matrix products, arithmetic and copies ran while one was open for 23% of the time, Pallas kernels for 36%

profile of v5, /device:TPU:0, one launch (start us, length us, event | category | flops | bytes accessed | tf_op | source)
XLA Modules:
  0.0 863.3 jit_solution(15335977309099426976)
XLA Ops:
  20.0 32.3 %collective-permute-done.slope_a.mask_a = bf16[1056,1024]{1,0:T(8,128)(2,1)} collective-permute-done((bf16[1056,1024]{1,0:T(8,128)(2,1)}, bf16[1056,1024]{1,0:T(8,128)(2,1)}, u32[]{:S(2)}, u32[]{:S(2)}) %collective-permute-start) | collective-permute-done | bytes 2162720 | tf_op jit(solution)/shard_map/ppermute | solution.py:67
  69.4 10.0 %collective-permute-done.1.slope_a.mask_a = bf16[1056,1024]{1,0:T(8,128)(2,1)} collective-permute-done((bf16[1056,1024]{1,0:T(8,128)(2,1)}, bf16[1056,1024]{1,0:T(8,128)(2,1)}, u32[]{:S(2)}, u32[]{:S(2)}) %collective-permute-start.1) | collective-permute-done | bytes 2162720 | tf_op jit(solution)/shard_map/ppermute | solution.py:67
  88.5 19.2 %shard_map.229 = (bf16[1024,512]{1,0:T(8,128)(2,1)S(1)}, bf16[1024,256]{1,0:T(8,128)(2,1)S(1)}, bf16[1024,256]{1,0:T(8,128)(2,1)S(1)}, bf16[1024,512]{1,0:T(8,128)(2,1)S(1)}, f32[2,4,1024]{2,1,0:T(4,128)S(1)}) custom-call(s32[1]{0:T(128)} %copy.137.length_ref, bf16[1024,1024]{1,0:T(8,128)(2,1)S(1)} %copy-done.2, bf16[1024,2048]{1,0:T(8,128)(2,1)S(1)} %copy-done.3, ...), custom_call_target="tpu_custom_call" | custom-call | flops 30000001024 | bytes 20971520 | tf_op jit(solution)/shard_map/pallas_call | solution.py:146
  112.0 27.9 %collective-permute-done.3.rest_3_ = bf16[1024,512]{1,0:T(8,128)(2,1)} collective-permute-done((bf16[1024,512]{1,0:T(8,128)(2,1)}, bf16[1024,512]{1,0:T(8,128)(2,1)}, u32[]{:S(2)}, u32[]{:S(2)}) %collective-permute-start.3) | collective-permute-done | bytes 1048608 | tf_op jit(solution)/shard_map/ppermute | solution.py:457
  142.4 19.6 %shard_map.230 = (bf16[1024,512]{1,0:T(8,128)(2,1)S(1)}, bf16[1024,256]{1,0:T(8,128)(2,1)S(1)}, bf16[1024,256]{1,0:T(8,128)(2,1)S(1)}, bf16[1024,512]{1,0:T(8,128)(2,1)S(1)}, f32[2,4,1024]{2,1,0:T(4,128)S(1)}) custom-call(s32[1]{0:T(128)} %copy.137.length_ref, bf16[1024,1024]{1,0:T(8,128)(2,1)S(1)} %copy-done.2, bf16[1024,2048]{1,0:T(8,128)(2,1)S(1)} %copy-done.4, ...), custom_call_target="tpu_custom_call" | custom-call | flops 30000001024 | bytes 20971520 | tf_op jit(solution)/shard_map/pallas_call | solution.py:146
  194.7 35.0 %collective-permute-done.11.rest_5_ = bf16[512,1024]{1,0:T(8,128)(2,1)} collective-permute-done((bf16[512,1024]{1,0:T(8,128)(2,1)}, bf16[512,1024]{1,0:T(8,128)(2,1)}, u32[]{:S(2)}, u32[]{:S(2)}) %collective-permute-start.11) | collective-permute-done | bytes 1048608 | tf_op jit(solution)/shard_map/ppermute | solution.py:457
  235.1 28.7 %shard_map.231 = (bf16[1088,1024]{1,0:T(8,128)(2,1)}, bf16[1088,1024]{1,0:T(8,128)(2,1)}, bf16[1024,1024]{1,0:T(8,128)(2,1)}, bf16[1024,1024]{1,0:T(8,128)(2,1)}...) custom-call(s32[2]{0:T(128)} %pad_add_fusion.ids_ref, ...), custom_call_target="tpu_custom_call" | custom-call | flops 33822867456 | bytes 41943040 | tf_op jit(solution)/shard_map/pallas_call | solution.py:387
  263.8 13.6 %collective-permute-done.16.rest_3_ = bf16[1024,512]{1,0:T(8,128)(2,1)} collective-permute-done((bf16[1024,512]{1,0:T(8,128)(2,1)}, bf16[1024,512]{1,0:T(8,128)(2,1)}, u32[]{:S(2)}, u32[]{:S(2)}) %collective-permute-start.16) | collective-permute-done | bytes 1048608 | tf_op jit(solution)/shard_map/ppermute | solution.py:457
  277.5 29.2 %shard_map.232 = (bf16[1088,1024]{1,0:T(8,128)(2,1)}, bf16[1088,1024]{1,0:T(8,128)(2,1)}, bf16[1024,1024]{1,0:T(8,128)(2,1)}, bf16[1024,1024]{1,0:T(8,128)(2,1)}...) custom-call(s32[2]{0:T(128)} %pad_add_fusion.ids_ref, ...), custom_call_target="tpu_custom_call", output_to_operand_aliasing={{4}: (16, {}), {5}: (17, {}), {6}: (18, {}), {7}: (19, {})} | custom-call | flops 33822867456 | bytes 41943040 | tf_op jit(solution)/shard_map/pallas_call | solution.py:387
  310.5 29.0 %shard_map.233 = (bf16[1088,1024]{1,0:T(8,128)(2,1)}, bf16[1088,1024]{1,0:T(8,128)(2,1)}, bf16[1024,1024]{1,0:T(8,128)(2,1)}, bf16[1024,1024]{1,0:T(8,128)(2,1)}...) custom-call(s32[2]{0:T(128)} %pad_add_fusion.ids_ref, ...), custom_call_target="tpu_custom_call", output_to_operand_aliasing={{4}: (16, {}), {5}: (17, {}), {6}: (18, {}), {7}: (19, {})} | custom-call | flops 33822867456 | bytes 41943040 | tf_op jit(solution)/shard_map/pallas_call | solution.py:387
  339.5 28.9 %shard_map.234 = (bf16[1088,1024]{1,0:T(8,128)(2,1)}, bf16[1088,1024]{1,0:T(8,128)(2,1)}, bf16[1024,1024]{1,0:T(8,128)(2,1)}, bf16[1024,1024]{1,0:T(8,128)(2,1)}...) custom-call(s32[2]{0:T(128)} %pad_add_fusion.2.ids_ref, ...), custom_call_target="tpu_custom_call" | custom-call | flops 33822867456 | bytes 41943040 | tf_op jit(solution)/shard_map/pallas_call | solution.py:387
  373.7 29.0 %shard_map.235 = (bf16[1088,1024]{1,0:T(8,128)(2,1)}, bf16[1088,1024]{1,0:T(8,128)(2,1)}, bf16[1024,1024]{1,0:T(8,128)(2,1)}, bf16[1024,1024]{1,0:T(8,128)(2,1)}...) custom-call(s32[2]{0:T(128)} %pad_add_fusion.2.ids_ref, ...), custom_call_target="tpu_custom_call", output_to_operand_aliasing={{4}: (16, {}), {5}: (17, {}), {6}: (18, {}), {7}: (19, {})} | custom-call | flops 33822867456 | bytes 41943040 | tf_op jit(solution)/shard_map/pallas_call | solution.py:387
  412.8 28.8 %shard_map.236 = (bf16[1088,1024]{1,0:T(8,128)(2,1)}, bf16[1088,1024]{1,0:T(8,128)(2,1)}, bf16[1024,1024]{1,0:T(8,128)(2,1)}, bf16[1024,1024]{1,0:T(8,128)(2,1)}...) custom-call(s32[2]{0:T(128)} %pad_add_fusion.2.ids_ref, ...), custom_call_target="tpu_custom_call", output_to_operand_aliasing={{4}: (16, {}), {5}: (17, {}), {6}: (18, {}), {7}: (19, {})} | custom-call | flops 33822867456 | bytes 41943040 | tf_op jit(solution)/shard_map/pallas_call | solution.py:387
  441.6 7.1 add_convert_fusion.2
  450.7 28.7 %shard_map.237 = (bf16[1088,1024]{1,0:T(8,128)(2,1)}, bf16[1088,1024]{1,0:T(8,128)(2,1)}, bf16[1024,1024]{1,0:T(8,128)(2,1)}, bf16[1024,1024]{1,0:T(8,128)(2,1)}...) custom-call(s32[2]{0:T(128)} %pad_add_fusion.2.ids_ref, ...), custom_call_target="tpu_custom_call", output_to_operand_aliasing={{4}: (16, {}), {5}: (17, {}), {6}: (18, {}), {7}: (19, {})} | custom-call | flops 33822867456 | bytes 41943040 | tf_op jit(solution)/shard_map/pallas_call | solution.py:387
  479.5 8.5 fusion.65
  488.0 8.4 fusion.60
  507.0 28.9 %shard_map.238 = (bf16[1088,1024]{1,0:T(8,128)(2,1)}, bf16[1088,1024]{1,0:T(8,128)(2,1)}, bf16[1024,1024]{1,0:T(8,128)(2,1)}, bf16[1024,1024]{1,0:T(8,128)(2,1)}...) custom-call(s32[2]{0:T(128)} %pad_add_fusion.ids_ref, ...), custom_call_target="tpu_custom_call", output_to_operand_aliasing={{4}: (16, {}), {5}: (17, {}), {6}: (18, {}), {7}: (19, {})} | custom-call | flops 33822867456 | bytes 41943040 | tf_op jit(solution)/shard_map/pallas_call | solution.py:387
  545.7 8.5 fusion.75
  558.7 8.6 fusion.70
  567.3 6.1 fusion.95
  582.5 8.0 collective-permute-done.32
  615.0 6.5 convolution_convert_fusion.1
  628.7 20.6 %shard_map.239 = (bf16[1024,512]{1,0:T(8,128)(2,1)S(1)}, bf16[1024,256]{1,0:T(8,128)(2,1)S(1)}, bf16[1024,256]{1,0:T(8,128)(2,1)S(1)}) custom-call(s32[1]{0:T(128)} %copy.137.length_ref, bf16[1024,512]{1,0:T(8,128)(2,1)S(1)} %copy-done.9, bf16[1024,256]{1,0:T(8,128)(2,1)S(1)} %copy-done.15, bf16[1024,256]{1,0:T(8,128)(2,1)S(1)} %copy-done.17, ...), custom_call_target="tpu_custom_call" | custom-call | flops 20000000000 | bytes 10485760 | tf_op jit(solution)/shard_map/pallas_call | solution.py:206
  664.5 23.7 %collective-permute-done.37 = bf16[512,1024]{1,0:T(8,128)(2,1)} collective-permute-done((bf16[512,1024]{1,0:T(8,128)(2,1)}, bf16[512,1024]{1,0:T(8,128)(2,1)}, u32[]{:S(2)}, u32[]{:S(2)}) %collective-permute-start.37) | collective-permute-done | bytes 1048608 | tf_op jit(solution)/shard_map/ppermute | solution.py:457
  690.5 20.1 %shard_map.240 = (bf16[1024,512]{1,0:T(8,128)(2,1)S(1)}, bf16[1024,256]{1,0:T(8,128)(2,1)S(1)}, bf16[1024,256]{1,0:T(8,128)(2,1)S(1)}) custom-call(s32[1]{0:T(128)} %copy.137.length_ref, bf16[1024,512]{1,0:T(8,128)(2,1)S(1)} %copy-done.7, bf16[1024,256]{1,0:T(8,128)(2,1)S(1)} %copy-done.11, bf16[1024,256]{1,0:T(8,128)(2,1)S(1)} %copy-done.13, ...), custom_call_target="tpu_custom_call" | custom-call | flops 20000000000 | bytes 10485760 | tf_op jit(solution)/shard_map/pallas_call | solution.py:206
  718.8 6.4 convolution_convert_fusion
  726.8 8.4 fusion.40
  749.5 23.4 %collective-permute-done.48 = f32[34,1024]{1,0:T(8,128)S(1)} collective-permute-done((f32[34,1024]{1,0:T(8,128)S(1)}, f32[34,1024]{1,0:T(8,128)S(1)}, u32[]{:S(2)}, u32[]{:S(2)}) %collective-permute-start.48) | collective-permute-done | bytes 139296 | tf_op jit(solution)/shard_map/ppermute | solution.py:746
  781.4 9.7 %collective-permute-done.50 = f32[34,1024]{1,0:T(8,128)S(1)} collective-permute-done((f32[34,1024]{1,0:T(8,128)S(1)}, f32[34,1024]{1,0:T(8,128)S(1)}, u32[]{:S(2)}, u32[]{:S(2)}) %collective-permute-start.50) | collective-permute-done | bytes 139296 | tf_op jit(solution)/shard_map/ppermute | solution.py:746
  794.2 13.9 %collective-permute-done.54 = bf16[512,1024]{1,0:T(8,128)(2,1)S(1)} collective-permute-done((bf16[512,1024]{1,0:T(8,128)(2,1)S(1)}, bf16[512,1024]{1,0:T(8,128)(2,1)S(1)}, u32[]{:S(2)}, u32[]{:S(2)}) %collective-permute-start.54) | collective-permute-done | bytes 1048608 | tf_op jit(solution)/shard_map/ppermute | solution.py:582
  825.3 11.9 %collective-permute-done.55 = bf16[512,1024]{1,0:T(8,128)(2,1)S(1)} collective-permute-done((bf16[512,1024]{1,0:T(8,128)(2,1)S(1)}, bf16[512,1024]{1,0:T(8,128)(2,1)S(1)}, u32[]{:S(2)}, u32[]{:S(2)}) %collective-permute-start.55) | collective-permute-done | bytes 1048608 | tf_op jit(solution)/shard_map/ppermute | solution.py:582
  (439 shorter events, 257.8 us)
Async XLA Ops:
  7.2 62.2 %all-gather.3.cloned.1.call-start = ((), (), s32[]{:S(2)}) async-start(), calls=%async_computation.2 | async-start | bytes 4456448 | tf_op jit(solution)/shard_map/all_gather | solution.py:451
  9.1 157.3 %all-gather.5.cloned.1.call-start = ((), (), s32[]{:S(2)}) async-start(), calls=%async_computation.3 | async-start | bytes 2228224 | tf_op jit(solution)/shard_map/all_gather | solution.py:453
  17.6 45.6 %collective-permute-start.7 = (bf16[1056,1024]{1,0:T(8,128)(2,1)}, bf16[1056,1024]{1,0:T(8,128)(2,1)}, u32[]{:S(2)}, u32[]{:S(2)}) collective-permute-start(bf16[1056,1024]{1,0:T(8,128)(2,1)} %pad_maximum_fusion.1.slope_a.mask_a), channel_id=1, source_target_pairs={{0,2},{2,0},{4,6},{6,4},{5,7},{7,5},{1,3},{3,1},{8,10},{10,8},{12,... | collective-permute-start | bytes 6488072 | tf_op jit(solution)/shard_map/ppermute | solution.py:70
  63.1 114.3 %collective-permute-start.8 = (bf16[1056,1024]{1,0:T(8,128)(2,1)}, bf16[1056,1024]{1,0:T(8,128)(2,1)}, u32[]{:S(2)}, u32[]{:S(2)}) collective-permute-start(bf16[1056,1024]{1,0:T(8,128)(2,1)} %collective-permute-done.slope_a.mask_a), channel_id=1, source_target_pairs={{0,2},{2,0},{4,6},{6,4},{5,7},{7,5},{1,3},{3,1},{8,10},{10,8},{12,... | collective-permute-start | bytes 6488072 | tf_op jit(solution)/shard_map/ppermute | solution.py:70
  79.4 84.0 %collective-permute-start.5 = (bf16[1024,512]{1,0:T(8,128)(2,1)}, bf16[1024,512]{1,0:T(8,128)(2,1)}, u32[]{:S(2)}, u32[]{:S(2)}) collective-permute-start(bf16[1024,512]{1,0:T(8,128)(2,1)} %get-tuple-element.250.rest_0_), channel_id=1, source_target_pairs={{0,16},{2,18},{4,20},{6,22},{8,24},{10,26},{12,28},{14,30},{16,0},... | collective-permute-start | bytes 3145736 | tf_op jit(solution)/shard_map/ppermute | solution.py:457
  82.0 58.0 %collective-permute-start.3 = (bf16[1024,512]{1,0:T(8,128)(2,1)}, bf16[1024,512]{1,0:T(8,128)(2,1)}, u32[]{:S(2)}, u32[]{:S(2)}) collective-permute-start(bf16[1024,512]{1,0:T(8,128)(2,1)} %get-tuple-element.250.rest_0_), channel_id=1, source_target_pairs={{0,8},{2,10},{4,12},{6,14},{8,0},{10,2},{12,4},{14,6},{16,24},{18,... | collective-permute-start | bytes 3145736 | tf_op jit(solution)/shard_map/ppermute | solution.py:457
  83.5 96.9 %collective-permute-start.9 = (bf16[1056,1024]{1,0:T(8,128)(2,1)}, bf16[1056,1024]{1,0:T(8,128)(2,1)}, u32[]{:S(2)}, u32[]{:S(2)}) collective-permute-start(bf16[1056,1024]{1,0:T(8,128)(2,1)} %collective-permute-done.1.slope_a.mask_a), channel_id=1, source_target_pairs={{0,2},{2,0},{4,6},{6,4},{5,7},{7,5},{1,3},{3,1},{8,10},{10,8},{12,... | collective-permute-start | bytes 6488072 | tf_op jit(solution)/shard_map/ppermute | solution.py:70
  86.0 754.1 %reduce-scatter.3.cloned.1.call-start = ((), (), s32[]{:S(2)}) async-start(), calls=%async_computation.4 | async-start | bytes 2228224 | tf_op jit(solution)/shard_map/reduce_scatter | solution.py:696
  142.4 43.0 %collective-permute-start.10 = (bf16[1056,1024]{1,0:T(8,128)(2,1)}, bf16[1056,1024]{1,0:T(8,128)(2,1)}, u32[]{:S(2)}, u32[]{:S(2)}) collective-permute-start(bf16[1056,1024]{1,0:T(8,128)(2,1)} %collective-permute-done.2.slope_a.mask_a), channel_id=1, source_target_pairs={{0,2},{2,0},{4,6},{6,4},{5,7},{7,5},{1,3},{3,1},{8,10},{10,8},{12,... | collective-permute-start | bytes 6488072 | tf_op jit(solution)/shard_map/ppermute | solution.py:70
  175.4 56.8 %collective-permute-start.12 = (bf16[1024,1024]{1,0:T(8,128)(2,1)}, bf16[1024,1024]{1,0:T(8,128)(2,1)}, u32[]{:S(2)}, u32[]{:S(2)}) collective-permute-start(bf16[1024,1024]{1,0:T(8,128)(2,1)} %multiply_convert_fusion.tokens_a), channel_id=1, source_target_pairs={{0,4},{6,2},{4,5},{7,6},{5,1},{3,7},{1,0},{2,3},{8,12},{14,10},{12... | collective-permute-start | bytes 6291464 | tf_op jit(solution)/shard_map/ppermute | solution.py:67
  177.2 55.0 %collective-permute-start.6 = (bf16[1024,1024]{1,0:T(8,128)(2,1)}, bf16[1024,1024]{1,0:T(8,128)(2,1)}, u32[]{:S(2)}, u32[]{:S(2)}) collective-permute-start(bf16[1024,1024]{1,0:T(8,128)(2,1)} %multiply_convert_fusion.tokens_a), channel_id=1, source_target_pairs={{0,2},{2,0},{4,6},{6,4},{5,7},{7,5},{1,3},{3,1},{8,10},{10,8},{12,... | collective-permute-start | bytes 6291464 | tf_op jit(solution)/shard_map/ppermute | solution.py:70
  183.3 80.4 %collective-permute-start.15 = (bf16[1024,512]{1,0:T(8,128)(2,1)}, bf16[1024,512]{1,0:T(8,128)(2,1)}, u32[]{:S(2)}, u32[]{:S(2)}) collective-permute-start(bf16[1024,512]{1,0:T(8,128)(2,1)} %get-tuple-element.251.rest_1_), channel_id=1, source_target_pairs={{0,16},{2,18},{4,20},{6,22},{8,24},{10,26},{12,28},{14,30},{16,0},... | collective-permute-start | bytes 3145736 | tf_op jit(solution)/shard_map/ppermute | solution.py:457
  183.4 46.3 %collective-permute-start.11 = (bf16[512,1024]{1,0:T(8,128)(2,1)}, bf16[512,1024]{1,0:T(8,128)(2,1)}, u32[]{:S(2)}, u32[]{:S(2)}) collective-permute-start(bf16[512,1024]{1,0:T(8,128)(2,1)} %dynamic-slice_bitcast_fusion.rest_2_), channel_id=1, source_target_pairs={{0,8},{2,10},{4,12},{6,14},{8,0},{10,2},{12,4},{14,6},{16,24},{18,... | collective-permute-start | bytes 3145736 | tf_op jit(solution)/shard_map/ppermute | solution.py:457
  185.5 121.2 %collective-permute-start.18 = (bf16[512,1024]{1,0:T(8,128)(2,1)}, bf16[512,1024]{1,0:T(8,128)(2,1)}, u32[]{:S(2)}, u32[]{:S(2)}) collective-permute-start(bf16[512,1024]{1,0:T(8,128)(2,1)} %dynamic-slice_bitcast_fusion.rest_2_), channel_id=1, source_target_pairs={{0,16},{2,18},{4,20},{6,22},{8,24},{10,26},{12,28},{14,30},{16,0},... | collective-permute-start | bytes 3145736 | tf_op jit(solution)/shard_map/ppermute | solution.py:457
  229.7 47.7 %collective-permute-start.16 = (bf16[1024,512]{1,0:T(8,128)(2,1)}, bf16[1024,512]{1,0:T(8,128)(2,1)}, u32[]{:S(2)}, u32[]{:S(2)}) collective-permute-start(bf16[1024,512]{1,0:T(8,128)(2,1)} %collective-permute-done.5.rest_0_), channel_id=1, source_target_pairs={{0,8},{2,10},{4,12},{6,14},{8,0},{10,2},{12,4},{14,6},{16,24},{18,... | collective-permute-start | bytes 3145736 | tf_op jit(solution)/shard_map/ppermute | solution.py:457
  232.2 45.2 %collective-permute-start.17 = (bf16[1024,1024]{1,0:T(8,128)(2,1)}, bf16[1024,1024]{1,0:T(8,128)(2,1)}, u32[]{:S(2)}, u32[]{:S(2)}) collective-permute-start(bf16[1024,1024]{1,0:T(8,128)(2,1)} %collective-permute-done.12.tokens_a), channel_id=1, source_target_pairs={{0,2},{2,0},{4,6},{6,4},{5,7},{7,5},{1,3},{3,1},{8,10},{10,8},{12,... | collective-permute-start | bytes 6291464 | tf_op jit(solution)/shard_map/ppermute | solution.py:70
  232.2 45.2 %collective-permute-start.13 = (bf16[1024,1024]{1,0:T(8,128)(2,1)}, bf16[1024,1024]{1,0:T(8,128)(2,1)}, u32[]{:S(2)}, u32[]{:S(2)}) collective-permute-start(bf16[1024,1024]{1,0:T(8,128)(2,1)} %collective-permute-done.12.tokens_a), channel_id=1, source_target_pairs={{0,4},{6,2},{4,5},{7,6},{5,1},{3,7},{1,0},{2,3},{8,12},{14,10},{12... | collective-permute-start | bytes 6291464 | tf_op jit(solution)/shard_map/ppermute | solution.py:67
  308.8 64.4 %collective-permute-start.14 = (bf16[1024,1024]{1,0:T(8,128)(2,1)}, bf16[1024,1024]{1,0:T(8,128)(2,1)}, u32[]{:S(2)}, u32[]{:S(2)}) collective-permute-start(bf16[1024,1024]{1,0:T(8,128)(2,1)} %collective-permute-done.13.tokens_a), channel_id=1, source_target_pairs={{0,4},{6,2},{4,5},{7,6},{5,1},{3,7},{1,0},{2,3},{8,12},{14,10},{12... | collective-permute-start | bytes 6291464 | tf_op jit(solution)/shard_map/ppermute | solution.py:67
  373.2 39.6 %collective-permute-start.22 = (bf16[1024,1024]{1,0:T(8,128)(2,1)}, bf16[1024,1024]{1,0:T(8,128)(2,1)}, u32[]{:S(2)}, u32[]{:S(2)}) collective-permute-start(bf16[1024,1024]{1,0:T(8,128)(2,1)} %collective-permute-done.14.tokens_a), channel_id=1, source_target_pairs={{0,2},{2,0},{4,6},{6,4},{5,7},{7,5},{1,3},{3,1},{8,10},{10,8},{12,... | collective-permute-start | bytes 6291464 | tf_op jit(solution)/shard_map/ppermute | solution.py:70
  448.7 58.3 %collective-permute-start.27 = (bf16[1088,1024]{1,0:T(8,128)(2,1)}, bf16[1088,1024]{1,0:T(8,128)(2,1)}, u32[]{:S(2)}, u32[]{:S(2)}) collective-permute-start(bf16[1088,1024]{1,0:T(8,128)(2,1)} %add_convert_fusion.2), channel_id=1, source_target_pairs={{0,4},{6,2},{4,5},{7,6},{5,1},{3,7},{1,0},{2,3},{8,12},{14,10},{12... | collective-permute-start | bytes 6684680 | tf_op jit(solution)/shard_map/ppermute | solution.py:67
  542.4 40.1 %collective-permute-start.31 = (bf16[512,1024]{1,0:T(8,128)(2,1)S(1)}, bf16[512,1024]{1,0:T(8,128)(2,1)S(1)}, u32[]{:S(2)}, u32[]{:S(2)}) collective-permute-start(bf16[512,1024]{1,0:T(8,128)(2,1)S(1)} %copy-done.64), channel_id=1, source_target_pairs={{0,8},{2,10},{4,12},{6,14},{8,0},{10,2},{12,4},{14,6},{16,24},{18,... | collective-permute-start | bytes 3145736 | tf_op jit(solution)/shard_map/ppermute | solution.py:457
  544.2 46.3 %collective-permute-start.32 = (bf16[512,1024]{1,0:T(8,128)(2,1)S(1)}, bf16[512,1024]{1,0:T(8,128)(2,1)S(1)}, u32[]{:S(2)}, u32[]{:S(2)}) collective-permute-start(bf16[512,1024]{1,0:T(8,128)(2,1)S(1)} %copy-done.98), channel_id=1, source_target_pairs={{0,8},{2,10},{4,12},{6,14},{8,0},{10,2},{12,4},{14,6},{16,24},{18,... | collective-permute-start | bytes 3145736 | tf_op jit(solution)/shard_map/ppermute | solution.py:457
  545.6 44.9 %collective-permute-start.25 = (bf16[1088,1024]{1,0:T(8,128)(2,1)S(1)}, bf16[1088,1024]{1,0:T(8,128)(2,1)S(1)}, u32[]{:S(2)}, u32[]{:S(2)}) collective-permute-start(bf16[1088,1024]{1,0:T(8,128)(2,1)S(1)} %add_convert_fusion.4), channel_id=1, source_target_pairs={{0,2},{2,0},{4,6},{6,4},{5,7},{7,5},{1,3},{3,1},{8,10},{10,8},{12,... | collective-permute-start | bytes 6684680 | tf_op jit(solution)/shard_map/ppermute | solution.py:70
  609.1 55.4 %collective-permute-start.36 = (bf16[512,1024]{1,0:T(8,128)(2,1)}, bf16[512,1024]{1,0:T(8,128)(2,1)}, u32[]{:S(2)}, u32[]{:S(2)}) collective-permute-start(bf16[512,1024]{1,0:T(8,128)(2,1)} %add_convert_fusion.20), channel_id=1, source_target_pairs={{0,16},{2,18},{4,20},{6,22},{8,24},{10,26},{12,28},{14,30},{16,0},... | collective-permute-start | bytes 3145736 | tf_op jit(solution)/shard_map/ppermute | solution.py:457
  613.0 75.3 %collective-permute-start.37 = (bf16[512,1024]{1,0:T(8,128)(2,1)}, bf16[512,1024]{1,0:T(8,128)(2,1)}, u32[]{:S(2)}, u32[]{:S(2)}) collective-permute-start(bf16[512,1024]{1,0:T(8,128)(2,1)} %get-tuple-element.370), channel_id=1, source_target_pairs={{0,8},{2,10},{4,12},{6,14},{8,0},{10,2},{12,4},{14,6},{16,24},{18,... | collective-permute-start | bytes 3145736 | tf_op jit(solution)/shard_map/ppermute | solution.py:457
  613.3 103.2 %collective-permute-start.40 = (bf16[512,1024]{1,0:T(8,128)(2,1)}, bf16[512,1024]{1,0:T(8,128)(2,1)}, u32[]{:S(2)}, u32[]{:S(2)}) collective-permute-start(bf16[512,1024]{1,0:T(8,128)(2,1)} %get-tuple-element.384), channel_id=1, source_target_pairs={{0,8},{2,10},{4,12},{6,14},{8,0},{10,2},{12,4},{14,6},{16,24},{18,... | collective-permute-start | bytes 3145736 | tf_op jit(solution)/shard_map/ppermute | solution.py:457
  621.6 222.2 %reduce-scatter.5.cloned.1.call-start = ((), (), s32[]{:S(2)}) async-start(), calls=%async_computation.5 | async-start | bytes 4456448 | tf_op jit(solution)/shard_map/reduce_scatter | solution.py:735
  625.0 63.2 %collective-permute-start.38 = (bf16[1024,1024]{1,0:T(8,128)(2,1)S(1)}, bf16[1024,1024]{1,0:T(8,128)(2,1)S(1)}, u32[]{:S(2)}, u32[]{:S(2)}) collective-permute-start(bf16[1024,1024]{1,0:T(8,128)(2,1)S(1)} %add_convert_fusion.11), channel_id=1, source_target_pairs={{0,2},{2,0},{4,6},{6,4},{5,7},{7,5},{1,3},{3,1},{8,10},{10,8},{12,... | collective-permute-start | bytes 6291464 | tf_op jit(solution)/shard_map/ppermute | solution.py:70
  658.4 58.1 %collective-permute-start.41 = (bf16[512,1024]{1,0:T(8,128)(2,1)S(1)}, bf16[512,1024]{1,0:T(8,128)(2,1)S(1)}, u32[]{:S(2)}, u32[]{:S(2)}) collective-permute-start(bf16[512,1024]{1,0:T(8,128)(2,1)S(1)} %add_convert_fusion.19), channel_id=1, source_target_pairs={{0,16},{2,18},{4,20},{6,22},{8,24},{10,26},{12,28},{14,30},{16,0},... | collective-permute-start | bytes 3145736 | tf_op jit(solution)/shard_map/ppermute | solution.py:457
  664.5 145.0 %collective-permute-start.42 = (bf16[512,1024]{1,0:T(8,128)(2,1)}, bf16[512,1024]{1,0:T(8,128)(2,1)}, u32[]{:S(2)}, u32[]{:S(2)}) collective-permute-start(bf16[512,1024]{1,0:T(8,128)(2,1)} %add_convert_fusion.18), channel_id=1, source_target_pairs={{0,16},{2,18},{4,20},{6,22},{8,24},{10,26},{12,28},{14,30},{16,0},... | collective-permute-start | bytes 3145736 | tf_op jit(solution)/shard_map/ppermute | solution.py:457
  688.3 121.2 %collective-permute-start.43 = (bf16[512,1024]{1,0:T(8,128)(2,1)}, bf16[512,1024]{1,0:T(8,128)(2,1)}, u32[]{:S(2)}, u32[]{:S(2)}) collective-permute-start(bf16[512,1024]{1,0:T(8,128)(2,1)} %fusion.95), channel_id=1, source_target_pairs={{0,8},{2,10},{4,12},{6,14},{8,0},{10,2},{12,4},{14,6},{16,24},{18,... | collective-permute-start | bytes 3145736 | tf_op jit(solution)/shard_map/ppermute | solution.py:457
  745.8 63.8 %collective-permute-start.45 = (bf16[1024,1024]{1,0:T(8,128)(2,1)S(1)}, bf16[1024,1024]{1,0:T(8,128)(2,1)S(1)}, u32[]{:S(2)}, u32[]{:S(2)}) collective-permute-start(bf16[1024,1024]{1,0:T(8,128)(2,1)S(1)} %add_convert_fusion.8), channel_id=1, source_target_pairs={{0,4},{6,2},{4,5},{7,6},{5,1},{3,7},{1,0},{2,3},{8,12},{14,10},{12... | collective-permute-start | bytes 6291464 | tf_op jit(solution)/shard_map/ppermute | solution.py:67
  (137 other events, 2157.2 us)
Sparse Core Ops, SparseCore 0:
  10.8 58.5 all-gather.2
  86.2 56.3 all-gather.4
  621.7 143.5 reduce-scatter.2
  769.5 74.2 reduce-scatter.4
